TPU v7x, 1024 devices: a whole 4x4x32 slice. The times are simulated.
1024 devices in a mesh: blk: 64 (over z_lo, y, core), group: 16 (over x, z_hi).
Axes of the slice: x: 4, y: 4, z: 32 (z_hi: 4, z_lo: 8; z = z_hi * 8 + z_lo), core: 2. Of those that a mesh axis runs over, the one named last changes fastest.
Arguments:
- picture_features_unnormed: float32 [196608, 768], P(('blk', 'group')), may hold values from -0.34280172 to 0.34280172, as said below
- caption_features_unnormed: float32 [196608, 768], P(('blk', 'group')), may hold values from -0.34280172 to 0.34280172, as said below
- example_match_key: int32 [196608], P(('blk', 'group')), may hold values from 0 to 24575, as said below
- picture_loss_share: float32 [196608], P(('blk', 'group')), may hold values from 0.6 to 45, as said below
- score_multiplier: float32 [1], replicated, may hold values from 5 to 15
- score_shift: float32 [1], replicated, may hold values from -5 to -3
Outputs:
- loss: float32 [1], replicated
- image_grad: float32 [196608, 768], P(('blk', 'group'))
- text_grad: float32 [196608, 768], P(('blk', 'group'))
Inputs may be any that keep to these rules, and one draw needn't show every extreme that they name: `picture_features_unnormed`: each row is the sum of a part shared by the image and the text of the same sample and a part of its own, times a row scale. `caption_features_unnormed`: each row is the sum of a part shared by the image and the text of the same sample and a part of its own, times a row scale. `example_match_key`: ids may repeat, also over all 192 samples of one device. `picture_loss_share`: positive.
All inputs are finite; a program needn't handle non-finite values.
Results may differ from a plain program's by a relative error of at most 0.0041.
Values may be sent and summed in bfloat16 or wider, within the bound.
No kernel may reach another device: no remote copies, remote signals or barrier semaphores. Data moves between devices by JAX's collectives and lax.ppermute only.
A program may use at most 32 MiB of HBM per device.

v0:
```python
import jax
import jax.numpy as jnp
from jax import lax
from jax.sharding import PartitionSpec as P

STEPS = 8


def from_behind(value, axis, steps):
    count = lax.axis_size(axis)
    pairs = [(source, (source + steps) % count) for source in range(count)]
    return lax.ppermute(value, axis, pairs)


def normalize(values):
    row_norm = jnp.sqrt(jnp.sum(values * values, -1, keepdims=True) + 1e-06)
    return (values / row_norm, row_norm)


def project_back(unit, grad_unit, row_norm):
    return (grad_unit - unit * jnp.sum(unit * grad_unit, -1, keepdims=True)) / row_norm


def multiplier_matrix(
    picture_features_halfwidth,
    loss_shares,
    picture_match_keys,
    caption_features_halfwidth,
    caption_match_keys,
    score_scaled_factor,
    shifted_scores,
):
    similarity_matrix = jnp.einsum(
        "rd,sd->rs",
        picture_features_halfwidth,
        caption_features_halfwidth,
        preferred_element_type=jnp.float32,
    )
    score_matrix = score_scaled_factor * similarity_matrix + shifted_scores
    target_signs = jnp.where(
        picture_match_keys[:, None] == caption_match_keys[None, :], 1.0, -1.0
    ).astype(jnp.float32)
    per_line_penalty = jnp.sum(jax.nn.softplus(-target_signs * score_matrix), -1)
    multiplier_entry = (
        loss_shares[:, None]
        * score_scaled_factor
        * -target_signs
        * jax.nn.sigmoid(-target_signs * score_matrix)
    ).astype(jnp.bfloat16)
    return (per_line_penalty, multiplier_entry)


def match_contributions(
    picture_features_halfwidth,
    loss_shares,
    picture_match_keys,
    caption_features_halfwidth,
    caption_match_keys,
    score_scaled_factor,
    shifted_scores,
):
    per_line_penalty, multiplier_entry = multiplier_matrix(
        picture_features_halfwidth,
        loss_shares,
        picture_match_keys,
        caption_features_halfwidth,
        caption_match_keys,
        score_scaled_factor,
        shifted_scores,
    )
    picture_derivative = jnp.dot(
        multiplier_entry, caption_features_halfwidth, preferred_element_type=jnp.float32
    )
    caption_derivative = jnp.einsum(
        "rs,rd->sd",
        multiplier_entry,
        picture_features_halfwidth,
        preferred_element_type=jnp.float32,
    )
    return (per_line_penalty, picture_derivative, caption_derivative)


def move_text(block, block_ids, distance):
    moved = from_behind(block, "blk", distance)
    moved_ids = from_behind(block_ids, "blk", distance)
    return (moved, moved_ids)


def move_grads(carried, distance):
    return from_behind(carried, "blk", distance)


def send_home(carried, distance):
    return from_behind(carried, "blk", distance)


def per_device(
    picture_features_unnormed,
    caption_features_unnormed,
    example_match_key,
    picture_loss_share,
    score_multiplier,
    score_shift,
):
    unit_img, img_norm = normalize(picture_features_unnormed)
    unit_txt, txt_norm = normalize(caption_features_unnormed)
    picture_features_halfwidth = unit_img.astype(jnp.bfloat16)
    caption_features_halfwidth = unit_txt.astype(jnp.bfloat16)
    score_scaled_factor = score_multiplier[0]
    shifted_scores = score_shift[0]
    half_steps = STEPS // 2
    incoming_features, incoming_match_keys = (caption_features_halfwidth, example_match_key)
    row_total = jnp.zeros(example_match_key.shape, jnp.float32)
    grad_unit_img = jnp.zeros(picture_features_unnormed.shape, jnp.float32)
    carried = None
    for number in range(STEPS):
        distance = -half_steps if number == 0 else 1
        incoming_features, incoming_match_keys = move_text(
            incoming_features, incoming_match_keys, distance
        )
        per_line_penalty, picture_derivative, caption_derivative = match_contributions(
            picture_features_halfwidth,
            picture_loss_share,
            example_match_key,
            incoming_features,
            incoming_match_keys,
            score_scaled_factor,
            shifted_scores,
        )
        row_total = row_total + per_line_penalty
        grad_unit_img = grad_unit_img + picture_derivative
        carried = caption_derivative if number == 0 else move_grads(carried, 1) + caption_derivative
    grad_unit_txt = send_home(carried, -(half_steps - 1))
    loss_part = jnp.sum(picture_loss_share * row_total)
    weight_part = jnp.sum(picture_loss_share)
    totals = lax.psum((loss_part, weight_part), ("blk", "group"))
    loss = (totals[0] / totals[1]).reshape(1)
    image_grad = project_back(unit_img, grad_unit_img, img_norm)
    text_grad = project_back(unit_txt, grad_unit_txt, txt_norm)
    return (loss, image_grad, text_grad)


def solution(mesh):
    placed = (
        P(("blk", "group"), None),
        P(("blk", "group"), None),
        P(("blk", "group")),
        P(("blk", "group")),
        P(),
        P(),
    )
    return jax.shard_map(
        per_device,
        mesh=mesh,
        in_specs=placed,
        out_specs=(P(), P(("blk", "group"), None), P(("blk", "group"), None)),
        check_vma=False,
    )
```

profile of v0, /device:TPU:1, one launch (start us, length us, event | category | flops | bytes accessed | tf_op | source)
XLA Modules:
  0.0 507.0 jit_solution(3161960679385795097)
XLA Ops:
  0.6 1.2 multiply_reduce_fusion.2
  2.0 16.5 %collective-permute-start.1 = (bf16[192,768]{1,0:T(8,128)(2,1)S(1)}, bf16[192,768]{1,0:T(8,128)(2,1)S(1)}, u32[]{:S(2)}, u32[]{:S(2)}) collective-permute-start(bf16[192,768]{1,0:T(8,128)(2,1)S(1)} %fusion.39), channel_id=1, source_target_pairs={{0,960},{16,976},{32,992},{48,1008},{64,0},{80,16},{96,32},{112,48... | collective-permute-start | bytes 884744 | tf_op jit(solution)/shard_map/ppermute | solution.py:12
  18.5 5.7 %collective-permute-done.1 = bf16[192,768]{1,0:T(8,128)(2,1)S(1)} collective-permute-done((bf16[192,768]{1,0:T(8,128)(2,1)S(1)}, bf16[192,768]{1,0:T(8,128)(2,1)S(1)}, u32[]{:S(2)}, u32[]{:S(2)}) %collective-permute-start.1) | collective-permute-done | bytes 294944 | tf_op jit(solution)/shard_map/ppermute | solution.py:12
  24.2 3.7 collective-permute-start.3
  27.9 4.0 collective-permute-done.3
  31.9 4.1 collective-permute-start.5
  36.0 13.7 %collective-permute-start = (s32[192]{0:T(256)S(1)}, s32[192]{0:T(256)S(1)}, u32[]{:S(2)}, u32[]{:S(2)}) collective-permute-start(s32[192]{0:T(256)S(1)} %copy-done.2), channel_id=1, source_target_pairs={{0,960},{16,976},{32,992},{48,1008},{64,0},{80,16},{96,32},{112,48... | collective-permute-start | bytes 2312 | tf_op jit(solution)/shard_map/ppermute | solution.py:12
  49.7 0.7 collective-permute-done
  50.4 2.4 collective-permute-start.2
  52.8 4.3 collective-permute-done.2
  57.1 8.8 %collective-permute-start.4 = (s32[192]{0:T(256)S(1)}, s32[192]{0:T(256)S(1)}, u32[]{:S(2)}, u32[]{:S(2)}) collective-permute-start(s32[192]{0:T(256)S(1)} %collective-permute-done.2), channel_id=1, source_target_pairs={{0,16},{16,32},{32,48},{48,64},{64,80},{80,96},{96,112},{112,128},... | collective-permute-start | bytes 2312 | tf_op jit(solution)/shard_map/ppermute | solution.py:12
  65.8 11.2 %collective-permute-done.4 = s32[192]{0:T(256)S(1)} collective-permute-done((s32[192]{0:T(256)S(1)}, s32[192]{0:T(256)S(1)}, u32[]{:S(2)}, u32[]{:S(2)}) %collective-permute-start.4) | collective-permute-done | bytes 800 | tf_op jit(solution)/shard_map/ppermute | solution.py:12
  77.0 1.9 collective-permute-start.6
  78.9 11.7 %collective-permute-done.6 = s32[192]{0:T(256)S(1)} collective-permute-done((s32[192]{0:T(256)S(1)}, s32[192]{0:T(256)S(1)}, u32[]{:S(2)}, u32[]{:S(2)}) %collective-permute-start.6) | collective-permute-done | bytes 800 | tf_op jit(solution)/shard_map/ppermute | solution.py:12
  90.6 1.9 collective-permute-start.8
  92.5 1.9 collective-permute-start.7
  94.6 9.6 %collective-permute-done.8 = s32[192]{0:T(256)S(1)} collective-permute-done((s32[192]{0:T(256)S(1)}, s32[192]{0:T(256)S(1)}, u32[]{:S(2)}, u32[]{:S(2)}) %collective-permute-start.8) | collective-permute-done | bytes 800 | tf_op jit(solution)/shard_map/ppermute | solution.py:12
  104.2 1.9 collective-permute-start.10
  106.1 11.7 %collective-permute-done.10 = s32[192]{0:T(256)S(1)} collective-permute-done((s32[192]{0:T(256)S(1)}, s32[192]{0:T(256)S(1)}, u32[]{:S(2)}, u32[]{:S(2)}) %collective-permute-start.10) | collective-permute-done | bytes 800 | tf_op jit(solution)/shard_map/ppermute | solution.py:12
  117.8 1.9 collective-permute-start.12
  119.7 1.9 collective-permute-start.9
  123.0 8.3 %collective-permute-done.12 = s32[192]{0:T(256)S(1)} collective-permute-done((s32[192]{0:T(256)S(1)}, s32[192]{0:T(256)S(1)}, u32[]{:S(2)}, u32[]{:S(2)}) %collective-permute-start.12) | collective-permute-done | bytes 800 | tf_op jit(solution)/shard_map/ppermute | solution.py:12
  131.4 1.9 collective-permute-start.14
  133.3 0.4 fusion.16
  133.8 1.9 collective-permute-start.11
  135.7 0.4 fusion.17
  136.1 0.4 fusion.18
  136.5 14.0 %collective-permute-done.11 = bf16[192,768]{1,0:T(8,128)(2,1)S(1)} collective-permute-done((bf16[192,768]{1,0:T(8,128)(2,1)S(1)}, bf16[192,768]{1,0:T(8,128)(2,1)S(1)}, u32[]{:S(2)}, u32[]{:S(2)}) %collective-permute-start.11) | collective-permute-done | bytes 294944 | tf_op jit(solution)/shard_map/ppermute | solution.py:12
  150.5 1.9 collective-permute-start.13
  152.4 0.4 fusion.19
  152.8 0.4 fusion.20
  153.2 14.0 %collective-permute-done.13 = bf16[192,768]{1,0:T(8,128)(2,1)S(1)} collective-permute-done((bf16[192,768]{1,0:T(8,128)(2,1)S(1)}, bf16[192,768]{1,0:T(8,128)(2,1)S(1)}, u32[]{:S(2)}, u32[]{:S(2)}) %collective-permute-start.13) | collective-permute-done | bytes 294944 | tf_op jit(solution)/shard_map/ppermute | solution.py:12
  167.2 1.9 collective-permute-start.15
  169.2 0.4 fusion.21
  169.6 0.4 fusion.22
  170.0 14.0 %collective-permute-done.15 = bf16[192,768]{1,0:T(8,128)(2,1)S(1)} collective-permute-done((bf16[192,768]{1,0:T(8,128)(2,1)S(1)}, bf16[192,768]{1,0:T(8,128)(2,1)S(1)}, u32[]{:S(2)}, u32[]{:S(2)}) %collective-permute-start.15) | collective-permute-done | bytes 294944 | tf_op jit(solution)/shard_map/ppermute | solution.py:12
  184.0 0.4 fusion.23
  184.4 0.7 copy-done.3
  185.1 0.6 fusion.40
  186.0 1.9 collective-permute-start.16
  187.9 15.3 %collective-permute-done.16 = f32[192,768]{1,0:T(8,128)S(1)} collective-permute-done((f32[192,768]{1,0:T(8,128)S(1)}, f32[192,768]{1,0:T(8,128)S(1)}, u32[]{:S(2)}, u32[]{:S(2)}) %collective-permute-start.16) | collective-permute-done | bytes 589856 | tf_op jit(solution)/shard_map/ppermute | solution.py:12
  203.4 1.9 collective-permute-start.17
  205.4 18.0 %collective-permute-done.17 = f32[192,768]{1,0:T(8,128)S(1)} collective-permute-done((f32[192,768]{1,0:T(8,128)S(1)}, f32[192,768]{1,0:T(8,128)S(1)}, u32[]{:S(2)}, u32[]{:S(2)}) %collective-permute-start.17) | collective-permute-done | bytes 589856 | tf_op jit(solution)/shard_map/ppermute | solution.py:12
  223.7 1.9 collective-permute-start.18
  225.6 18.0 %collective-permute-done.18 = f32[192,768]{1,0:T(8,128)S(1)} collective-permute-done((f32[192,768]{1,0:T(8,128)S(1)}, f32[192,768]{1,0:T(8,128)S(1)}, u32[]{:S(2)}, u32[]{:S(2)}) %collective-permute-start.18) | collective-permute-done | bytes 589856 | tf_op jit(solution)/shard_map/ppermute | solution.py:12
  243.9 1.9 collective-permute-start.19
  245.8 18.0 %collective-permute-done.19 = f32[192,768]{1,0:T(8,128)S(1)} collective-permute-done((f32[192,768]{1,0:T(8,128)S(1)}, f32[192,768]{1,0:T(8,128)S(1)}, u32[]{:S(2)}, u32[]{:S(2)}) %collective-permute-start.19) | collective-permute-done | bytes 589856 | tf_op jit(solution)/shard_map/ppermute | solution.py:12
  264.1 1.9 collective-permute-start.20
  266.0 18.1 %collective-permute-done.20 = f32[192,768]{1,0:T(8,128)S(1)} collective-permute-done((f32[192,768]{1,0:T(8,128)S(1)}, f32[192,768]{1,0:T(8,128)S(1)}, u32[]{:S(2)}, u32[]{:S(2)}) %collective-permute-start.20) | collective-permute-done | bytes 589856 | tf_op jit(solution)/shard_map/ppermute | solution.py:12
  284.4 1.9 collective-permute-start.21
  286.7 0.4 convolution_add_fusion.7
  287.0 0.4 convolution_add_fusion.6
  287.4 17.1 %collective-permute-done.21 = f32[192,768]{1,0:T(8,128)S(1)} collective-permute-done((f32[192,768]{1,0:T(8,128)S(1)}, f32[192,768]{1,0:T(8,128)S(1)}, u32[]{:S(2)}, u32[]{:S(2)}) %collective-permute-start.21) | collective-permute-done | bytes 589856 | tf_op jit(solution)/shard_map/ppermute | solution.py:12
  304.8 1.9 collective-permute-start.22
  306.7 0.4 convolution_add_fusion.5
  307.1 0.4 convolution_add_fusion.4
  307.4 0.4 convolution_add_fusion.3
  307.8 17.1 %collective-permute-done.22 = f32[192,768]{1,0:T(8,128)S(1)} collective-permute-done((f32[192,768]{1,0:T(8,128)S(1)}, f32[192,768]{1,0:T(8,128)S(1)}, u32[]{:S(2)}, u32[]{:S(2)}) %collective-permute-start.22) | collective-permute-done | bytes 589856 | tf_op jit(solution)/shard_map/ppermute | solution.py:12
  325.2 1.9 collective-permute-start.23
  327.1 0.4 convolution_add_fusion.2
  327.4 174.4 %all-reduce = (f32[]{:T(128)}, f32[]{:T(128)}) all-reduce(f32[]{:T(128)} %get-tuple-element.4, f32[]{:T(128)} %get-tuple-element.3), channel_id=1, replica_groups=mesh['blk'=64,'group'=16] {'blk','group'}, use_global_device_ids=true, to_apply=%region_11.12 | all-reduce | flops 2 | bytes 16 | tf_op jit(solution)/shard_map/psum | solution.py:136
  503.2 0.5 multiply_reduce_fusion.1
  503.6 1.0 subtract_divide_fusion.1
  504.8 1.0 subtract_divide_fusion
  (27 shorter events, 3.3 us)
Async XLA Ops:
  0.6 1.3 copy-start
  1.9 92.6 %copy-start.1 = (f32[192,768]{1,0:T(8,128)S(1)}, f32[192,768]{1,0:T(8,128)}, u32[]{:S(2)}) copy-start(f32[192,768]{1,0:T(8,128)} %param.6) | copy-start | bytes 1769476
  1.9 34.0 %copy-start.2 = (s32[192]{0:T(256)S(1)}, s32[192]{0:T(256)}, u32[]{:S(2)}) copy-start(s32[192]{0:T(256)} %param.8) | copy-start | bytes 2308
  2.0 22.1 %collective-permute-start.1 = (bf16[192,768]{1,0:T(8,128)(2,1)S(1)}, bf16[192,768]{1,0:T(8,128)(2,1)S(1)}, u32[]{:S(2)}, u32[]{:S(2)}) collective-permute-start(bf16[192,768]{1,0:T(8,128)(2,1)S(1)} %fusion.39), channel_id=1, source_target_pairs={{0,960},{16,976},{32,992},{48,1008},{64,0},{80,16},{96,32},{112,48... | collective-permute-start | bytes 884744 | tf_op jit(solution)/shard_map/ppermute | solution.py:12
  24.2 7.7 %collective-permute-start.3 = (bf16[192,768]{1,0:T(8,128)(2,1)S(1)}, bf16[192,768]{1,0:T(8,128)(2,1)S(1)}, u32[]{:S(2)}, u32[]{:S(2)}) collective-permute-start(bf16[192,768]{1,0:T(8,128)(2,1)S(1)} %collective-permute-done.1), channel_id=1, source_target_pairs={{0,16},{16,32},{32,48},{48,64},{64,80},{80,96},{96,112},{112,128},... | collective-permute-start | bytes 884744 | tf_op jit(solution)/shard_map/ppermute | solution.py:12
  31.9 60.6 %collective-permute-start.5 = (bf16[192,768]{1,0:T(8,128)(2,1)S(1)}, bf16[192,768]{1,0:T(8,128)(2,1)S(1)}, u32[]{:S(2)}, u32[]{:S(2)}) collective-permute-start(bf16[192,768]{1,0:T(8,128)(2,1)S(1)} %collective-permute-done.3), channel_id=1, source_target_pairs={{0,16},{16,32},{32,48},{48,64},{64,80},{80,96},{96,112},{112,128},... | collective-permute-start | bytes 884744 | tf_op jit(solution)/shard_map/ppermute | solution.py:12
  36.0 14.4 %collective-permute-start = (s32[192]{0:T(256)S(1)}, s32[192]{0:T(256)S(1)}, u32[]{:S(2)}, u32[]{:S(2)}) collective-permute-start(s32[192]{0:T(256)S(1)} %copy-done.2), channel_id=1, source_target_pairs={{0,960},{16,976},{32,992},{48,1008},{64,0},{80,16},{96,32},{112,48... | collective-permute-start | bytes 2312 | tf_op jit(solution)/shard_map/ppermute | solution.py:12
  50.4 6.7 %collective-permute-start.2 = (s32[192]{0:T(256)S(1)}, s32[192]{0:T(256)S(1)}, u32[]{:S(2)}, u32[]{:S(2)}) collective-permute-start(s32[192]{0:T(256)S(1)} %collective-permute-done), channel_id=1, source_target_pairs={{0,16},{16,32},{32,48},{48,64},{64,80},{80,96},{96,112},{112,128},... | collective-permute-start | bytes 2312 | tf_op jit(solution)/shard_map/ppermute | solution.py:12
  57.1 19.9 %collective-permute-start.4 = (s32[192]{0:T(256)S(1)}, s32[192]{0:T(256)S(1)}, u32[]{:S(2)}, u32[]{:S(2)}) collective-permute-start(s32[192]{0:T(256)S(1)} %collective-permute-done.2), channel_id=1, source_target_pairs={{0,16},{16,32},{32,48},{48,64},{64,80},{80,96},{96,112},{112,128},... | collective-permute-start | bytes 2312 | tf_op jit(solution)/shard_map/ppermute | solution.py:12
  77.0 13.6 %collective-permute-start.6 = (s32[192]{0:T(256)S(1)}, s32[192]{0:T(256)S(1)}, u32[]{:S(2)}, u32[]{:S(2)}) collective-permute-start(s32[192]{0:T(256)S(1)} %collective-permute-done.4), channel_id=1, source_target_pairs={{0,16},{16,32},{32,48},{48,64},{64,80},{80,96},{96,112},{112,128},... | collective-permute-start | bytes 2312 | tf_op jit(solution)/shard_map/ppermute | solution.py:12
  90.6 13.6 %collective-permute-start.8 = (s32[192]{0:T(256)S(1)}, s32[192]{0:T(256)S(1)}, u32[]{:S(2)}, u32[]{:S(2)}) collective-permute-start(s32[192]{0:T(256)S(1)} %collective-permute-done.6), channel_id=1, source_target_pairs={{0,16},{16,32},{32,48},{48,64},{64,80},{80,96},{96,112},{112,128},... | collective-permute-start | bytes 2312 | tf_op jit(solution)/shard_map/ppermute | solution.py:12
  92.5 27.2 %collective-permute-start.7 = (bf16[192,768]{1,0:T(8,128)(2,1)S(1)}, bf16[192,768]{1,0:T(8,128)(2,1)S(1)}, u32[]{:S(2)}, u32[]{:S(2)}) collective-permute-start(bf16[192,768]{1,0:T(8,128)(2,1)S(1)} %collective-permute-done.5), channel_id=1, source_target_pairs={{0,16},{16,32},{32,48},{48,64},{64,80},{80,96},{96,112},{112,128},... | collective-permute-start | bytes 884744 | tf_op jit(solution)/shard_map/ppermute | solution.py:12
  104.2 13.6 %collective-permute-start.10 = (s32[192]{0:T(256)S(1)}, s32[192]{0:T(256)S(1)}, u32[]{:S(2)}, u32[]{:S(2)}) collective-permute-start(s32[192]{0:T(256)S(1)} %collective-permute-done.8), channel_id=1, source_target_pairs={{0,16},{16,32},{32,48},{48,64},{64,80},{80,96},{96,112},{112,128},... | collective-permute-start | bytes 2312 | tf_op jit(solution)/shard_map/ppermute | solution.py:12
  117.8 13.6 %collective-permute-start.12 = (s32[192]{0:T(256)S(1)}, s32[192]{0:T(256)S(1)}, u32[]{:S(2)}, u32[]{:S(2)}) collective-permute-start(s32[192]{0:T(256)S(1)} %collective-permute-done.10), channel_id=1, source_target_pairs={{0,16},{16,32},{32,48},{48,64},{64,80},{80,96},{96,112},{112,128},... | collective-permute-start | bytes 2312 | tf_op jit(solution)/shard_map/ppermute | solution.py:12
  119.7 14.0 %collective-permute-start.9 = (bf16[192,768]{1,0:T(8,128)(2,1)S(1)}, bf16[192,768]{1,0:T(8,128)(2,1)S(1)}, u32[]{:S(2)}, u32[]{:S(2)}) collective-permute-start(bf16[192,768]{1,0:T(8,128)(2,1)S(1)} %collective-permute-done.7), channel_id=1, source_target_pairs={{0,16},{16,32},{32,48},{48,64},{64,80},{80,96},{96,112},{112,128},... | collective-permute-start | bytes 884744 | tf_op jit(solution)/shard_map/ppermute | solution.py:12
  131.4 38.6 %collective-permute-start.14 = (s32[192]{0:T(256)S(1)}, s32[192]{0:T(256)S(1)}, u32[]{:S(2)}, u32[]{:S(2)}) collective-permute-start(s32[192]{0:T(256)S(1)} %collective-permute-done.12), channel_id=1, source_target_pairs={{0,16},{16,32},{32,48},{48,64},{64,80},{80,96},{96,112},{112,128},... | collective-permute-start | bytes 2312 | tf_op jit(solution)/shard_map/ppermute | solution.py:12
  133.8 16.7 %collective-permute-start.11 = (bf16[192,768]{1,0:T(8,128)(2,1)S(1)}, bf16[192,768]{1,0:T(8,128)(2,1)S(1)}, u32[]{:S(2)}, u32[]{:S(2)}) collective-permute-start(bf16[192,768]{1,0:T(8,128)(2,1)S(1)} %collective-permute-done.9), channel_id=1, source_target_pairs={{0,16},{16,32},{32,48},{48,64},{64,80},{80,96},{96,112},{112,128},... | collective-permute-start | bytes 884744 | tf_op jit(solution)/shard_map/ppermute | solution.py:12
  150.5 16.7 %collective-permute-start.13 = (bf16[192,768]{1,0:T(8,128)(2,1)S(1)}, bf16[192,768]{1,0:T(8,128)(2,1)S(1)}, u32[]{:S(2)}, u32[]{:S(2)}) collective-permute-start(bf16[192,768]{1,0:T(8,128)(2,1)S(1)} %collective-permute-done.11), channel_id=1, source_target_pairs={{0,16},{16,32},{32,48},{48,64},{64,80},{80,96},{96,112},{112,128},... | collective-permute-start | bytes 884744 | tf_op jit(solution)/shard_map/ppermute | solution.py:12
  167.2 16.7 %collective-permute-start.15 = (bf16[192,768]{1,0:T(8,128)(2,1)S(1)}, bf16[192,768]{1,0:T(8,128)(2,1)S(1)}, u32[]{:S(2)}, u32[]{:S(2)}) collective-permute-start(bf16[192,768]{1,0:T(8,128)(2,1)S(1)} %collective-permute-done.13), channel_id=1, source_target_pairs={{0,16},{16,32},{32,48},{48,64},{64,80},{80,96},{96,112},{112,128},... | collective-permute-start | bytes 884744 | tf_op jit(solution)/shard_map/ppermute | solution.py:12
  184.4 0.7 copy-start.3
  186.0 17.2 %collective-permute-start.16 = (f32[192,768]{1,0:T(8,128)S(1)}, f32[192,768]{1,0:T(8,128)S(1)}, u32[]{:S(2)}, u32[]{:S(2)}) collective-permute-start(f32[192,768]{1,0:T(8,128)S(1)} %fusion.24), channel_id=1, source_target_pairs={{0,16},{16,32},{32,48},{48,64},{64,80},{80,96},{96,112},{112,128},... | collective-permute-start | bytes 1769480 | tf_op jit(solution)/shard_map/ppermute | solution.py:12
  203.4 19.9 %collective-permute-start.17 = (f32[192,768]{1,0:T(8,128)S(1)}, f32[192,768]{1,0:T(8,128)S(1)}, u32[]{:S(2)}, u32[]{:S(2)}) collective-permute-start(f32[192,768]{1,0:T(8,128)S(1)} %convolution_add_fusion), channel_id=1, source_target_pairs={{0,16},{16,32},{32,48},{48,64},{64,80},{80,96},{96,112},{112,128},... | collective-permute-start | bytes 1769480 | tf_op jit(solution)/shard_map/ppermute | solution.py:12
  223.7 19.9 %collective-permute-start.18 = (f32[192,768]{1,0:T(8,128)S(1)}, f32[192,768]{1,0:T(8,128)S(1)}, u32[]{:S(2)}, u32[]{:S(2)}) collective-permute-start(f32[192,768]{1,0:T(8,128)S(1)} %fusion.27), channel_id=1, source_target_pairs={{0,16},{16,32},{32,48},{48,64},{64,80},{80,96},{96,112},{112,128},... | collective-permute-start | bytes 1769480 | tf_op jit(solution)/shard_map/ppermute | solution.py:12
  243.9 19.9 %collective-permute-start.19 = (f32[192,768]{1,0:T(8,128)S(1)}, f32[192,768]{1,0:T(8,128)S(1)}, u32[]{:S(2)}, u32[]{:S(2)}) collective-permute-start(f32[192,768]{1,0:T(8,128)S(1)} %fusion.29), channel_id=1, source_target_pairs={{0,16},{16,32},{32,48},{48,64},{64,80},{80,96},{96,112},{112,128},... | collective-permute-start | bytes 1769480 | tf_op jit(solution)/shard_map/ppermute | solution.py:12
  264.1 20.0 %collective-permute-start.20 = (f32[192,768]{1,0:T(8,128)S(1)}, f32[192,768]{1,0:T(8,128)S(1)}, u32[]{:S(2)}, u32[]{:S(2)}) collective-permute-start(f32[192,768]{1,0:T(8,128)S(1)} %fusion.31), channel_id=1, source_target_pairs={{0,16},{16,32},{32,48},{48,64},{64,80},{80,96},{96,112},{112,128},... | collective-permute-start | bytes 1769480 | tf_op jit(solution)/shard_map/ppermute | solution.py:12
  284.4 20.1 %collective-permute-start.21 = (f32[192,768]{1,0:T(8,128)S(1)}, f32[192,768]{1,0:T(8,128)S(1)}, u32[]{:S(2)}, u32[]{:S(2)}) collective-permute-start(f32[192,768]{1,0:T(8,128)S(1)} %fusion.33), channel_id=1, source_target_pairs={{0,16},{16,32},{32,48},{48,64},{64,80},{80,96},{96,112},{112,128},... | collective-permute-start | bytes 1769480 | tf_op jit(solution)/shard_map/ppermute | solution.py:12
  304.8 20.1 %collective-permute-start.22 = (f32[192,768]{1,0:T(8,128)S(1)}, f32[192,768]{1,0:T(8,128)S(1)}, u32[]{:S(2)}, u32[]{:S(2)}) collective-permute-start(f32[192,768]{1,0:T(8,128)S(1)} %fusion.35), channel_id=1, source_target_pairs={{0,16},{16,32},{32,48},{48,64},{64,80},{80,96},{96,112},{112,128},... | collective-permute-start | bytes 1769480 | tf_op jit(solution)/shard_map/ppermute | solution.py:12
  325.2 179.5 %collective-permute-start.23 = (f32[192,768]{1,0:T(8,128)S(1)}, f32[192,768]{1,0:T(8,128)S(1)}, u32[]{:S(2)}, u32[]{:S(2)}) collective-permute-start(f32[192,768]{1,0:T(8,128)S(1)} %fusion.37), channel_id=1, source_target_pairs={{0,976},{16,992},{32,1008},{48,0},{64,16},{80,32},{96,48},{112,64}... | collective-permute-start | bytes 1769480 | tf_op jit(solution)/shard_map/ppermute | solution.py:12
where the time goes:
time: 508 us; the launch traced here: 507 us
  waiting for transfers between devices  231 us (45%)
  blocking collectives  174 us (34%)
  starting transfers between devices  83.6 us (16%)
  matrix products  8.47 us (2%)
    ppermute x24, waiting for transfers between devices, from_behind(): return lax.ppermute(value, axis, pairs)  231 us
    psum x1, blocking collectives, per_device(): totals = lax.psum((loss_part, weight_part), ('blk', 'group'))  174 us
    ppermute x24, starting transfers between devices, from_behind(): return lax.ppermute(value, axis, pairs)  83.6 us
  transfers between devices with their start and end apart: 24, of which 20 were waited for; matrix products, arithmetic and copies ran while one was open for 1% of the time, Pallas kernels for 0%

commit v1 on v0

v1 whole, which is shorter than its diff:
```python
import jax
import jax.numpy as jnp
from jax import lax
from jax.experimental import pallas as pl
from jax.experimental.pallas import tpu as pltpu
from jax.sharding import PartitionSpec as P

EXTRA = 16
CHUNK = 32
FAR = 2
VMEM_BYTES = 32 * 1024 * 1024


def from_ahead(value, axis, steps):
    count = lax.axis_size(axis)
    pairs = [((target + steps) % count, target) for target in range(count)]
    return lax.ppermute(value, axis, pairs)


def row_norms(values):
    return jnp.sqrt(jnp.sum(values * values, -1, keepdims=True) + 1e-06)


def vmem(count):
    return [pl.BlockSpec(memory_space=pltpu.VMEM)] * count


def call(kernel, outs, args, specs, scratch, flops, transcendentals, moved):
    return pl.pallas_call(
        kernel,
        out_shape=outs,
        in_specs=specs,
        out_specs=vmem(len(outs)),
        scratch_shapes=scratch,
        compiler_params=pltpu.CompilerParams(vmem_limit_bytes=VMEM_BYTES),
        cost_estimate=pl.CostEstimate(
            flops=flops, bytes_accessed=moved, transcendentals=transcendentals
        ),
    )(*args)


def prepare_kernel(img_ref, txt_ref, key_ref, weight_ref, pair_ref, img_out, txt_out):
    rows, width = img_ref.shape
    block = rows + EXTRA
    key = key_ref[...]
    weight = weight_ref[...]
    high = weight.astype(jnp.bfloat16).astype(jnp.float32)
    middle = (weight - high).astype(jnp.bfloat16).astype(jnp.float32)
    low = (weight - high) - middle
    line = lax.broadcasted_iota(jnp.int32, (EXTRA, width), 0)
    extra = jnp.zeros((EXTRA, width), jnp.float32)
    parts = (
        (key >> 8).astype(jnp.float32),
        (key & 255).astype(jnp.float32),
        high,
        middle,
        low,
    )
    for number, part in enumerate(parts):
        extra = jnp.where(line == number, part, extra)
    extra = extra.astype(jnp.bfloat16)
    for start, source, alone in ((0, img_ref, img_out), (block, txt_ref, txt_out)):
        values = source[...]
        unit = (values / row_norms(values)).astype(jnp.bfloat16)
        alone[0:rows, :] = unit
        alone[rows:block, :] = extra
        pair_ref[start : start + rows, :] = unit
        pair_ref[start + rows : start + block, :] = extra


def tile_kernel(
    scale_ref,
    shift_ref,
    weight_ref,
    pair_ref,
    img_ref,
    before_ref,
    own_ref,
    after_ref,
    sums_ref,
    pair_out,
    img_out,
    before_out,
    after_out,
    own_out,
    txts,
    imgs,
    scores,
    factors,
    columns,
):
    rows = own_ref.shape[0] - EXTRA
    width = own_ref.shape[1]
    block = rows + EXTRA
    scale = scale_ref[0]
    shift = shift_ref[0]

    imgs[0:rows, :] = pair_ref[0:rows, :]
    imgs[rows : 2 * rows, :] = img_ref[0:rows, :]
    txts[0:rows, :] = before_ref[0:rows, :]
    txts[rows : 2 * rows, :] = own_ref[0:rows, :]
    txts[2 * rows : 3 * rows, :] = after_ref[0:rows, :]
    txts[3 * rows : 4 * rows, :] = pair_ref[block : block + rows, :]

    lane = lax.broadcasted_iota(jnp.int32, (1, 4 * rows), 1)
    txt_keys = jnp.zeros((1, 4 * rows), jnp.float32)
    for slot, (source, start) in enumerate(
        ((before_ref, rows), (own_ref, rows), (after_ref, rows), (pair_ref, block + rows))
    ):
        extra = source[start : start + EXTRA, :].astype(jnp.float32)
        keys = extra[0:1] * 256.0 + extra[1:2]
        txt_keys = jnp.where(lane >= slot * rows, keys, txt_keys)

    one = lax.broadcasted_iota(jnp.int32, (rows, 256), 0) == lax.broadcasted_iota(
        jnp.int32, (rows, 256), 1
    )
    one = jnp.where(one, 1.0, 0.0).astype(jnp.bfloat16)
    for slot, source in enumerate((pair_ref, img_ref)):
        columns[slot * rows : (slot + 1) * rows, :] = lax.dot_general(
            one,
            source[rows : rows + EXTRA, 0:256],
            (((1,), (1,)), ((), ())),
            preferred_element_type=jnp.float32,
        )

    scores[...] = lax.dot_general(
        imgs[...], txts[...], (((1,), (1,)), ((), ())), preferred_element_type=jnp.float32
    )

    def step(number, total):
        here = pl.ds(pl.multiple_of(number * CHUNK, CHUNK), CHUNK)
        column = columns[here, :]
        img_keys = column[:, 0:1] * 256.0 + column[:, 1:2]
        weights = (column[:, 2:3] + column[:, 3:4]) + column[:, 4:5]
        same = img_keys == txt_keys
        score = scale * scores[here, :] + shift
        argument = jnp.where(same, -score, score)
        small = jnp.exp(-jnp.abs(argument))
        penalty = jnp.maximum(argument, 0.0) + jnp.log1p(small)
        share = 1.0 / (1.0 + small)
        sigmoid = jnp.where(argument >= 0.0, share, small * share)
        scaled = weights * scale
        factors[here, :] = (jnp.where(same, -scaled, scaled) * sigmoid).astype(jnp.bfloat16)
        return total + weights * penalty

    total = lax.fori_loop(
        0, 2 * rows // CHUNK, step, jnp.zeros((CHUNK, 4 * rows), jnp.float32)
    )
    loss_part = jnp.sum(jnp.sum(total, 0, keepdims=True), 1, keepdims=True)
    weight_part = jnp.sum(weight_ref[...], 1, keepdims=True)
    place = lax.broadcasted_iota(jnp.int32, sums_ref.shape, 1)
    sums_ref[...] = jnp.where(
        place == 0, loss_part, jnp.where(place == 1, weight_part, 0.0)
    )

    img_grads = jnp.dot(factors[...], txts[...], preferred_element_type=jnp.float32)
    img_grads = img_grads.astype(jnp.bfloat16)
    pair_out[0:rows, :] = img_grads[0:rows]
    img_out[...] = img_grads[rows : 2 * rows]
    txt_grads = lax.dot_general(
        factors[...], imgs[...], (((0,), (0,)), ((), ())), preferred_element_type=jnp.float32
    )
    before_out[...] = txt_grads[0:rows].astype(jnp.bfloat16)
    own_out[...] = txt_grads[rows : 2 * rows]
    after_out[...] = txt_grads[2 * rows : 3 * rows].astype(jnp.bfloat16)
    pair_out[rows : 2 * rows, :] = txt_grads[3 * rows : 4 * rows].astype(jnp.bfloat16)


def finish_kernel(
    img_ref, txt_ref, pair_ref, far_ref, after_ref, before_ref, own_ref, img_out, txt_out
):
    rows = img_ref.shape[0]

    def finish(values, grad):
        norm = row_norms(values)
        unit = values / norm
        return (grad - unit * jnp.sum(unit * grad, -1, keepdims=True)) / norm

    wide = lambda part: part.astype(jnp.float32)
    img_out[...] = finish(img_ref[...], wide(pair_ref[0:rows, :]) + wide(far_ref[...]))
    txt_out[...] = finish(
        txt_ref[...],
        (own_ref[...] + wide(before_ref[...]))
        + (wide(after_ref[...]) + wide(pair_ref[rows : 2 * rows, :])),
    )


def sum_over(part, axis):
    count = lax.axis_size(axis)
    spread = jnp.broadcast_to(part, (count, part.shape[-1]))
    gathered = lax.all_to_all(spread, axis, 0, 0, tiled=True)
    return jnp.sum(gathered, 0, keepdims=True)


def per_device(image_emb, text_emb, keys, weights, scale, shift):
    rows, width = image_emb.shape
    block = rows + EXTRA
    half = lambda *shape: jax.ShapeDtypeStruct(shape, jnp.bfloat16)
    full = lambda *shape: jax.ShapeDtypeStruct(shape, jnp.float32)
    repeats = width // rows
    wide_keys = jnp.tile(keys, repeats).reshape(1, width)
    wide_weights = jnp.tile(weights, repeats).reshape(1, width)
    pair, img_block, txt_block = call(
        prepare_kernel,
        [half(2 * block, width), half(block, width), half(block, width)],
        (image_emb, text_emb, wide_keys, wide_weights),
        vmem(4),
        [],
        6 * rows * width,
        0,
        16 * rows * width,
    )
    pair_ahead = from_ahead(pair, "blk", FAR)
    img_behind = from_ahead(img_block, "blk", -FAR)
    txt_after = from_ahead(txt_block, "blk", 1)
    txt_before = from_ahead(txt_block, "blk", -1)
    sums, pair_part, img_part, before_part, after_part, own_part = call(
        tile_kernel,
        [
            full(8, 128),
            half(2 * rows, width),
            half(rows, width),
            half(rows, width),
            half(rows, width),
            full(rows, width),
        ],
        (
            scale,
            shift,
            weights.reshape(1, rows),
            pair_ahead,
            img_behind,
            txt_before,
            txt_block,
            txt_after,
        ),
        [pl.BlockSpec(memory_space=pltpu.SMEM)] * 2 + vmem(6),
        [
            pltpu.VMEM((4 * rows, width), jnp.bfloat16),
            pltpu.VMEM((2 * rows, width), jnp.bfloat16),
            pltpu.VMEM((2 * rows, 4 * rows), jnp.float32),
            pltpu.VMEM((2 * rows, 4 * rows), jnp.bfloat16),
            pltpu.VMEM((2 * rows, EXTRA), jnp.float32),
        ],
        48 * rows * rows * width,
        24 * rows * rows,
        28 * rows * width,
    )
    pair_back = from_ahead(pair_part, "blk", -FAR)
    far_back = from_ahead(img_part, "blk", FAR)
    after_back = from_ahead(before_part, "blk", 1)
    before_back = from_ahead(after_part, "blk", -1)
    image_grad, text_grad = call(
        finish_kernel,
        [full(rows, width), full(rows, width)],
        (
            image_emb,
            text_emb,
            pair_back,
            far_back,
            after_back,
            before_back,
            own_part,
        ),
        vmem(7),
        [],
        20 * rows * width,
        0,
        30 * rows * width,
    )
    sums = sum_over(sum_over(sums[0:1], "blk"), "group")
    loss = sums[0, 0:1] / sums[0, 1:2]
    return (loss, image_grad, text_grad)


def solution(mesh):
    split = ("blk", "group")
    placed = (P(split, None), P(split, None), P(split), P(split), P(), P())
    return jax.shard_map(
        per_device,
        mesh=mesh,
        in_specs=placed,
        out_specs=(P(), P(split, None), P(split, None)),
        check_vma=False,
    )
```

time: 508 us -> 143 us (0.28)
  waiting for transfers between devices: 231 us -> 9.73 us
  blocking collectives: 174 us -> 46.1 us
  starting transfers between devices: 83.6 us -> 69.1 us
  matrix products: 8.47 us -> 0 us
  Pallas kernels: 0 us -> 7.65 us
    ppermute x24 -> x8, waiting for transfers between devices: 231 us -> 9.73 us  [from_ahead(): return lax.ppermute(value, axis, pairs)]
    psum x1 -> x0, blocking collectives: 174 us -> none  [per_device(): totals = lax.psum((loss_part, weight_part), ('blk', 'group'))]
    all_to_all x0 -> x1, blocking collectives: none -> 46.1 us  [sum_over(): gathered = lax.all_to_all(spread, axis, 0, 0, tiled=True)]
    ppermute x24 -> x8, starting transfers between devices: 83.6 us -> 43.6 us  [from_ahead(): return lax.ppermute(value, axis, pairs)]
    all_to_all x0 -> x1, starting transfers between devices: none -> 25.5 us  [sum_over(): gathered = lax.all_to_all(spread, axis, 0, 0, tiled=True)]
    dot_general x24 -> x0, matrix products: 8.47 us -> none  [the longest x8 3.25 us: multiplier_matrix(): jnp.einsum('rd,sd->rs', picture_features_halfwidth, caption_features_half...]
    pallas_call x0 -> x3, Pallas kernels: none -> 7.65 us  [call(): pl.pallas_call(kernel, out_shape=outs, in_specs=specs, out_specs=vmem(len...]
  transfers between devices with their start and end apart: 24 -> 9, of which waited for: 20 -> 1; matrix products, arithmetic and copies ran while one was open for 1% -> 1% of each run, Pallas kernels for 0% -> 0%
where the time goes in v1:
time: 143 us
  starting transfers between devices  69.1 us (48%)
  blocking collectives  46.1 us (32%)
  waiting for transfers between devices  9.73 us (7%)
  Pallas kernels  7.65 us (5%)
  local copies, waits for them, and re-layouts  4.82 us (3%)
  between operations  4.61 us (3%)
    all_to_all x1, blocking collectives, sum_over(): gathered = lax.all_to_all(spread, axis, 0, 0, tiled=True)  46.1 us
    ppermute x8, starting transfers between devices, from_ahead(): return lax.ppermute(value, axis, pairs)  43.6 us
    all_to_all x1, starting transfers between devices, sum_over(): gathered = lax.all_to_all(spread, axis, 0, 0, tiled=True)  25.5 us
    ppermute x8, waiting for transfers between devices, from_ahead(): return lax.ppermute(value, axis, pairs)  9.73 us
    pallas_call x3, Pallas kernels, call(): pl.pallas_call(kernel, out_shape=outs, in_specs=specs, out_specs=vmem(len...  7.65 us
  transfers between devices with their start and end apart: 9, of which 1 were waited for; matrix products, arithmetic and copies ran while one was open for 1% of the time, Pallas kernels for 0%

profile of v1, /device:TPU:1, one launch (start us, length us, event | category | flops | bytes accessed | tf_op | source)
XLA Modules:
  0.0 142.8 jit_solution(17999924320579909495)
XLA Ops:
  0.6 0.7 tile.4
  1.3 0.0 copy-start.4
  1.3 0.1 reshape_tile.6.key_ref
  1.4 0.6 copy-done.4
  2.0 0.1 reshape_tile.7.weight_ref
  2.1 0.0 copy-start
  2.1 1.1 copy-done
  3.1 0.0 copy-start.2
  3.1 1.1 copy-done.2
  4.2 0.2 shard_map.85
  4.4 16.2 %collective-permute-start = (bf16[416,768]{1,0:T(8,128)(2,1)S(1)}, bf16[416,768]{1,0:T(8,128)(2,1)S(1)}, u32[]{:S(2)}, u32[]{:S(2)}) collective-permute-start(bf16[416,768]{1,0:T(8,128)(2,1)S(1)} %get-tuple-element.14), channel_id=1, source_target_pairs={{32,0},{48,16},{64,32},{80,48},{96,64},{112,80},{128,96},{144,112}... | collective-permute-start | bytes 1916936 | tf_op jit(solution)/shard_map/ppermute | solution.py:17
  20.6 1.9 %collective-permute-start.1 = (bf16[208,768]{1,0:T(8,128)(2,1)S(1)}, bf16[208,768]{1,0:T(8,128)(2,1)S(1)}, u32[]{:S(2)}, u32[]{:S(2)}) collective-permute-start(bf16[208,768]{1,0:T(8,128)(2,1)S(1)} %get-tuple-element.15), channel_id=1, source_target_pairs={{992,0},{1008,16},{0,32},{16,48},{32,64},{48,80},{64,96},{80,112},... | collective-permute-start | bytes 958472 | tf_op jit(solution)/shard_map/ppermute | solution.py:17
  22.5 3.8 %collective-permute-start.3 = (bf16[208,768]{1,0:T(8,128)(2,1)S(1)}, bf16[208,768]{1,0:T(8,128)(2,1)S(1)}, u32[]{:S(2)}, u32[]{:S(2)}) collective-permute-start(bf16[208,768]{1,0:T(8,128)(2,1)S(1)} %get-tuple-element.16.own_ref), channel_id=1, source_target_pairs={{16,0},{32,16},{48,32},{64,48},{80,64},{96,80},{112,96},{128,112},... | collective-permute-start | bytes 958472 | tf_op jit(solution)/shard_map/ppermute | solution.py:17
  26.4 1.9 %collective-permute-start.2 = (bf16[208,768]{1,0:T(8,128)(2,1)S(1)}, bf16[208,768]{1,0:T(8,128)(2,1)S(1)}, u32[]{:S(2)}, u32[]{:S(2)}) collective-permute-start(bf16[208,768]{1,0:T(8,128)(2,1)S(1)} %get-tuple-element.16.own_ref), channel_id=1, source_target_pairs={{1008,0},{0,16},{16,32},{32,48},{48,64},{64,80},{80,96},{96,112},{... | collective-permute-start | bytes 958472 | tf_op jit(solution)/shard_map/ppermute | solution.py:17
  29.6 9.7 %collective-permute-done.1.img_ref = bf16[208,768]{1,0:T(8,128)(2,1)S(1)} collective-permute-done((bf16[208,768]{1,0:T(8,128)(2,1)S(1)}, bf16[208,768]{1,0:T(8,128)(2,1)S(1)}, u32[]{:S(2)}, u32[]{:S(2)}) %collective-permute-start.1) | collective-permute-done | bytes 319520 | tf_op jit(solution)/shard_map/ppermute | solution.py:17
  39.3 0.0 collective-permute-done.3.after_ref
  39.3 0.0 collective-permute-done.2.before_ref
  39.3 0.0 collective-permute-done.pair_ref
  39.3 0.0 copy-start.1
  39.3 0.0 copy-start.3
  39.3 5.9 %shard_map.86 = (f32[8,128]{1,0:T(8,128)S(1)}, bf16[384,768]{1,0:T(8,128)(2,1)}, bf16[192,768]{1,0:T(8,128)(2,1)}, bf16[192,768]{1,0:T(8,128)(2,1)}, bf16[192,76...) custom-call(f32[1]{0:T(128)S(6)} %copy.11.scale_ref, f32[1]{0:T(128)S(6)} %copy.12.shift_ref, f32[1,192]{1,0:T(1,128)S(1)} %bitcast.7, ...), custom_call_target="tpu_custom_call" | custom-call | flops 1358954496 | bytes 4128768 | tf_op jit(solution)/shard_map/pallas_call | solution.py:29
  45.3 1.9 %collective-permute-start.4 = (bf16[384,768]{1,0:T(8,128)(2,1)}, bf16[384,768]{1,0:T(8,128)(2,1)S(1)}, u32[]{:S(2)}, u32[]{:S(2)}) collective-permute-start(bf16[384,768]{1,0:T(8,128)(2,1)} %get-tuple-element.18), channel_id=1, source_target_pairs={{992,0},{1008,16},{0,32},{16,48},{32,64},{48,80},{64,96},{80,112},... | collective-permute-start | bytes 1769480 | tf_op jit(solution)/shard_map/ppermute | solution.py:17
  47.2 0.6 broadcast_in_dim.6
  47.8 25.5 %all-to-all-start = ((f32[64,1,128]{2,1,0:T(1,128)}), f32[64,1,128]{2,1,0:T(1,128)}, u32[]{:S(2)}, u32[]{:S(2)}) async-start(f32[64,1,128]{2,1,0:T(1,128)} %broadcast_in_dim.6), calls=%async_computation | async-start | bytes 65536 | tf_op jit(solution)/shard_map/all_to_all | solution.py:191
  73.3 12.3 %collective-permute-start.5 = (bf16[192,768]{1,0:T(8,128)(2,1)}, bf16[192,768]{1,0:T(8,128)(2,1)S(1)}, u32[]{:S(2)}, u32[]{:S(2)}) collective-permute-start(bf16[192,768]{1,0:T(8,128)(2,1)} %get-tuple-element.19), channel_id=1, source_target_pairs={{32,0},{48,16},{64,32},{80,48},{96,64},{112,80},{128,96},{144,112}... | collective-permute-start | bytes 884744 | tf_op jit(solution)/shard_map/ppermute | solution.py:17
  85.6 2.5 %collective-permute-start.6 = (bf16[192,768]{1,0:T(8,128)(2,1)}, bf16[192,768]{1,0:T(8,128)(2,1)S(1)}, u32[]{:S(2)}, u32[]{:S(2)}) collective-permute-start(bf16[192,768]{1,0:T(8,128)(2,1)} %get-tuple-element.20), channel_id=1, source_target_pairs={{16,0},{32,16},{48,32},{64,48},{80,64},{96,80},{112,96},{128,112},... | collective-permute-start | bytes 884744 | tf_op jit(solution)/shard_map/ppermute | solution.py:17
  88.1 3.0 %collective-permute-start.7 = (bf16[192,768]{1,0:T(8,128)(2,1)S(1)}, bf16[192,768]{1,0:T(8,128)(2,1)S(1)}, u32[]{:S(2)}, u32[]{:S(2)}) collective-permute-start(bf16[192,768]{1,0:T(8,128)(2,1)S(1)} %get-tuple-element.21), channel_id=1, source_target_pairs={{1008,0},{0,16},{16,32},{32,48},{48,64},{64,80},{80,96},{96,112},{... | collective-permute-start | bytes 884744 | tf_op jit(solution)/shard_map/ppermute | solution.py:17
  91.2 0.0 all-to-all-done
  91.2 0.8 reduce_sum.18
  92.0 46.1 %all_to_all.12 = f32[16,1,128]{2,1,0:T(1,128)S(1)} all-to-all(f32[16,1,128]{2,1,0:T(1,128)S(1)} %broadcast_in_dim.7), channel_id=1, replica_groups=mesh['blk'=64,'group'=16] {'group'}, dimensions={0} | all-to-all | bytes 16384 | tf_op jit(solution)/shard_map/all_to_all | solution.py:191
  138.1 0.6 fusion
  140.1 0.0 collective-permute-done.5.far_ref
  140.1 0.0 collective-permute-done.6.after_ref
  140.1 0.0 collective-permute-done.7.before_ref
  140.1 0.0 collective-permute-done.4.pair_ref
  140.2 0.0 copy-done.1
  140.2 0.0 copy-done.3
  140.2 1.5 %shard_map.87 = (f32[192,768]{1,0:T(8,128)}, f32[192,768]{1,0:T(8,128)}) custom-call(f32[192,768]{1,0:T(8,128)S(1)} %copy-done.1, f32[192,768]{1,0:T(8,128)S(1)} %copy-done.3, bf16[384,768]{1,0:T(8,128)(2,1)S(1)} %collective-permute-done.4.pair_ref, bf16[192,768]{1,0:T(8,128)(2,1)S(1)} %collective-permute-done.5.far_ref, ...), custom_call_target="tpu_custom_call" | custom-call | flops 2949120 | bytes 4423680 | tf_op jit(solution)/shard_map/pallas_call | solution.py:29
  (4 shorter events, 0.0 us)
Async XLA Ops:
  1.3 0.7 copy-start.4
  2.1 1.1 copy-start
  3.1 1.1 copy-start.2
  4.4 34.9 %collective-permute-start = (bf16[416,768]{1,0:T(8,128)(2,1)S(1)}, bf16[416,768]{1,0:T(8,128)(2,1)S(1)}, u32[]{:S(2)}, u32[]{:S(2)}) collective-permute-start(bf16[416,768]{1,0:T(8,128)(2,1)S(1)} %get-tuple-element.14), channel_id=1, source_target_pairs={{32,0},{48,16},{64,32},{80,48},{96,64},{112,80},{128,96},{144,112}... | collective-permute-start | bytes 1916936 | tf_op jit(solution)/shard_map/ppermute | solution.py:17
  20.6 18.7 %collective-permute-start.1 = (bf16[208,768]{1,0:T(8,128)(2,1)S(1)}, bf16[208,768]{1,0:T(8,128)(2,1)S(1)}, u32[]{:S(2)}, u32[]{:S(2)}) collective-permute-start(bf16[208,768]{1,0:T(8,128)(2,1)S(1)} %get-tuple-element.15), channel_id=1, source_target_pairs={{992,0},{1008,16},{0,32},{16,48},{32,64},{48,80},{64,96},{80,112},... | collective-permute-start | bytes 958472 | tf_op jit(solution)/shard_map/ppermute | solution.py:17
  22.5 16.8 %collective-permute-start.3 = (bf16[208,768]{1,0:T(8,128)(2,1)S(1)}, bf16[208,768]{1,0:T(8,128)(2,1)S(1)}, u32[]{:S(2)}, u32[]{:S(2)}) collective-permute-start(bf16[208,768]{1,0:T(8,128)(2,1)S(1)} %get-tuple-element.16.own_ref), channel_id=1, source_target_pairs={{16,0},{32,16},{48,32},{64,48},{80,64},{96,80},{112,96},{128,112},... | collective-permute-start | bytes 958472 | tf_op jit(solution)/shard_map/ppermute | solution.py:17
  26.4 12.9 %collective-permute-start.2 = (bf16[208,768]{1,0:T(8,128)(2,1)S(1)}, bf16[208,768]{1,0:T(8,128)(2,1)S(1)}, u32[]{:S(2)}, u32[]{:S(2)}) collective-permute-start(bf16[208,768]{1,0:T(8,128)(2,1)S(1)} %get-tuple-element.16.own_ref), channel_id=1, source_target_pairs={{1008,0},{0,16},{16,32},{32,48},{48,64},{64,80},{80,96},{96,112},{... | collective-permute-start | bytes 958472 | tf_op jit(solution)/shard_map/ppermute | solution.py:17
  39.3 100.8 %copy-start.1 = (f32[192,768]{1,0:T(8,128)S(1)}, f32[192,768]{1,0:T(8,128)}, u32[]{:S(2)}) copy-start(f32[192,768]{1,0:T(8,128)} %img_ref.3) | copy-start | bytes 1769476
  39.3 100.8 %copy-start.3 = (f32[192,768]{1,0:T(8,128)S(1)}, f32[192,768]{1,0:T(8,128)}, u32[]{:S(2)}) copy-start(f32[192,768]{1,0:T(8,128)} %txt_ref.3) | copy-start | bytes 1769476
  45.3 94.9 %collective-permute-start.4 = (bf16[384,768]{1,0:T(8,128)(2,1)}, bf16[384,768]{1,0:T(8,128)(2,1)S(1)}, u32[]{:S(2)}, u32[]{:S(2)}) collective-permute-start(bf16[384,768]{1,0:T(8,128)(2,1)} %get-tuple-element.18), channel_id=1, source_target_pairs={{992,0},{1008,16},{0,32},{16,48},{32,64},{48,80},{64,96},{80,112},... | collective-permute-start | bytes 1769480 | tf_op jit(solution)/shard_map/ppermute | solution.py:17
  47.8 43.4 %all-to-all-start = ((f32[64,1,128]{2,1,0:T(1,128)}), f32[64,1,128]{2,1,0:T(1,128)}, u32[]{:S(2)}, u32[]{:S(2)}) async-start(f32[64,1,128]{2,1,0:T(1,128)} %broadcast_in_dim.6), calls=%async_computation | async-start | bytes 65536 | tf_op jit(solution)/shard_map/all_to_all | solution.py:191
  73.3 66.9 %collective-permute-start.5 = (bf16[192,768]{1,0:T(8,128)(2,1)}, bf16[192,768]{1,0:T(8,128)(2,1)S(1)}, u32[]{:S(2)}, u32[]{:S(2)}) collective-permute-start(bf16[192,768]{1,0:T(8,128)(2,1)} %get-tuple-element.19), channel_id=1, source_target_pairs={{32,0},{48,16},{64,32},{80,48},{96,64},{112,80},{128,96},{144,112}... | collective-permute-start | bytes 884744 | tf_op jit(solution)/shard_map/ppermute | solution.py:17
  85.6 54.5 %collective-permute-start.6 = (bf16[192,768]{1,0:T(8,128)(2,1)}, bf16[192,768]{1,0:T(8,128)(2,1)S(1)}, u32[]{:S(2)}, u32[]{:S(2)}) collective-permute-start(bf16[192,768]{1,0:T(8,128)(2,1)} %get-tuple-element.20), channel_id=1, source_target_pairs={{16,0},{32,16},{48,32},{64,48},{80,64},{96,80},{112,96},{128,112},... | collective-permute-start | bytes 884744 | tf_op jit(solution)/shard_map/ppermute | solution.py:17
  88.1 52.0 %collective-permute-start.7 = (bf16[192,768]{1,0:T(8,128)(2,1)S(1)}, bf16[192,768]{1,0:T(8,128)(2,1)S(1)}, u32[]{:S(2)}, u32[]{:S(2)}) collective-permute-start(bf16[192,768]{1,0:T(8,128)(2,1)S(1)} %get-tuple-element.21), channel_id=1, source_target_pairs={{1008,0},{0,16},{16,32},{32,48},{48,64},{64,80},{80,96},{96,112},{... | collective-permute-start | bytes 884744 | tf_op jit(solution)/shard_map/ppermute | solution.py:17

commit v2 on v1

--- a/solution.py
+++ b/solution.py
@@ -8,7 +8,9 @@
 EXTRA = 16
 CHUNK = 32
 FAR = 2
-VMEM_BYTES = 32 * 1024 * 1024
+VMEM_BYTES = 16 * 1024 * 1024
+PLANE = 8
+Z_HI = 4
 
 
 def from_ahead(value, axis, steps):
@@ -25,30 +27,38 @@
     return [pl.BlockSpec(memory_space=pltpu.VMEM)] * count
 
 
-def call(kernel, outs, args, specs, scratch, flops, transcendentals, moved):
+def call(kernel, outs, args, specs, scratch, flops, transcendentals, moved, limit):
     return pl.pallas_call(
         kernel,
         out_shape=outs,
         in_specs=specs,
         out_specs=vmem(len(outs)),
         scratch_shapes=scratch,
-        compiler_params=pltpu.CompilerParams(vmem_limit_bytes=VMEM_BYTES),
+        compiler_params=pltpu.CompilerParams(vmem_limit_bytes=limit),
         cost_estimate=pl.CostEstimate(
             flops=flops, bytes_accessed=moved, transcendentals=transcendentals
         ),
     )(*args)
 
 
-def prepare_kernel(img_ref, txt_ref, key_ref, weight_ref, pair_ref, img_out, txt_out):
-    rows, width = img_ref.shape
+def prepare_kernel(
+    img_ref, txt_ref, key_ref, weight_ref, pair_ref, txt_out, img_out, again_out, img_buf, txt_buf, sems
+):
+    rows, width = img_buf.shape
     block = rows + EXTRA
+    copies = [
+        pltpu.make_async_copy(source, target, sems.at[number])
+        for number, (source, target) in enumerate(((img_ref, img_buf), (txt_ref, txt_buf)))
+    ]
+    for copy in copies:
+        copy.start()
     key = key_ref[...]
     weight = weight_ref[...]
     high = weight.astype(jnp.bfloat16).astype(jnp.float32)
     middle = (weight - high).astype(jnp.bfloat16).astype(jnp.float32)
     low = (weight - high) - middle
-    line = lax.broadcasted_iota(jnp.int32, (EXTRA, width), 0)
-    extra = jnp.zeros((EXTRA, width), jnp.float32)
+    line = lax.broadcasted_iota(jnp.int32, (EXTRA, rows), 0)
+    extra = jnp.zeros((EXTRA, rows), jnp.float32)
     parts = (
         (key >> 8).astype(jnp.float32),
         (key & 255).astype(jnp.float32),
@@ -58,49 +68,61 @@
     )
     for number, part in enumerate(parts):
         extra = jnp.where(line == number, part, extra)
-    extra = extra.astype(jnp.bfloat16)
-    for start, source, alone in ((0, img_ref, img_out), (block, txt_ref, txt_out)):
+    place = lax.broadcasted_iota(jnp.int32, (rows, width), 1) - lax.broadcasted_iota(
+        jnp.int32, (rows, width), 0
+    )
+    hit = place == 0
+    for number in range(1, width // rows):
+        hit = jnp.logical_or(hit, place == number * rows)
+    extra = jnp.dot(
+        extra.astype(jnp.bfloat16),
+        jnp.where(hit, 1.0, 0.0).astype(jnp.bfloat16),
+        preferred_element_type=jnp.float32,
+    ).astype(jnp.bfloat16)
+    for start, source, alone, copy in (
+        (0, img_buf, (img_out,), copies[0]),
+        (block, txt_buf, (txt_out, again_out), copies[1]),
+    ):
+        copy.wait()
         values = source[...]
         unit = (values / row_norms(values)).astype(jnp.bfloat16)
-        alone[0:rows, :] = unit
-        alone[rows:block, :] = extra
-        pair_ref[start : start + rows, :] = unit
-        pair_ref[start + rows : start + block, :] = extra
-
-
-def tile_kernel(
-    scale_ref,
-    shift_ref,
-    weight_ref,
-    pair_ref,
-    img_ref,
-    before_ref,
-    own_ref,
-    after_ref,
-    sums_ref,
-    pair_out,
-    img_out,
-    before_out,
-    after_out,
-    own_out,
-    txts,
-    imgs,
-    scores,
-    factors,
-    columns,
-):
-    rows = own_ref.shape[0] - EXTRA
-    width = own_ref.shape[1]
+        for target in (*alone, pair_ref.at[start : start + block]):
+            target[0:rows, :] = unit
+            target[rows:block, :] = extra
+
+
+def stack_blocks(rows, pair_ref, after_ref, img_ref, before_ref, own_ref, txts, imgs):
     block = rows + EXTRA
-    scale = scale_ref[0]
-    shift = shift_ref[0]
-
     imgs[0:rows, :] = pair_ref[0:rows, :]
     imgs[rows : 2 * rows, :] = img_ref[0:rows, :]
     txts[0:rows, :] = before_ref[0:rows, :]
     txts[rows : 2 * rows, :] = own_ref[0:rows, :]
     txts[2 * rows : 3 * rows, :] = after_ref[0:rows, :]
     txts[3 * rows : 4 * rows, :] = pair_ref[block : block + rows, :]
+
+
+def score_kernel(
+    scale_ref,
+    shift_ref,
+    weight_ref,
+    pair_ref,
+    after_ref,
+    img_ref,
+    before_ref,
+    own_ref,
+    sums_ref,
+    factors,
+    txts,
+    imgs,
+    scores,
+    columns,
+):
+    rows = own_ref.shape[0] - EXTRA
+    block = rows + EXTRA
+    scale = scale_ref[0]
+    shift = shift_ref[0]
+
+    stack_blocks(rows, pair_ref, after_ref, img_ref, before_ref, own_ref, txts, imgs)
 
     lane = lax.broadcasted_iota(jnp.int32, (1, 4 * rows), 1)
     txt_keys = jnp.zeros((1, 4 * rows), jnp.float32)
@@ -153,6 +175,24 @@
         place == 0, loss_part, jnp.where(place == 1, weight_part, 0.0)
     )
 
+
+def grad_kernel(
+    factors,
+    pair_ref,
+    after_ref,
+    img_ref,
+    before_ref,
+    own_ref,
+    pair_out,
+    img_out,
+    before_out,
+    after_out,
+    own_out,
+    txts,
+    imgs,
+):
+    rows = own_out.shape[0]
+    stack_blocks(rows, pair_ref, after_ref, img_ref, before_ref, own_ref, txts, imgs)
     img_grads = jnp.dot(factors[...], txts[...], preferred_element_type=jnp.float32)
     img_grads = img_grads.astype(jnp.bfloat16)
     pair_out[0:rows, :] = img_grads[0:rows]
@@ -167,7 +207,8 @@
 
 
 def finish_kernel(
-    img_ref, txt_ref, pair_ref, far_ref, after_ref, before_ref, own_ref, img_out, txt_out
+    img_ref, txt_ref, pair_ref, before_ref, far_ref, after_ref, own_ref, sums_ref,
+    img_out, txt_out, loss_out
 ):
     rows = img_ref.shape[0]
 
@@ -183,13 +224,27 @@
         (own_ref[...] + wide(before_ref[...]))
         + (wide(after_ref[...]) + wide(pair_ref[rows : 2 * rows, :])),
     )
-
-
-def sum_over(part, axis):
-    count = lax.axis_size(axis)
-    spread = jnp.broadcast_to(part, (count, part.shape[-1]))
-    gathered = lax.all_to_all(spread, axis, 0, 0, tiled=True)
-    return jnp.sum(gathered, 0, keepdims=True)
+    sums = jnp.sum(sums_ref[...], 0, keepdims=True)
+    loss_out[...] = sums[:, 0:1] / sums[:, 1:2]
+
+
+def exchange(part, groups):
+    count = len(groups[0])
+    spread = jnp.broadcast_to(part.reshape(1, 1, -1), (count, 1, part.shape[-1]))
+    return lax.all_to_all(
+        spread, ("blk", "group"), 0, 0, tiled=True, axis_index_groups=groups
+    ).reshape(count, -1)
+
+
+def plane_and_column_groups():
+    blk, group = lax.axis_size("blk"), lax.axis_size("group")
+    planes, columns = {}, {}
+    for number in range(blk * group):
+        first, second = number // group, number % group
+        z = (second % Z_HI, first // PLANE)
+        planes.setdefault(z, []).append(number)
+        columns.setdefault((first % PLANE, second // Z_HI), []).append(number)
+    return list(planes.values()), list(columns.values())
 
 
 def per_device(image_emb, text_emb, keys, weights, scale, shift):
@@ -197,80 +252,95 @@
     block = rows + EXTRA
     half = lambda *shape: jax.ShapeDtypeStruct(shape, jnp.bfloat16)
     full = lambda *shape: jax.ShapeDtypeStruct(shape, jnp.float32)
-    repeats = width // rows
-    wide_keys = jnp.tile(keys, repeats).reshape(1, width)
-    wide_weights = jnp.tile(weights, repeats).reshape(1, width)
-    pair, img_block, txt_block = call(
+    smem = [pl.BlockSpec(memory_space=pltpu.SMEM)] * 2
+    hbm = [pl.BlockSpec(memory_space=pltpu.HBM)] * 2
+    row_weights = weights.reshape(1, rows)
+    fixed = [pltpu.with_memory_space_constraint(x, pltpu.HBM) for x in (image_emb, text_emb)]
+    pair, txt_block, img_block, txt_again = call(
         prepare_kernel,
-        [half(2 * block, width), half(block, width), half(block, width)],
-        (image_emb, text_emb, wide_keys, wide_weights),
-        vmem(4),
-        [],
+        [half(2 * block, width)] + [half(block, width)] * 3,
+        (*fixed, keys.reshape(1, rows), row_weights),
+        hbm + vmem(2),
+        [
+            pltpu.VMEM((rows, width), jnp.float32),
+            pltpu.VMEM((rows, width), jnp.float32),
+            pltpu.SemaphoreType.DMA((2,)),
+        ],
         6 * rows * width,
         0,
         16 * rows * width,
+        VMEM_BYTES,
     )
     pair_ahead = from_ahead(pair, "blk", FAR)
+    txt_after = from_ahead(txt_block, "blk", 1)
     img_behind = from_ahead(img_block, "blk", -FAR)
-    txt_after = from_ahead(txt_block, "blk", 1)
-    txt_before = from_ahead(txt_block, "blk", -1)
-    sums, pair_part, img_part, before_part, after_part, own_part = call(
-        tile_kernel,
+    txt_before = from_ahead(txt_again, "blk", -1)
+    blocks = (pair_ahead, txt_after, img_behind, txt_before, txt_block)
+    stacks = [
+        pltpu.VMEM((4 * rows, width), jnp.bfloat16),
+        pltpu.VMEM((2 * rows, width), jnp.bfloat16),
+    ]
+    sums, factors = call(
+        score_kernel,
+        [full(8, 128), half(2 * rows, 4 * rows)],
+        (scale, shift, row_weights, *blocks),
+        smem + vmem(6),
+        stacks
+        + [
+            pltpu.VMEM((2 * rows, 4 * rows), jnp.float32),
+            pltpu.VMEM((2 * rows, EXTRA), jnp.float32),
+        ],
+        16 * rows * rows * width,
+        24 * rows * rows,
+        28 * rows * width,
+        VMEM_BYTES,
+    )
+    parts = call(
+        grad_kernel,
         [
-            full(8, 128),
             half(2 * rows, width),
             half(rows, width),
             half(rows, width),
             half(rows, width),
             full(rows, width),
         ],
-        (
-            scale,
-            shift,
-            weights.reshape(1, rows),
-            pair_ahead,
-            img_behind,
-            txt_before,
-            txt_block,
-            txt_after,
-        ),
-        [pl.BlockSpec(memory_space=pltpu.SMEM)] * 2 + vmem(6),
-        [
-            pltpu.VMEM((4 * rows, width), jnp.bfloat16),
-            pltpu.VMEM((2 * rows, width), jnp.bfloat16),
-            pltpu.VMEM((2 * rows, 4 * rows), jnp.float32),
-            pltpu.VMEM((2 * rows, 4 * rows), jnp.bfloat16),
-            pltpu.VMEM((2 * rows, EXTRA), jnp.float32),
-        ],
-        48 * rows * rows * width,
-        24 * rows * rows,
+        (factors, *blocks),
+        vmem(6),
+        stacks,
+        32 * rows * rows * width,
+        0,
         28 * rows * width,
-    )
+        VMEM_BYTES,
+    )
+    planes, columns = plane_and_column_groups()
+    gathered = exchange(sums[0:1], planes)
+    pair_part, img_part, before_part, after_part, own_part = parts
     pair_back = from_ahead(pair_part, "blk", -FAR)
+    before_back = from_ahead(after_part, "blk", -1)
     far_back = from_ahead(img_part, "blk", FAR)
     after_back = from_ahead(before_part, "blk", 1)
-    before_back = from_ahead(after_part, "blk", -1)
-    image_grad, text_grad = call(
+    gathered = exchange(jnp.sum(gathered, 0, keepdims=True), columns)
+    image_grad, text_grad, loss = call(
         finish_kernel,
-        [full(rows, width), full(rows, width)],
+        [full(rows, width), full(rows, width), full(1, 1)],
         (
             image_emb,
             text_emb,
             pair_back,
+            before_back,
             far_back,
             after_back,
-            before_back,
             own_part,
+            gathered,
         ),
-        vmem(7),
+        vmem(8),
         [],
         20 * rows * width,
         0,
         30 * rows * width,
-    )
-    sums = sum_over(sum_over(sums[0:1], "blk"), "group")
-    loss = sums[0, 0:1] / sums[0, 1:2]
-    return (loss, image_grad, text_grad)
+        VMEM_BYTES,
+    )
+    return (loss.reshape(1), image_grad, text_grad)
 
 
 def solution(mesh):

time: 143 us -> 124 us (0.87)
  starting transfers between devices: 69.1 us -> 47.5 us
  blocking collectives: 46.1 us -> 54 us
  local copies, waits for them, and re-layouts: 4.82 us -> 1.36 us
  between operations: 4.61 us -> 2.07 us
    all_to_all x1 -> x0, starting transfers between devices: 25.5 us -> none  [sum_over(): gathered = lax.all_to_all(spread, axis, 0, 0, tiled=True)]
    all_to_all x1 -> x2, blocking collectives: 46.1 us -> 54 us  [exchange(): lax.all_to_all(spread, ('blk', 'group'), 0, 0, tiled=True, axis_index_gro...]
    ppermute x8, starting transfers between devices: 43.6 us -> 47.5 us  [from_ahead(): return lax.ppermute(value, axis, pairs)]
    unnamed x10 -> x8, local copies, waits for them, and re-layouts: 2.73 us -> 0.69 us
    pallas_call x3 -> x4, Pallas kernels: 7.65 us -> 8.75 us  [call(): pl.pallas_call(kernel, out_shape=outs, in_specs=specs, out_specs=vmem(len...]
  transfers between devices with their start and end apart: 9 -> 8, of which waited for: 1 -> 1; matrix products, arithmetic and copies ran while one was open for 1% -> 1% of each run, Pallas kernels for 0% -> 0%
where the time goes in v2:
time: 124 us
  blocking collectives  54 us (44%)
  starting transfers between devices  47.5 us (38%)
  waiting for transfers between devices  9.73 us (8%)
  Pallas kernels  8.75 us (7%)
  between operations  2.07 us (2%)
  local copies, waits for them, and re-layouts  1.36 us (1%)
    all_to_all x2, blocking collectives, exchange(): lax.all_to_all(spread, ('blk', 'group'), 0, 0, tiled=True, axis_index_gro...  54 us
    ppermute x8, starting transfers between devices, from_ahead(): return lax.ppermute(value, axis, pairs)  47.5 us
    ppermute x8, waiting for transfers between devices, from_ahead(): return lax.ppermute(value, axis, pairs)  9.73 us
    pallas_call x4, Pallas kernels, call(): pl.pallas_call(kernel, out_shape=outs, in_specs=specs, out_specs=vmem(len...  8.75 us
  transfers between devices with their start and end apart: 8, of which 1 were waited for; matrix products, arithmetic and copies ran while one was open for 1% of the time, Pallas kernels for 0%

profile of v2, /device:TPU:1, one launch (start us, length us, event | category | flops | bytes accessed | tf_op | source)
XLA Modules:
  0.0 123.9 jit_solution(3170190064737190556)
XLA Ops:
  0.6 0.0 copy-start.3
  0.6 0.0 copy-start.2
  0.7 0.7 copy-done.3
  1.3 0.0 copy-done.2
  1.3 1.4 %shard_map.85 = (bf16[416,768]{1,0:T(8,128)(2,1)S(1)}, bf16[208,768]{1,0:T(8,128)(2,1)S(1)}, bf16[208,768]{1,0:T(8,128)(2,1)S(1)}, bf16[208,768]{1,0:T(8,128)(2,1)S(1)}) custom-call(f32[192,768]{1,0:T(8,128)} %img_ref.3, f32[192,768]{1,0:T(8,128)} %txt_ref.3, s32[1,192]{1,0:T(1,128)S(1)} %bitcast.10, f32[1,192]{1,0:T(1,128)S(1)} %bitcast.8), custom_call_target="tpu_custom_call" | custom-call | flops 884736 | bytes 2359296 | tf_op jit(solution)/shard_map/pallas_call | solution.py:31
  2.8 16.2 %collective-permute-start = (bf16[416,768]{1,0:T(8,128)(2,1)S(1)}, bf16[416,768]{1,0:T(8,128)(2,1)S(1)}, u32[]{:S(2)}, u32[]{:S(2)}) collective-permute-start(bf16[416,768]{1,0:T(8,128)(2,1)S(1)} %get-tuple-element.17), channel_id=1, source_target_pairs={{32,0},{48,16},{64,32},{80,48},{96,64},{112,80},{128,96},{144,112}... | collective-permute-start | bytes 1916936 | tf_op jit(solution)/shard_map/ppermute | solution.py:19
  18.9 1.9 %collective-permute-start.2 = (bf16[208,768]{1,0:T(8,128)(2,1)S(1)}, bf16[208,768]{1,0:T(8,128)(2,1)S(1)}, u32[]{:S(2)}, u32[]{:S(2)}) collective-permute-start(bf16[208,768]{1,0:T(8,128)(2,1)S(1)} %get-tuple-element.19), channel_id=1, source_target_pairs={{992,0},{1008,16},{0,32},{16,48},{32,64},{48,80},{64,96},{80,112},... | collective-permute-start | bytes 958472 | tf_op jit(solution)/shard_map/ppermute | solution.py:19
  20.9 3.4 %collective-permute-start.3 = (bf16[208,768]{1,0:T(8,128)(2,1)S(1)}, bf16[208,768]{1,0:T(8,128)(2,1)S(1)}, u32[]{:S(2)}, u32[]{:S(2)}) collective-permute-start(bf16[208,768]{1,0:T(8,128)(2,1)S(1)} %get-tuple-element.20), channel_id=1, source_target_pairs={{1008,0},{0,16},{16,32},{32,48},{48,64},{64,80},{80,96},{96,112},{... | collective-permute-start | bytes 958472 | tf_op jit(solution)/shard_map/ppermute | solution.py:19
  24.3 2.3 %collective-permute-start.1 = (bf16[208,768]{1,0:T(8,128)(2,1)S(1)}, bf16[208,768]{1,0:T(8,128)(2,1)S(1)}, u32[]{:S(2)}, u32[]{:S(2)}) collective-permute-start(bf16[208,768]{1,0:T(8,128)(2,1)S(1)} %get-tuple-element.18.own_ref), channel_id=1, source_target_pairs={{16,0},{32,16},{48,32},{64,48},{80,64},{96,80},{112,96},{128,112},... | collective-permute-start | bytes 958472 | tf_op jit(solution)/shard_map/ppermute | solution.py:19
  27.9 9.7 %collective-permute-done.2.img_ref = bf16[208,768]{1,0:T(8,128)(2,1)S(1)} collective-permute-done((bf16[208,768]{1,0:T(8,128)(2,1)S(1)}, bf16[208,768]{1,0:T(8,128)(2,1)S(1)}, u32[]{:S(2)}, u32[]{:S(2)}) %collective-permute-start.2) | collective-permute-done | bytes 319520 | tf_op jit(solution)/shard_map/ppermute | solution.py:19
  37.6 0.0 collective-permute-done.3.before_ref
  37.6 0.0 collective-permute-done.1.after_ref
  37.6 0.0 collective-permute-done.pair_ref
  37.6 3.6 %shard_map.86 = (f32[8,128]{1,0:T(8,128)S(1)}, bf16[384,768]{1,0:T(8,128)(2,1)S(1)}) custom-call(f32[1]{0:T(128)S(6)} %copy.10.scale_ref, f32[1]{0:T(128)S(6)} %copy.11.shift_ref, f32[1,192]{1,0:T(1,128)S(1)} %bitcast.9, bf16[416,768]{1,0:T(8,128)(2,1)S(1)} %collective-permute-done.pair_ref, bf16[208,768]{1,0:T(8,128)(2,1)S(1)} %collective-permute-done.1.after_ref, ...), custom_call_target="tpu_custom_call" | custom-call | flops 452984832 | bytes 4128768 | tf_op jit(solution)/shard_map/pallas_call | solution.py:31
  41.2 0.0 copy-start
  41.2 0.0 copy-start.1
  41.2 2.2 %shard_map.87 = (bf16[384,768]{1,0:T(8,128)(2,1)}, bf16[192,768]{1,0:T(8,128)(2,1)}, bf16[192,768]{1,0:T(8,128)(2,1)S(1)}, bf16[192,768]{1,0:T(8,128)(2,1)}, f32[192,768]{1,0:T(8,128)S(1)}) custom-call(bf16[384,768]{1,0:T(8,128)(2,1)S(1)} %get-tuple-element.21.factors, bf16[416,768]{1,0:T(8,128)(2,1)S(1)} %collective-permute-done.pair_ref, ...), custom_call_target="tpu_custom_call" | custom-call | flops 905969664 | bytes 4128768 | tf_op jit(solution)/shard_map/pallas_call | solution.py:31
  43.4 1.9 %collective-permute-start.4 = (bf16[384,768]{1,0:T(8,128)(2,1)}, bf16[384,768]{1,0:T(8,128)(2,1)S(1)}, u32[]{:S(2)}, u32[]{:S(2)}) collective-permute-start(bf16[384,768]{1,0:T(8,128)(2,1)} %get-tuple-element.22), channel_id=1, source_target_pairs={{992,0},{1008,16},{0,32},{16,48},{32,64},{48,80},{64,96},{80,112},... | collective-permute-start | bytes 1769480 | tf_op jit(solution)/shard_map/ppermute | solution.py:19
  45.3 1.9 %collective-permute-start.5 = (bf16[192,768]{1,0:T(8,128)(2,1)}, bf16[192,768]{1,0:T(8,128)(2,1)S(1)}, u32[]{:S(2)}, u32[]{:S(2)}) collective-permute-start(bf16[192,768]{1,0:T(8,128)(2,1)} %get-tuple-element.23), channel_id=1, source_target_pairs={{1008,0},{0,16},{16,32},{32,48},{48,64},{64,80},{80,96},{96,112},{... | collective-permute-start | bytes 884744 | tf_op jit(solution)/shard_map/ppermute | solution.py:19
  47.2 17.2 %collective-permute-start.6 = (bf16[192,768]{1,0:T(8,128)(2,1)}, bf16[192,768]{1,0:T(8,128)(2,1)S(1)}, u32[]{:S(2)}, u32[]{:S(2)}) collective-permute-start(bf16[192,768]{1,0:T(8,128)(2,1)} %get-tuple-element.24), channel_id=1, source_target_pairs={{32,0},{48,16},{64,32},{80,48},{96,64},{112,80},{128,96},{144,112}... | collective-permute-start | bytes 884744 | tf_op jit(solution)/shard_map/ppermute | solution.py:19
  64.5 2.6 %collective-permute-start.7 = (bf16[192,768]{1,0:T(8,128)(2,1)S(1)}, bf16[192,768]{1,0:T(8,128)(2,1)S(1)}, u32[]{:S(2)}, u32[]{:S(2)}) collective-permute-start(bf16[192,768]{1,0:T(8,128)(2,1)S(1)} %get-tuple-element.25), channel_id=1, source_target_pairs={{16,0},{32,16},{48,32},{64,48},{80,64},{96,80},{112,96},{128,112},... | collective-permute-start | bytes 884744 | tf_op jit(solution)/shard_map/ppermute | solution.py:19
  67.1 12.6 %all_to_all.10 = f32[32,1,128]{2,1,0:T(1,128)S(1)} all-to-all(f32[32,1,128]{2,1,0:T(1,128)S(1)} %broadcast_in_dim.13), channel_id=1, replica_groups={{0,4,8,12,16,20,24,28,32,36,40,44,48,52,56,60,64,68,72,76,80,84,88,92,9..., dimensions={0} | all-to-all | bytes 32768 | tf_op jit(solution)/shard_map/all_to_all | solution.py:234
  79.8 0.5 reduce_sum.9
  80.3 0.7 broadcast_in_dim.14
  80.9 41.4 %all_to_all.11 = f32[32,1,128]{2,1,0:T(1,128)S(1)} all-to-all(f32[32,1,128]{2,1,0:T(1,128)S(1)} %broadcast_in_dim.14), channel_id=1, replica_groups={{0,1,2,3,128,129,130,131,256,257,258,259,384,385,386,387,512,513,514,51..., dimensions={0} | all-to-all | bytes 32768 | tf_op jit(solution)/shard_map/all_to_all | solution.py:234
  122.3 0.0 collective-permute-done.5.before_ref
  122.3 0.0 collective-permute-done.6.far_ref
  122.3 0.0 collective-permute-done.7.after_ref
  122.3 0.0 collective-permute-done.4.pair_ref
  122.3 0.0 copy-done
  122.3 0.0 copy-done.1
  122.4 1.6 %shard_map.88 = (f32[192,768]{1,0:T(8,128)}, f32[192,768]{1,0:T(8,128)}, f32[1,1]{1,0:T(1,128)}) custom-call(f32[192,768]{1,0:T(8,128)S(1)} %copy-done, f32[192,768]{1,0:T(8,128)S(1)} %copy-done.1, bf16[384,768]{1,0:T(8,128)(2,1)S(1)} %collective-permute-done.4.pair_ref, bf16[192,768]{1,0:T(8,128)(2,1)S(1)} %collective-permute-done.5.before_ref, ...), custom_call_target="tpu_custom_call" | custom-call | flops 2949120 | bytes 4423680 | tf_op jit(solution)/shard_map/pallas_call | solution.py:31
  (2 shorter events, 0.0 us)
Async XLA Ops:
  0.6 0.7 copy-start.3
  0.6 0.7 copy-start.2
  2.8 34.9 %collective-permute-start = (bf16[416,768]{1,0:T(8,128)(2,1)S(1)}, bf16[416,768]{1,0:T(8,128)(2,1)S(1)}, u32[]{:S(2)}, u32[]{:S(2)}) collective-permute-start(bf16[416,768]{1,0:T(8,128)(2,1)S(1)} %get-tuple-element.17), channel_id=1, source_target_pairs={{32,0},{48,16},{64,32},{80,48},{96,64},{112,80},{128,96},{144,112}... | collective-permute-start | bytes 1916936 | tf_op jit(solution)/shard_map/ppermute | solution.py:19
  18.9 18.7 %collective-permute-start.2 = (bf16[208,768]{1,0:T(8,128)(2,1)S(1)}, bf16[208,768]{1,0:T(8,128)(2,1)S(1)}, u32[]{:S(2)}, u32[]{:S(2)}) collective-permute-start(bf16[208,768]{1,0:T(8,128)(2,1)S(1)} %get-tuple-element.19), channel_id=1, source_target_pairs={{992,0},{1008,16},{0,32},{16,48},{32,64},{48,80},{64,96},{80,112},... | collective-permute-start | bytes 958472 | tf_op jit(solution)/shard_map/ppermute | solution.py:19
  20.9 16.8 %collective-permute-start.3 = (bf16[208,768]{1,0:T(8,128)(2,1)S(1)}, bf16[208,768]{1,0:T(8,128)(2,1)S(1)}, u32[]{:S(2)}, u32[]{:S(2)}) collective-permute-start(bf16[208,768]{1,0:T(8,128)(2,1)S(1)} %get-tuple-element.20), channel_id=1, source_target_pairs={{1008,0},{0,16},{16,32},{32,48},{48,64},{64,80},{80,96},{96,112},{... | collective-permute-start | bytes 958472 | tf_op jit(solution)/shard_map/ppermute | solution.py:19
  24.3 13.3 %collective-permute-start.1 = (bf16[208,768]{1,0:T(8,128)(2,1)S(1)}, bf16[208,768]{1,0:T(8,128)(2,1)S(1)}, u32[]{:S(2)}, u32[]{:S(2)}) collective-permute-start(bf16[208,768]{1,0:T(8,128)(2,1)S(1)} %get-tuple-element.18.own_ref), channel_id=1, source_target_pairs={{16,0},{32,16},{48,32},{64,48},{80,64},{96,80},{112,96},{128,112},... | collective-permute-start | bytes 958472 | tf_op jit(solution)/shard_map/ppermute | solution.py:19
  41.2 81.1 %copy-start = (f32[192,768]{1,0:T(8,128)S(1)}, f32[192,768]{1,0:T(8,128)}, u32[]{:S(2)}) copy-start(f32[192,768]{1,0:T(8,128)} %img_ref.3) | copy-start | bytes 1769476
  41.2 81.1 %copy-start.1 = (f32[192,768]{1,0:T(8,128)S(1)}, f32[192,768]{1,0:T(8,128)}, u32[]{:S(2)}) copy-start(f32[192,768]{1,0:T(8,128)} %txt_ref.3) | copy-start | bytes 1769476
  43.4 78.9 %collective-permute-start.4 = (bf16[384,768]{1,0:T(8,128)(2,1)}, bf16[384,768]{1,0:T(8,128)(2,1)S(1)}, u32[]{:S(2)}, u32[]{:S(2)}) collective-permute-start(bf16[384,768]{1,0:T(8,128)(2,1)} %get-tuple-element.22), channel_id=1, source_target_pairs={{992,0},{1008,16},{0,32},{16,48},{32,64},{48,80},{64,96},{80,112},... | collective-permute-start | bytes 1769480 | tf_op jit(solution)/shard_map/ppermute | solution.py:19
  45.3 77.0 %collective-permute-start.5 = (bf16[192,768]{1,0:T(8,128)(2,1)}, bf16[192,768]{1,0:T(8,128)(2,1)S(1)}, u32[]{:S(2)}, u32[]{:S(2)}) collective-permute-start(bf16[192,768]{1,0:T(8,128)(2,1)} %get-tuple-element.23), channel_id=1, source_target_pairs={{1008,0},{0,16},{16,32},{32,48},{48,64},{64,80},{80,96},{96,112},{... | collective-permute-start | bytes 884744 | tf_op jit(solution)/shard_map/ppermute | solution.py:19
  47.2 75.1 %collective-permute-start.6 = (bf16[192,768]{1,0:T(8,128)(2,1)}, bf16[192,768]{1,0:T(8,128)(2,1)S(1)}, u32[]{:S(2)}, u32[]{:S(2)}) collective-permute-start(bf16[192,768]{1,0:T(8,128)(2,1)} %get-tuple-element.24), channel_id=1, source_target_pairs={{32,0},{48,16},{64,32},{80,48},{96,64},{112,80},{128,96},{144,112}... | collective-permute-start | bytes 884744 | tf_op jit(solution)/shard_map/ppermute | solution.py:19
  64.5 57.8 %collective-permute-start.7 = (bf16[192,768]{1,0:T(8,128)(2,1)S(1)}, bf16[192,768]{1,0:T(8,128)(2,1)S(1)}, u32[]{:S(2)}, u32[]{:S(2)}) collective-permute-start(bf16[192,768]{1,0:T(8,128)(2,1)S(1)} %get-tuple-element.25), channel_id=1, source_target_pairs={{16,0},{32,16},{48,32},{64,48},{80,64},{96,80},{112,96},{128,112},... | collective-permute-start | bytes 884744 | tf_op jit(solution)/shard_map/ppermute | solution.py:19

commit v3 on v2

--- a/solution.py
+++ b/solution.py
@@ -272,9 +272,9 @@
         VMEM_BYTES,
     )
     pair_ahead = from_ahead(pair, "blk", FAR)
-    txt_after = from_ahead(txt_block, "blk", 1)
+    txt_after = from_ahead(txt_again, "blk", 1)
     img_behind = from_ahead(img_block, "blk", -FAR)
-    txt_before = from_ahead(txt_again, "blk", -1)
+    txt_before = from_ahead(txt_block, "blk", -1)
     blocks = (pair_ahead, txt_after, img_behind, txt_before, txt_block)
     stacks = [
         pltpu.VMEM((4 * rows, width), jnp.bfloat16),

time: 124 us -> 127 us (1.024)
  waiting for transfers between devices: 9.73 us -> 13.8 us
  starting transfers between devices: 47.5 us -> 46.2 us
    ppermute x8, waiting for transfers between devices: 9.73 us -> 13.8 us  [from_ahead(): return lax.ppermute(value, axis, pairs)]
  transfers between devices with their start and end apart: 8 -> 8, of which waited for: 1 -> 2; matrix products, arithmetic and copies ran while one was open for 1% -> 1% of each run, Pallas kernels for 0% -> 0%
where the time goes in v3:
time: 127 us
  blocking collectives  54 us (43%)
  starting transfers between devices  46.2 us (36%)
  waiting for transfers between devices  13.8 us (11%)
  Pallas kernels  8.73 us (7%)
  between operations  2.07 us (2%)
  local copies, waits for them, and re-layouts  1.36 us (1%)
    all_to_all x2, blocking collectives, exchange(): lax.all_to_all(spread, ('blk', 'group'), 0, 0, tiled=True, axis_index_gro...  54 us
    ppermute x8, starting transfers between devices, from_ahead(): return lax.ppermute(value, axis, pairs)  46.2 us
    ppermute x8, waiting for transfers between devices, from_ahead(): return lax.ppermute(value, axis, pairs)  13.8 us
    pallas_call x4, Pallas kernels, call(): pl.pallas_call(kernel, out_shape=outs, in_specs=specs, out_specs=vmem(len...  8.73 us
  transfers between devices with their start and end apart: 8, of which 2 were waited for; matrix products, arithmetic and copies ran while one was open for 1% of the time, Pallas kernels for 0%

profile of v3, /device:TPU:1, one launch (start us, length us, event | category | flops | bytes accessed | tf_op | source)
XLA Modules:
  0.0 126.8 jit_solution(398550078259272540)
XLA Ops:
  0.6 0.0 copy-start.3
  0.6 0.0 copy-start.2
  0.7 0.7 copy-done.3
  1.3 0.0 copy-done.2
  1.3 1.4 %shard_map.85 = (bf16[416,768]{1,0:T(8,128)(2,1)S(1)}, bf16[208,768]{1,0:T(8,128)(2,1)S(1)}, bf16[208,768]{1,0:T(8,128)(2,1)S(1)}, bf16[208,768]{1,0:T(8,128)(2,1)S(1)}) custom-call(f32[192,768]{1,0:T(8,128)} %img_ref.3, f32[192,768]{1,0:T(8,128)} %txt_ref.3, s32[1,192]{1,0:T(1,128)S(1)} %bitcast.10, f32[1,192]{1,0:T(1,128)S(1)} %bitcast.8), custom_call_target="tpu_custom_call" | custom-call | flops 884736 | bytes 2359296 | tf_op jit(solution)/shard_map/pallas_call | solution.py:31
  2.8 16.2 %collective-permute-start = (bf16[416,768]{1,0:T(8,128)(2,1)S(1)}, bf16[416,768]{1,0:T(8,128)(2,1)S(1)}, u32[]{:S(2)}, u32[]{:S(2)}) collective-permute-start(bf16[416,768]{1,0:T(8,128)(2,1)S(1)} %get-tuple-element.17), channel_id=1, source_target_pairs={{32,0},{48,16},{64,32},{80,48},{96,64},{112,80},{128,96},{144,112}... | collective-permute-start | bytes 1916936 | tf_op jit(solution)/shard_map/ppermute | solution.py:19
  18.9 2.9 %collective-permute-start.1 = (bf16[208,768]{1,0:T(8,128)(2,1)S(1)}, bf16[208,768]{1,0:T(8,128)(2,1)S(1)}, u32[]{:S(2)}, u32[]{:S(2)}) collective-permute-start(bf16[208,768]{1,0:T(8,128)(2,1)S(1)} %get-tuple-element.18), channel_id=1, source_target_pairs={{16,0},{32,16},{48,32},{64,48},{80,64},{96,80},{112,96},{128,112},... | collective-permute-start | bytes 958472 | tf_op jit(solution)/shard_map/ppermute | solution.py:19
  21.8 2.6 %collective-permute-start.2 = (bf16[208,768]{1,0:T(8,128)(2,1)S(1)}, bf16[208,768]{1,0:T(8,128)(2,1)S(1)}, u32[]{:S(2)}, u32[]{:S(2)}) collective-permute-start(bf16[208,768]{1,0:T(8,128)(2,1)S(1)} %get-tuple-element.19), channel_id=1, source_target_pairs={{992,0},{1008,16},{0,32},{16,48},{32,64},{48,80},{64,96},{80,112},... | collective-permute-start | bytes 958472 | tf_op jit(solution)/shard_map/ppermute | solution.py:19
  24.4 2.0 %collective-permute-start.3 = (bf16[208,768]{1,0:T(8,128)(2,1)S(1)}, bf16[208,768]{1,0:T(8,128)(2,1)S(1)}, u32[]{:S(2)}, u32[]{:S(2)}) collective-permute-start(bf16[208,768]{1,0:T(8,128)(2,1)S(1)} %get-tuple-element.20.own_ref), channel_id=1, source_target_pairs={{1008,0},{0,16},{16,32},{32,48},{48,64},{64,80},{80,96},{96,112},{... | collective-permute-start | bytes 958472 | tf_op jit(solution)/shard_map/ppermute | solution.py:19
  27.7 4.2 %collective-permute-done.1.after_ref = bf16[208,768]{1,0:T(8,128)(2,1)S(1)} collective-permute-done((bf16[208,768]{1,0:T(8,128)(2,1)S(1)}, bf16[208,768]{1,0:T(8,128)(2,1)S(1)}, u32[]{:S(2)}, u32[]{:S(2)}) %collective-permute-start.1) | collective-permute-done | bytes 319520 | tf_op jit(solution)/shard_map/ppermute | solution.py:19
  32.0 9.6 %collective-permute-done.2.img_ref = bf16[208,768]{1,0:T(8,128)(2,1)S(1)} collective-permute-done((bf16[208,768]{1,0:T(8,128)(2,1)S(1)}, bf16[208,768]{1,0:T(8,128)(2,1)S(1)}, u32[]{:S(2)}, u32[]{:S(2)}) %collective-permute-start.2) | collective-permute-done | bytes 319520 | tf_op jit(solution)/shard_map/ppermute | solution.py:19
  41.6 0.0 collective-permute-done.3.before_ref
  41.6 0.0 collective-permute-done.pair_ref
  41.6 3.6 %shard_map.86 = (f32[8,128]{1,0:T(8,128)S(1)}, bf16[384,768]{1,0:T(8,128)(2,1)S(1)}) custom-call(f32[1]{0:T(128)S(6)} %copy.10.scale_ref, f32[1]{0:T(128)S(6)} %copy.11.shift_ref, f32[1,192]{1,0:T(1,128)S(1)} %bitcast.9, bf16[416,768]{1,0:T(8,128)(2,1)S(1)} %collective-permute-done.pair_ref, bf16[208,768]{1,0:T(8,128)(2,1)S(1)} %collective-permute-done.1.after_ref, ...), custom_call_target="tpu_custom_call" | custom-call | flops 452984832 | bytes 4128768 | tf_op jit(solution)/shard_map/pallas_call | solution.py:31
  45.1 0.0 copy-start
  45.1 0.0 copy-start.1
  45.1 2.2 %shard_map.87 = (bf16[384,768]{1,0:T(8,128)(2,1)}, bf16[192,768]{1,0:T(8,128)(2,1)}, bf16[192,768]{1,0:T(8,128)(2,1)S(1)}, bf16[192,768]{1,0:T(8,128)(2,1)}, f32[192,768]{1,0:T(8,128)S(1)}) custom-call(bf16[384,768]{1,0:T(8,128)(2,1)S(1)} %get-tuple-element.21.factors, bf16[416,768]{1,0:T(8,128)(2,1)S(1)} %collective-permute-done.pair_ref, ...), custom_call_target="tpu_custom_call" | custom-call | flops 905969664 | bytes 4128768 | tf_op jit(solution)/shard_map/pallas_call | solution.py:31
  47.3 1.9 %collective-permute-start.4 = (bf16[384,768]{1,0:T(8,128)(2,1)}, bf16[384,768]{1,0:T(8,128)(2,1)S(1)}, u32[]{:S(2)}, u32[]{:S(2)}) collective-permute-start(bf16[384,768]{1,0:T(8,128)(2,1)} %get-tuple-element.22), channel_id=1, source_target_pairs={{992,0},{1008,16},{0,32},{16,48},{32,64},{48,80},{64,96},{80,112},... | collective-permute-start | bytes 1769480 | tf_op jit(solution)/shard_map/ppermute | solution.py:19
  49.2 1.9 %collective-permute-start.5 = (bf16[192,768]{1,0:T(8,128)(2,1)}, bf16[192,768]{1,0:T(8,128)(2,1)S(1)}, u32[]{:S(2)}, u32[]{:S(2)}) collective-permute-start(bf16[192,768]{1,0:T(8,128)(2,1)} %get-tuple-element.23), channel_id=1, source_target_pairs={{1008,0},{0,16},{16,32},{32,48},{48,64},{64,80},{80,96},{96,112},{... | collective-permute-start | bytes 884744 | tf_op jit(solution)/shard_map/ppermute | solution.py:19
  51.2 16.2 %collective-permute-start.6 = (bf16[192,768]{1,0:T(8,128)(2,1)}, bf16[192,768]{1,0:T(8,128)(2,1)S(1)}, u32[]{:S(2)}, u32[]{:S(2)}) collective-permute-start(bf16[192,768]{1,0:T(8,128)(2,1)} %get-tuple-element.24), channel_id=1, source_target_pairs={{32,0},{48,16},{64,32},{80,48},{96,64},{112,80},{128,96},{144,112}... | collective-permute-start | bytes 884744 | tf_op jit(solution)/shard_map/ppermute | solution.py:19
  67.4 2.6 %collective-permute-start.7 = (bf16[192,768]{1,0:T(8,128)(2,1)S(1)}, bf16[192,768]{1,0:T(8,128)(2,1)S(1)}, u32[]{:S(2)}, u32[]{:S(2)}) collective-permute-start(bf16[192,768]{1,0:T(8,128)(2,1)S(1)} %get-tuple-element.25), channel_id=1, source_target_pairs={{16,0},{32,16},{48,32},{64,48},{80,64},{96,80},{112,96},{128,112},... | collective-permute-start | bytes 884744 | tf_op jit(solution)/shard_map/ppermute | solution.py:19
  70.0 12.6 %all_to_all.10 = f32[32,1,128]{2,1,0:T(1,128)S(1)} all-to-all(f32[32,1,128]{2,1,0:T(1,128)S(1)} %broadcast_in_dim.13), channel_id=1, replica_groups={{0,4,8,12,16,20,24,28,32,36,40,44,48,52,56,60,64,68,72,76,80,84,88,92,9..., dimensions={0} | all-to-all | bytes 32768 | tf_op jit(solution)/shard_map/all_to_all | solution.py:234
  82.6 0.5 reduce_sum.9
  83.1 0.7 broadcast_in_dim.14
  83.8 41.4 %all_to_all.11 = f32[32,1,128]{2,1,0:T(1,128)S(1)} all-to-all(f32[32,1,128]{2,1,0:T(1,128)S(1)} %broadcast_in_dim.14), channel_id=1, replica_groups={{0,1,2,3,128,129,130,131,256,257,258,259,384,385,386,387,512,513,514,51..., dimensions={0} | all-to-all | bytes 32768 | tf_op jit(solution)/shard_map/all_to_all | solution.py:234
  125.2 0.0 collective-permute-done.5.before_ref
  125.2 0.0 collective-permute-done.6.far_ref
  125.2 0.0 collective-permute-done.7.after_ref
  125.2 0.0 collective-permute-done.4.pair_ref
  125.2 0.0 copy-done
  125.2 0.0 copy-done.1
  125.2 1.6 %shard_map.88 = (f32[192,768]{1,0:T(8,128)}, f32[192,768]{1,0:T(8,128)}, f32[1,1]{1,0:T(1,128)}) custom-call(f32[192,768]{1,0:T(8,128)S(1)} %copy-done, f32[192,768]{1,0:T(8,128)S(1)} %copy-done.1, bf16[384,768]{1,0:T(8,128)(2,1)S(1)} %collective-permute-done.4.pair_ref, bf16[192,768]{1,0:T(8,128)(2,1)S(1)} %collective-permute-done.5.before_ref, ...), custom_call_target="tpu_custom_call" | custom-call | flops 2949120 | bytes 4423680 | tf_op jit(solution)/shard_map/pallas_call | solution.py:31
  (2 shorter events, 0.0 us)
Async XLA Ops:
  0.6 0.7 copy-start.3
  0.6 0.7 copy-start.2
  2.8 38.8 %collective-permute-start = (bf16[416,768]{1,0:T(8,128)(2,1)S(1)}, bf16[416,768]{1,0:T(8,128)(2,1)S(1)}, u32[]{:S(2)}, u32[]{:S(2)}) collective-permute-start(bf16[416,768]{1,0:T(8,128)(2,1)S(1)} %get-tuple-element.17), channel_id=1, source_target_pairs={{32,0},{48,16},{64,32},{80,48},{96,64},{112,80},{128,96},{144,112}... | collective-permute-start | bytes 1916936 | tf_op jit(solution)/shard_map/ppermute | solution.py:19
  18.9 13.0 %collective-permute-start.1 = (bf16[208,768]{1,0:T(8,128)(2,1)S(1)}, bf16[208,768]{1,0:T(8,128)(2,1)S(1)}, u32[]{:S(2)}, u32[]{:S(2)}) collective-permute-start(bf16[208,768]{1,0:T(8,128)(2,1)S(1)} %get-tuple-element.18), channel_id=1, source_target_pairs={{16,0},{32,16},{48,32},{64,48},{80,64},{96,80},{112,96},{128,112},... | collective-permute-start | bytes 958472 | tf_op jit(solution)/shard_map/ppermute | solution.py:19
  21.8 19.8 %collective-permute-start.2 = (bf16[208,768]{1,0:T(8,128)(2,1)S(1)}, bf16[208,768]{1,0:T(8,128)(2,1)S(1)}, u32[]{:S(2)}, u32[]{:S(2)}) collective-permute-start(bf16[208,768]{1,0:T(8,128)(2,1)S(1)} %get-tuple-element.19), channel_id=1, source_target_pairs={{992,0},{1008,16},{0,32},{16,48},{32,64},{48,80},{64,96},{80,112},... | collective-permute-start | bytes 958472 | tf_op jit(solution)/shard_map/ppermute | solution.py:19
  24.4 17.2 %collective-permute-start.3 = (bf16[208,768]{1,0:T(8,128)(2,1)S(1)}, bf16[208,768]{1,0:T(8,128)(2,1)S(1)}, u32[]{:S(2)}, u32[]{:S(2)}) collective-permute-start(bf16[208,768]{1,0:T(8,128)(2,1)S(1)} %get-tuple-element.20.own_ref), channel_id=1, source_target_pairs={{1008,0},{0,16},{16,32},{32,48},{48,64},{64,80},{80,96},{96,112},{... | collective-permute-start | bytes 958472 | tf_op jit(solution)/shard_map/ppermute | solution.py:19
  45.1 80.1 %copy-start = (f32[192,768]{1,0:T(8,128)S(1)}, f32[192,768]{1,0:T(8,128)}, u32[]{:S(2)}) copy-start(f32[192,768]{1,0:T(8,128)} %img_ref.3) | copy-start | bytes 1769476
  45.1 80.1 %copy-start.1 = (f32[192,768]{1,0:T(8,128)S(1)}, f32[192,768]{1,0:T(8,128)}, u32[]{:S(2)}) copy-start(f32[192,768]{1,0:T(8,128)} %txt_ref.3) | copy-start | bytes 1769476
  47.3 77.9 %collective-permute-start.4 = (bf16[384,768]{1,0:T(8,128)(2,1)}, bf16[384,768]{1,0:T(8,128)(2,1)S(1)}, u32[]{:S(2)}, u32[]{:S(2)}) collective-permute-start(bf16[384,768]{1,0:T(8,128)(2,1)} %get-tuple-element.22), channel_id=1, source_target_pairs={{992,0},{1008,16},{0,32},{16,48},{32,64},{48,80},{64,96},{80,112},... | collective-permute-start | bytes 1769480 | tf_op jit(solution)/shard_map/ppermute | solution.py:19
  49.2 76.0 %collective-permute-start.5 = (bf16[192,768]{1,0:T(8,128)(2,1)}, bf16[192,768]{1,0:T(8,128)(2,1)S(1)}, u32[]{:S(2)}, u32[]{:S(2)}) collective-permute-start(bf16[192,768]{1,0:T(8,128)(2,1)} %get-tuple-element.23), channel_id=1, source_target_pairs={{1008,0},{0,16},{16,32},{32,48},{48,64},{64,80},{80,96},{96,112},{... | collective-permute-start | bytes 884744 | tf_op jit(solution)/shard_map/ppermute | solution.py:19
  51.2 74.0 %collective-permute-start.6 = (bf16[192,768]{1,0:T(8,128)(2,1)}, bf16[192,768]{1,0:T(8,128)(2,1)S(1)}, u32[]{:S(2)}, u32[]{:S(2)}) collective-permute-start(bf16[192,768]{1,0:T(8,128)(2,1)} %get-tuple-element.24), channel_id=1, source_target_pairs={{32,0},{48,16},{64,32},{80,48},{96,64},{112,80},{128,96},{144,112}... | collective-permute-start | bytes 884744 | tf_op jit(solution)/shard_map/ppermute | solution.py:19
  67.4 57.8 %collective-permute-start.7 = (bf16[192,768]{1,0:T(8,128)(2,1)S(1)}, bf16[192,768]{1,0:T(8,128)(2,1)S(1)}, u32[]{:S(2)}, u32[]{:S(2)}) collective-permute-start(bf16[192,768]{1,0:T(8,128)(2,1)S(1)} %get-tuple-element.25), channel_id=1, source_target_pairs={{16,0},{32,16},{48,32},{64,48},{80,64},{96,80},{112,96},{128,112},... | collective-permute-start | bytes 884744 | tf_op jit(solution)/shard_map/ppermute | solution.py:19

commit v4 on v2

--- a/solution.py
+++ b/solution.py
@@ -313,7 +313,9 @@
         VMEM_BYTES,
     )
     planes, columns = plane_and_column_groups()
+    parts, sums = lax.optimization_barrier((parts, sums))
     gathered = exchange(sums[0:1], planes)
+    parts, gathered = lax.optimization_barrier((parts, gathered))
     pair_part, img_part, before_part, after_part, own_part = parts
     pair_back = from_ahead(pair_part, "blk", -FAR)
     before_back = from_ahead(after_part, "blk", -1)

time: 124 us -> 124 us (level)
  starting transfers between devices: 47.5 us -> 42.8 us
  blocking collectives: 54 us -> 57.8 us
    ppermute x8, starting transfers between devices: 47.5 us -> 42.8 us  [from_ahead(): return lax.ppermute(value, axis, pairs)]
    all_to_all x2, blocking collectives: 54 us -> 57.8 us  [exchange(): lax.all_to_all(spread, ('blk', 'group'), 0, 0, tiled=True, axis_index_gro...]
where the time goes in v4:
time: 124 us; the launch traced here: 123 us
  blocking collectives  57.8 us (47%)
  starting transfers between devices  42.8 us (35%)
  waiting for transfers between devices  9.73 us (8%)
  Pallas kernels  8.72 us (7%)
  between operations  2.05 us (2%)
  local copies, waits for them, and re-layouts  1.37 us (1%)
    all_to_all x2, blocking collectives, exchange(): lax.all_to_all(spread, ('blk', 'group'), 0, 0, tiled=True, axis_index_gro...  57.8 us
    ppermute x8, starting transfers between devices, from_ahead(): return lax.ppermute(value, axis, pairs)  42.8 us
    ppermute x8, waiting for transfers between devices, from_ahead(): return lax.ppermute(value, axis, pairs)  9.73 us
    pallas_call x4, Pallas kernels, call(): pl.pallas_call(kernel, out_shape=outs, in_specs=specs, out_specs=vmem(len...  8.72 us
  transfers between devices with their start and end apart: 8, of which 1 were waited for; matrix products, arithmetic and copies ran while one was open for 1% of the time, Pallas kernels for 0%

profile of v4, /device:TPU:1, one launch (start us, length us, event | category | flops | bytes accessed | tf_op | source)
XLA Modules:
  0.0 123.1 jit_solution(15495471525392997944)
XLA Ops:
  0.6 0.0 copy-start.3
  0.6 0.0 copy-start.2
  0.7 0.7 copy-done.3
  1.3 0.0 copy-done.2
  1.3 1.4 %shard_map.85 = (bf16[416,768]{1,0:T(8,128)(2,1)S(1)}, bf16[208,768]{1,0:T(8,128)(2,1)S(1)}, bf16[208,768]{1,0:T(8,128)(2,1)S(1)}, bf16[208,768]{1,0:T(8,128)(2,1)S(1)}) custom-call(f32[192,768]{1,0:T(8,128)} %img_ref.3, f32[192,768]{1,0:T(8,128)} %txt_ref.3, s32[1,192]{1,0:T(1,128)S(1)} %bitcast.10, f32[1,192]{1,0:T(1,128)S(1)} %bitcast.8), custom_call_target="tpu_custom_call" | custom-call | flops 884736 | bytes 2359296 | tf_op jit(solution)/shard_map/pallas_call | solution.py:31
  2.8 16.2 %collective-permute-start = (bf16[416,768]{1,0:T(8,128)(2,1)S(1)}, bf16[416,768]{1,0:T(8,128)(2,1)S(1)}, u32[]{:S(2)}, u32[]{:S(2)}) collective-permute-start(bf16[416,768]{1,0:T(8,128)(2,1)S(1)} %get-tuple-element.29), channel_id=1, source_target_pairs={{32,0},{48,16},{64,32},{80,48},{96,64},{112,80},{128,96},{144,112}... | collective-permute-start | bytes 1916936 | tf_op jit(solution)/shard_map/ppermute | solution.py:19
  18.9 1.9 %collective-permute-start.2 = (bf16[208,768]{1,0:T(8,128)(2,1)S(1)}, bf16[208,768]{1,0:T(8,128)(2,1)S(1)}, u32[]{:S(2)}, u32[]{:S(2)}) collective-permute-start(bf16[208,768]{1,0:T(8,128)(2,1)S(1)} %get-tuple-element.31), channel_id=1, source_target_pairs={{992,0},{1008,16},{0,32},{16,48},{32,64},{48,80},{64,96},{80,112},... | collective-permute-start | bytes 958472 | tf_op jit(solution)/shard_map/ppermute | solution.py:19
  20.9 3.4 %collective-permute-start.3 = (bf16[208,768]{1,0:T(8,128)(2,1)S(1)}, bf16[208,768]{1,0:T(8,128)(2,1)S(1)}, u32[]{:S(2)}, u32[]{:S(2)}) collective-permute-start(bf16[208,768]{1,0:T(8,128)(2,1)S(1)} %get-tuple-element.32), channel_id=1, source_target_pairs={{1008,0},{0,16},{16,32},{32,48},{48,64},{64,80},{80,96},{96,112},{... | collective-permute-start | bytes 958472 | tf_op jit(solution)/shard_map/ppermute | solution.py:19
  24.3 2.3 %collective-permute-start.1 = (bf16[208,768]{1,0:T(8,128)(2,1)S(1)}, bf16[208,768]{1,0:T(8,128)(2,1)S(1)}, u32[]{:S(2)}, u32[]{:S(2)}) collective-permute-start(bf16[208,768]{1,0:T(8,128)(2,1)S(1)} %get-tuple-element.30.own_ref), channel_id=1, source_target_pairs={{16,0},{32,16},{48,32},{64,48},{80,64},{96,80},{112,96},{128,112},... | collective-permute-start | bytes 958472 | tf_op jit(solution)/shard_map/ppermute | solution.py:19
  27.9 9.7 %collective-permute-done.2.img_ref = bf16[208,768]{1,0:T(8,128)(2,1)S(1)} collective-permute-done((bf16[208,768]{1,0:T(8,128)(2,1)S(1)}, bf16[208,768]{1,0:T(8,128)(2,1)S(1)}, u32[]{:S(2)}, u32[]{:S(2)}) %collective-permute-start.2) | collective-permute-done | bytes 319520 | tf_op jit(solution)/shard_map/ppermute | solution.py:19
  37.6 0.0 collective-permute-done.3.before_ref
  37.6 0.0 collective-permute-done.1.after_ref
  37.6 0.0 collective-permute-done.pair_ref
  37.6 3.6 %shard_map.86 = (f32[8,128]{1,0:T(8,128)S(1)}, bf16[384,768]{1,0:T(8,128)(2,1)S(1)}) custom-call(f32[1]{0:T(128)S(6)} %copy.9.scale_ref, f32[1]{0:T(128)S(6)} %copy.10.shift_ref, f32[1,192]{1,0:T(1,128)S(1)} %bitcast.9, bf16[416,768]{1,0:T(8,128)(2,1)S(1)} %collective-permute-done.pair_ref, bf16[208,768]{1,0:T(8,128)(2,1)S(1)} %collective-permute-done.1.after_ref, ...), custom_call_target="tpu_custom_call" | custom-call | flops 452984832 | bytes 4128768 | tf_op jit(solution)/shard_map/pallas_call | solution.py:31
  41.2 0.0 copy-start
  41.2 0.0 copy-start.1
  41.2 2.2 %shard_map.87 = (bf16[384,768]{1,0:T(8,128)(2,1)}, bf16[192,768]{1,0:T(8,128)(2,1)}, bf16[192,768]{1,0:T(8,128)(2,1)S(1)}, bf16[192,768]{1,0:T(8,128)(2,1)}, f32[192,768]{1,0:T(8,128)S(1)}) custom-call(bf16[384,768]{1,0:T(8,128)(2,1)S(1)} %get-tuple-element.33.factors, bf16[416,768]{1,0:T(8,128)(2,1)S(1)} %collective-permute-done.pair_ref, ...), custom_call_target="tpu_custom_call" | custom-call | flops 905969664 | bytes 4128768 | tf_op jit(solution)/shard_map/pallas_call | solution.py:31
  43.4 16.5 %all_to_all.10 = f32[32,1,128]{2,1,0:T(1,128)S(1)} all-to-all(f32[32,1,128]{2,1,0:T(1,128)S(1)} %broadcast_in_dim.13), channel_id=1, replica_groups={{0,4,8,12,16,20,24,28,32,36,40,44,48,52,56,60,64,68,72,76,80,84,88,92,9..., dimensions={0} | all-to-all | bytes 32768 | tf_op jit(solution)/shard_map/all_to_all | solution.py:234
  59.9 2.2 %collective-permute-start.4 = (bf16[384,768]{1,0:T(8,128)(2,1)}, bf16[384,768]{1,0:T(8,128)(2,1)S(1)}, u32[]{:S(2)}, u32[]{:S(2)}) collective-permute-start(bf16[384,768]{1,0:T(8,128)(2,1)} %get-tuple-element.46), channel_id=1, source_target_pairs={{992,0},{1008,16},{0,32},{16,48},{32,64},{48,80},{64,96},{80,112},... | collective-permute-start | bytes 1769480 | tf_op jit(solution)/shard_map/ppermute | solution.py:19
  62.1 3.0 %collective-permute-start.5 = (bf16[192,768]{1,0:T(8,128)(2,1)}, bf16[192,768]{1,0:T(8,128)(2,1)S(1)}, u32[]{:S(2)}, u32[]{:S(2)}) collective-permute-start(bf16[192,768]{1,0:T(8,128)(2,1)} %get-tuple-element.47), channel_id=1, source_target_pairs={{1008,0},{0,16},{16,32},{32,48},{48,64},{64,80},{80,96},{96,112},{... | collective-permute-start | bytes 884744 | tf_op jit(solution)/shard_map/ppermute | solution.py:19
  65.1 11.8 %collective-permute-start.6 = (bf16[192,768]{1,0:T(8,128)(2,1)}, bf16[192,768]{1,0:T(8,128)(2,1)S(1)}, u32[]{:S(2)}, u32[]{:S(2)}) collective-permute-start(bf16[192,768]{1,0:T(8,128)(2,1)} %get-tuple-element.48), channel_id=1, source_target_pairs={{32,0},{48,16},{64,32},{80,48},{96,64},{112,80},{128,96},{144,112}... | collective-permute-start | bytes 884744 | tf_op jit(solution)/shard_map/ppermute | solution.py:19
  76.9 2.0 %collective-permute-start.7 = (bf16[192,768]{1,0:T(8,128)(2,1)S(1)}, bf16[192,768]{1,0:T(8,128)(2,1)S(1)}, u32[]{:S(2)}, u32[]{:S(2)}) collective-permute-start(bf16[192,768]{1,0:T(8,128)(2,1)S(1)} %get-tuple-element.49), channel_id=1, source_target_pairs={{16,0},{32,16},{48,32},{64,48},{80,64},{96,80},{112,96},{128,112},... | collective-permute-start | bytes 884744 | tf_op jit(solution)/shard_map/ppermute | solution.py:19
  78.9 0.5 reduce_sum.9
  79.4 0.7 broadcast_in_dim.14
  80.1 41.4 %all_to_all.11 = f32[32,1,128]{2,1,0:T(1,128)S(1)} all-to-all(f32[32,1,128]{2,1,0:T(1,128)S(1)} %broadcast_in_dim.14), channel_id=1, replica_groups={{0,1,2,3,128,129,130,131,256,257,258,259,384,385,386,387,512,513,514,51..., dimensions={0} | all-to-all | bytes 32768 | tf_op jit(solution)/shard_map/all_to_all | solution.py:234
  121.5 0.0 collective-permute-done.5.before_ref
  121.5 0.0 collective-permute-done.6.far_ref
  121.5 0.0 collective-permute-done.7.after_ref
  121.5 0.0 collective-permute-done.4.pair_ref
  121.5 0.0 copy-done
  121.5 0.0 copy-done.1
  121.5 1.6 %shard_map.88 = (f32[192,768]{1,0:T(8,128)}, f32[192,768]{1,0:T(8,128)}, f32[1,1]{1,0:T(1,128)}) custom-call(f32[192,768]{1,0:T(8,128)S(1)} %copy-done, f32[192,768]{1,0:T(8,128)S(1)} %copy-done.1, bf16[384,768]{1,0:T(8,128)(2,1)S(1)} %collective-permute-done.4.pair_ref, bf16[192,768]{1,0:T(8,128)(2,1)S(1)} %collective-permute-done.5.before_ref, ...), custom_call_target="tpu_custom_call" | custom-call | flops 2949120 | bytes 4423680 | tf_op jit(solution)/shard_map/pallas_call | solution.py:31
  (2 shorter events, 0.0 us)
Async XLA Ops:
  0.6 0.7 copy-start.3
  0.6 0.7 copy-start.2
  2.8 34.9 %collective-permute-start = (bf16[416,768]{1,0:T(8,128)(2,1)S(1)}, bf16[416,768]{1,0:T(8,128)(2,1)S(1)}, u32[]{:S(2)}, u32[]{:S(2)}) collective-permute-start(bf16[416,768]{1,0:T(8,128)(2,1)S(1)} %get-tuple-element.29), channel_id=1, source_target_pairs={{32,0},{48,16},{64,32},{80,48},{96,64},{112,80},{128,96},{144,112}... | collective-permute-start | bytes 1916936 | tf_op jit(solution)/shard_map/ppermute | solution.py:19
  18.9 18.7 %collective-permute-start.2 = (bf16[208,768]{1,0:T(8,128)(2,1)S(1)}, bf16[208,768]{1,0:T(8,128)(2,1)S(1)}, u32[]{:S(2)}, u32[]{:S(2)}) collective-permute-start(bf16[208,768]{1,0:T(8,128)(2,1)S(1)} %get-tuple-element.31), channel_id=1, source_target_pairs={{992,0},{1008,16},{0,32},{16,48},{32,64},{48,80},{64,96},{80,112},... | collective-permute-start | bytes 958472 | tf_op jit(solution)/shard_map/ppermute | solution.py:19
  20.9 16.8 %collective-permute-start.3 = (bf16[208,768]{1,0:T(8,128)(2,1)S(1)}, bf16[208,768]{1,0:T(8,128)(2,1)S(1)}, u32[]{:S(2)}, u32[]{:S(2)}) collective-permute-start(bf16[208,768]{1,0:T(8,128)(2,1)S(1)} %get-tuple-element.32), channel_id=1, source_target_pairs={{1008,0},{0,16},{16,32},{32,48},{48,64},{64,80},{80,96},{96,112},{... | collective-permute-start | bytes 958472 | tf_op jit(solution)/shard_map/ppermute | solution.py:19
  24.3 13.3 %collective-permute-start.1 = (bf16[208,768]{1,0:T(8,128)(2,1)S(1)}, bf16[208,768]{1,0:T(8,128)(2,1)S(1)}, u32[]{:S(2)}, u32[]{:S(2)}) collective-permute-start(bf16[208,768]{1,0:T(8,128)(2,1)S(1)} %get-tuple-element.30.own_ref), channel_id=1, source_target_pairs={{16,0},{32,16},{48,32},{64,48},{80,64},{96,80},{112,96},{128,112},... | collective-permute-start | bytes 958472 | tf_op jit(solution)/shard_map/ppermute | solution.py:19
  41.2 80.3 %copy-start = (f32[192,768]{1,0:T(8,128)S(1)}, f32[192,768]{1,0:T(8,128)}, u32[]{:S(2)}) copy-start(f32[192,768]{1,0:T(8,128)} %img_ref.3) | copy-start | bytes 1769476
  41.2 80.3 %copy-start.1 = (f32[192,768]{1,0:T(8,128)S(1)}, f32[192,768]{1,0:T(8,128)}, u32[]{:S(2)}) copy-start(f32[192,768]{1,0:T(8,128)} %txt_ref.3) | copy-start | bytes 1769476
  59.9 61.6 %collective-permute-start.4 = (bf16[384,768]{1,0:T(8,128)(2,1)}, bf16[384,768]{1,0:T(8,128)(2,1)S(1)}, u32[]{:S(2)}, u32[]{:S(2)}) collective-permute-start(bf16[384,768]{1,0:T(8,128)(2,1)} %get-tuple-element.46), channel_id=1, source_target_pairs={{992,0},{1008,16},{0,32},{16,48},{32,64},{48,80},{64,96},{80,112},... | collective-permute-start | bytes 1769480 | tf_op jit(solution)/shard_map/ppermute | solution.py:19
  62.1 59.4 %collective-permute-start.5 = (bf16[192,768]{1,0:T(8,128)(2,1)}, bf16[192,768]{1,0:T(8,128)(2,1)S(1)}, u32[]{:S(2)}, u32[]{:S(2)}) collective-permute-start(bf16[192,768]{1,0:T(8,128)(2,1)} %get-tuple-element.47), channel_id=1, source_target_pairs={{1008,0},{0,16},{16,32},{32,48},{48,64},{64,80},{80,96},{96,112},{... | collective-permute-start | bytes 884744 | tf_op jit(solution)/shard_map/ppermute | solution.py:19
  65.1 56.4 %collective-permute-start.6 = (bf16[192,768]{1,0:T(8,128)(2,1)}, bf16[192,768]{1,0:T(8,128)(2,1)S(1)}, u32[]{:S(2)}, u32[]{:S(2)}) collective-permute-start(bf16[192,768]{1,0:T(8,128)(2,1)} %get-tuple-element.48), channel_id=1, source_target_pairs={{32,0},{48,16},{64,32},{80,48},{96,64},{112,80},{128,96},{144,112}... | collective-permute-start | bytes 884744 | tf_op jit(solution)/shard_map/ppermute | solution.py:19
  76.9 44.6 %collective-permute-start.7 = (bf16[192,768]{1,0:T(8,128)(2,1)S(1)}, bf16[192,768]{1,0:T(8,128)(2,1)S(1)}, u32[]{:S(2)}, u32[]{:S(2)}) collective-permute-start(bf16[192,768]{1,0:T(8,128)(2,1)S(1)} %get-tuple-element.49), channel_id=1, source_target_pairs={{16,0},{32,16},{48,32},{64,48},{80,64},{96,80},{112,96},{128,112},... | collective-permute-start | bytes 884744 | tf_op jit(solution)/shard_map/ppermute | solution.py:19

commit v5 on v3

--- a/solution.py
+++ b/solution.py
@@ -7,16 +7,35 @@
 
 EXTRA = 16
 CHUNK = 32
-FAR = 2
 VMEM_BYTES = 16 * 1024 * 1024
 PLANE = 8
 Z_HI = 4
 
 
-def from_ahead(value, axis, steps):
-    count = lax.axis_size(axis)
-    pairs = [((target + steps) % count, target) for target in range(count)]
-    return lax.ppermute(value, axis, pairs)
+def exchange_pairs(value, distance, keep):
+    count = lax.axis_size("blk")
+    pairs = []
+    for first in range(count):
+        if keep(first):
+            second = (first + distance) % count
+            pairs += [(first, second), (second, first)]
+    return lax.ppermute(value, "blk", sorted(pairs))
+
+
+def with_chip_inside(value):
+    return exchange_pairs(value, 2, lambda first: first % 4 < 2)
+
+
+def with_chip_across(value):
+    return exchange_pairs(value, 2, lambda first: first % 4 >= 2)
+
+
+def with_next_core(value):
+    return exchange_pairs(value, 1, lambda first: first % 2 == 1)
+
+
+def with_other_core(value):
+    return exchange_pairs(value, 1, lambda first: first % 2 == 0)
 
 
 def row_norms(values):
@@ -42,7 +61,7 @@
 
 
 def prepare_kernel(
-    img_ref, txt_ref, key_ref, weight_ref, pair_ref, txt_out, img_out, again_out, img_buf, txt_buf, sems
+    img_ref, txt_ref, key_ref, weight_ref, pair_ref, txt_out, img_buf, txt_buf, sems
 ):
     rows, width = img_buf.shape
     block = rows + EXTRA
@@ -80,8 +99,8 @@
         preferred_element_type=jnp.float32,
     ).astype(jnp.bfloat16)
     for start, source, alone, copy in (
-        (0, img_buf, (img_out,), copies[0]),
-        (block, txt_buf, (txt_out, again_out), copies[1]),
+        (0, img_buf, (), copies[0]),
+        (block, txt_buf, (txt_out,), copies[1]),
     ):
         copy.wait()
         values = source[...]
@@ -91,24 +110,32 @@
             target[rows:block, :] = extra
 
 
-def stack_blocks(rows, pair_ref, after_ref, img_ref, before_ref, own_ref, txts, imgs):
+def stack_blocks(rows, odd_ref, inside_ref, across_ref, next_ref, other_ref, own_ref, txts, imgs):
     block = rows + EXTRA
-    imgs[0:rows, :] = pair_ref[0:rows, :]
-    imgs[rows : 2 * rows, :] = img_ref[0:rows, :]
-    txts[0:rows, :] = before_ref[0:rows, :]
+    imgs[0:rows, :] = inside_ref[0:rows, :]
+    imgs[rows : 2 * rows, :] = across_ref[0:rows, :]
+    txts[0:rows, :] = next_ref[0:rows, :]
     txts[rows : 2 * rows, :] = own_ref[0:rows, :]
-    txts[2 * rows : 3 * rows, :] = after_ref[0:rows, :]
-    txts[3 * rows : 4 * rows, :] = pair_ref[block : block + rows, :]
+    txts[2 * rows : 3 * rows, :] = other_ref[0:rows, :]
+
+    @pl.when(odd_ref[0] == 0)
+    def _():
+        txts[3 * rows : 4 * rows, :] = inside_ref[block : block + rows, :]
+
+    @pl.when(odd_ref[0] == 1)
+    def _():
+        txts[3 * rows : 4 * rows, :] = across_ref[block : block + rows, :]
 
 
 def score_kernel(
     scale_ref,
     shift_ref,
+    odd_ref,
     weight_ref,
-    pair_ref,
-    after_ref,
-    img_ref,
-    before_ref,
+    inside_ref,
+    across_ref,
+    next_ref,
+    other_ref,
     own_ref,
     sums_ref,
     factors,
@@ -122,14 +149,19 @@
     scale = scale_ref[0]
     shift = shift_ref[0]
 
-    stack_blocks(rows, pair_ref, after_ref, img_ref, before_ref, own_ref, txts, imgs)
+    stack_blocks(rows, odd_ref, inside_ref, across_ref, next_ref, other_ref, own_ref, txts, imgs)
 
     lane = lax.broadcasted_iota(jnp.int32, (1, 4 * rows), 1)
     txt_keys = jnp.zeros((1, 4 * rows), jnp.float32)
-    for slot, (source, start) in enumerate(
-        ((before_ref, rows), (own_ref, rows), (after_ref, rows), (pair_ref, block + rows))
-    ):
-        extra = source[start : start + EXTRA, :].astype(jnp.float32)
+    ahead = jnp.where(
+        odd_ref[0] == 0,
+        inside_ref[block + rows : 2 * block, :].astype(jnp.float32),
+        across_ref[block + rows : 2 * block, :].astype(jnp.float32),
+    )
+    extras = [
+        source[rows:block, :].astype(jnp.float32) for source in (next_ref, own_ref, other_ref)
+    ]
+    for slot, extra in enumerate((*extras, ahead)):
         keys = extra[0:1] * 256.0 + extra[1:2]
         txt_keys = jnp.where(lane >= slot * rows, keys, txt_keys)
 
@@ -137,7 +169,7 @@
         jnp.int32, (rows, 256), 1
     )
     one = jnp.where(one, 1.0, 0.0).astype(jnp.bfloat16)
-    for slot, source in enumerate((pair_ref, img_ref)):
+    for slot, source in enumerate((inside_ref, across_ref)):
         columns[slot * rows : (slot + 1) * rows, :] = lax.dot_general(
             one,
             source[rows : rows + EXTRA, 0:256],
@@ -177,37 +209,41 @@
 
 
 def grad_kernel(
+    odd_ref,
     factors,
-    pair_ref,
-    after_ref,
-    img_ref,
-    before_ref,
+    inside_ref,
+    across_ref,
+    next_ref,
+    other_ref,
     own_ref,
-    pair_out,
-    img_out,
-    before_out,
-    after_out,
+    inside_out,
+    across_out,
+    next_out,
+    other_out,
     own_out,
     txts,
     imgs,
 ):
     rows = own_out.shape[0]
-    stack_blocks(rows, pair_ref, after_ref, img_ref, before_ref, own_ref, txts, imgs)
+    stack_blocks(rows, odd_ref, inside_ref, across_ref, next_ref, other_ref, own_ref, txts, imgs)
     img_grads = jnp.dot(factors[...], txts[...], preferred_element_type=jnp.float32)
     img_grads = img_grads.astype(jnp.bfloat16)
-    pair_out[0:rows, :] = img_grads[0:rows]
-    img_out[...] = img_grads[rows : 2 * rows]
+    inside_out[0:rows, :] = img_grads[0:rows]
+    across_out[0:rows, :] = img_grads[rows : 2 * rows]
     txt_grads = lax.dot_general(
         factors[...], imgs[...], (((0,), (0,)), ((), ())), preferred_element_type=jnp.float32
     )
-    before_out[...] = txt_grads[0:rows].astype(jnp.bfloat16)
+    next_out[...] = txt_grads[0:rows].astype(jnp.bfloat16)
     own_out[...] = txt_grads[rows : 2 * rows]
-    after_out[...] = txt_grads[2 * rows : 3 * rows].astype(jnp.bfloat16)
-    pair_out[rows : 2 * rows, :] = txt_grads[3 * rows : 4 * rows].astype(jnp.bfloat16)
+    other_out[...] = txt_grads[2 * rows : 3 * rows].astype(jnp.bfloat16)
+    odd = odd_ref[0].astype(jnp.float32)
+    ahead = txt_grads[3 * rows : 4 * rows]
+    inside_out[rows : 2 * rows, :] = (ahead * (1.0 - odd)).astype(jnp.bfloat16)
+    across_out[rows : 2 * rows, :] = (ahead * odd).astype(jnp.bfloat16)
 
 
 def finish_kernel(
-    img_ref, txt_ref, pair_ref, before_ref, far_ref, after_ref, own_ref, sums_ref,
+    img_ref, txt_ref, across_ref, inside_ref, next_ref, other_ref, own_ref, sums_ref,
     img_out, txt_out, loss_out
 ):
     rows = img_ref.shape[0]
@@ -218,11 +254,12 @@
         return (grad - unit * jnp.sum(unit * grad, -1, keepdims=True)) / norm
 
     wide = lambda part: part.astype(jnp.float32)
-    img_out[...] = finish(img_ref[...], wide(pair_ref[0:rows, :]) + wide(far_ref[...]))
+    img_out[...] = finish(img_ref[...], wide(inside_ref[0:rows, :]) + wide(across_ref[0:rows, :]))
     txt_out[...] = finish(
         txt_ref[...],
-        (own_ref[...] + wide(before_ref[...]))
-        + (wide(after_ref[...]) + wide(pair_ref[rows : 2 * rows, :])),
+        (own_ref[...] + wide(next_ref[...]))
+        + (wide(other_ref[...]) + wide(inside_ref[rows : 2 * rows, :]))
+        + wide(across_ref[rows : 2 * rows, :]),
     )
     sums = jnp.sum(sums_ref[...], 0, keepdims=True)
     loss_out[...] = sums[:, 0:1] / sums[:, 1:2]
@@ -252,13 +289,13 @@
     block = rows + EXTRA
     half = lambda *shape: jax.ShapeDtypeStruct(shape, jnp.bfloat16)
     full = lambda *shape: jax.ShapeDtypeStruct(shape, jnp.float32)
-    smem = [pl.BlockSpec(memory_space=pltpu.SMEM)] * 2
+    smem = [pl.BlockSpec(memory_space=pltpu.SMEM)]
     hbm = [pl.BlockSpec(memory_space=pltpu.HBM)] * 2
     row_weights = weights.reshape(1, rows)
     fixed = [pltpu.with_memory_space_constraint(x, pltpu.HBM) for x in (image_emb, text_emb)]
-    pair, txt_block, img_block, txt_again = call(
+    pair, txt_block = call(
         prepare_kernel,
-        [half(2 * block, width)] + [half(block, width)] * 3,
+        [half(2 * block, width), half(block, width)],
         (*fixed, keys.reshape(1, rows), row_weights),
         hbm + vmem(2),
         [
@@ -271,11 +308,12 @@
         16 * rows * width,
         VMEM_BYTES,
     )
-    pair_ahead = from_ahead(pair, "blk", FAR)
-    txt_after = from_ahead(txt_again, "blk", 1)
-    img_behind = from_ahead(img_block, "blk", -FAR)
-    txt_before = from_ahead(txt_block, "blk", -1)
-    blocks = (pair_ahead, txt_after, img_behind, txt_before, txt_block)
+    odd = ((lax.axis_index("blk") >> 1) & 1).astype(jnp.int32).reshape(1)
+    across = with_chip_across(pair)
+    inside = with_chip_inside(pair)
+    next_core = with_next_core(txt_block)
+    other_core = with_other_core(txt_block)
+    blocks = (inside, across, next_core, other_core, txt_block)
     stacks = [
         pltpu.VMEM((4 * rows, width), jnp.bfloat16),
         pltpu.VMEM((2 * rows, width), jnp.bfloat16),
@@ -283,8 +321,8 @@
     sums, factors = call(
         score_kernel,
         [full(8, 128), half(2 * rows, 4 * rows)],
-        (scale, shift, row_weights, *blocks),
-        smem + vmem(6),
+        (scale, shift, odd, row_weights, *blocks),
+        smem * 3 + vmem(6),
         stacks
         + [
             pltpu.VMEM((2 * rows, 4 * rows), jnp.float32),
@@ -299,13 +337,13 @@
         grad_kernel,
         [
             half(2 * rows, width),
-            half(rows, width),
+            half(2 * rows, width),
             half(rows, width),
             half(rows, width),
             full(rows, width),
         ],
-        (factors, *blocks),
-        vmem(6),
+        (odd, factors, *blocks),
+        smem + vmem(6),
         stacks,
         32 * rows * rows * width,
         0,
@@ -314,11 +352,11 @@
     )
     planes, columns = plane_and_column_groups()
     gathered = exchange(sums[0:1], planes)
-    pair_part, img_part, before_part, after_part, own_part = parts
-    pair_back = from_ahead(pair_part, "blk", -FAR)
-    before_back = from_ahead(after_part, "blk", -1)
-    far_back = from_ahead(img_part, "blk", FAR)
-    after_back = from_ahead(before_part, "blk", 1)
+    inside_part, across_part, next_part, other_part, own_part = parts
+    across_back = with_chip_across(across_part)
+    inside_back = with_chip_inside(inside_part)
+    next_back = with_next_core(next_part)
+    other_back = with_other_core(other_part)
     gathered = exchange(jnp.sum(gathered, 0, keepdims=True), columns)
     image_grad, text_grad, loss = call(
         finish_kernel,
@@ -326,10 +364,10 @@
         (
             image_emb,
             text_emb,
-            pair_back,
-            before_back,
-            far_back,
-            after_back,
+            across_back,
+            inside_back,
+            next_back,
+            other_back,
             own_part,
             gathered,
         ),

time: 127 us -> 123 us (0.969)
  starting transfers between devices: 46.2 us -> 42.7 us
  waiting for transfers between devices: 13.8 us -> 12.1 us
  Pallas kernels: 8.73 us -> 10.2 us
  local copies, waits for them, and re-layouts: 1.36 us -> 2.67 us
  blocking collectives: 54 us -> 52.7 us
    ppermute x8, starting transfers between devices: 46.2 us -> 42.7 us  [exchange_pairs(): return lax.ppermute(value, 'blk', sorted(pairs))]
    unnamed x8 -> x16, local copies, waits for them, and re-layouts: 0.69 us -> 2.64 us
    ppermute x8, waiting for transfers between devices: 13.8 us -> 12.1 us  [exchange_pairs(): return lax.ppermute(value, 'blk', sorted(pairs))]
    pallas_call x4, Pallas kernels: 8.73 us -> 10.2 us  [call(): pl.pallas_call(kernel, out_shape=outs, in_specs=specs, out_specs=vmem(len...]
    all_to_all x2, blocking collectives: 54 us -> 52.7 us  [exchange(): lax.all_to_all(spread, ('blk', 'group'), 0, 0, tiled=True, axis_index_gro...]
  transfers between devices with their start and end apart: 8 -> 8, of which waited for: 2 -> 1; matrix products, arithmetic and copies ran while one was open for 1% -> 0% of each run, Pallas kernels for 0% -> 0%
where the time goes in v5:
time: 123 us; the launch traced here: 122 us
  blocking collectives  52.7 us (43%)
  starting transfers between devices  42.7 us (35%)
  waiting for transfers between devices  12.1 us (10%)
  Pallas kernels  10.2 us (8%)
  local copies, waits for them, and re-layouts  2.67 us (2%)
  between operations  2.09 us (2%)
    all_to_all x2, blocking collectives, exchange(): lax.all_to_all(spread, ('blk', 'group'), 0, 0, tiled=True, axis_index_gro...  52.7 us
    ppermute x8, starting transfers between devices, exchange_pairs(): return lax.ppermute(value, 'blk', sorted(pairs))  42.7 us
    ppermute x8, waiting for transfers between devices, exchange_pairs(): return lax.ppermute(value, 'blk', sorted(pairs))  12.1 us
    pallas_call x4, Pallas kernels, call(): pl.pallas_call(kernel, out_shape=outs, in_specs=specs, out_specs=vmem(len...  10.2 us
    unnamed x16, local copies, waits for them, and re-layouts  2.64 us
  transfers between devices with their start and end apart: 8, of which 1 were waited for; matrix products, arithmetic and copies ran while one was open for 0% of the time, Pallas kernels for 0%

profile of v5, /device:TPU:1, one launch (start us, length us, event | category | flops | bytes accessed | tf_op | source)
XLA Modules:
  0.0 122.4 jit_solution(909084334306623633)
XLA Ops:
  0.6 0.0 copy-start.7
  0.6 0.0 copy-start.6
  0.7 0.7 copy-done.7
  1.3 0.0 copy-done.6
  1.3 1.4 %shard_map.85 = (bf16[416,768]{1,0:T(8,128)(2,1)S(1)}, bf16[208,768]{1,0:T(8,128)(2,1)S(1)}) custom-call(f32[192,768]{1,0:T(8,128)} %img_ref.3, f32[192,768]{1,0:T(8,128)} %txt_ref.3, s32[1,192]{1,0:T(1,128)S(1)} %bitcast.11, f32[1,192]{1,0:T(1,128)S(1)} %bitcast.9), custom_call_target="tpu_custom_call" | custom-call | flops 884736 | bytes 2359296 | tf_op jit(solution)/shard_map/pallas_call | solution.py:50
  2.8 16.2 %collective-permute-start.1 = (bf16[416,768]{1,0:T(8,128)(2,1)S(1)}, bf16[416,768]{1,0:T(8,128)(2,1)S(1)}, u32[]{:S(2)}, u32[]{:S(2)}) collective-permute-start(bf16[416,768]{1,0:T(8,128)(2,1)S(1)} %get-tuple-element.15), channel_id=1, source_target_pairs={{0,992},{16,1008},{32,64},{48,80},{64,32},{80,48},{96,128},{112,14... | collective-permute-start | bytes 1916936 | tf_op jit(solution)/shard_map/ppermute | solution.py:22
  18.9 1.9 %collective-permute-start = (bf16[416,768]{1,0:T(8,128)(2,1)S(1)}, bf16[416,768]{1,0:T(8,128)(2,1)S(1)}, u32[]{:S(2)}, u32[]{:S(2)}) collective-permute-start(bf16[416,768]{1,0:T(8,128)(2,1)S(1)} %get-tuple-element.15), channel_id=1, source_target_pairs={{0,32},{16,48},{32,0},{48,16},{64,96},{80,112},{96,64},{112,80},{1... | collective-permute-start | bytes 1916936 | tf_op jit(solution)/shard_map/ppermute | solution.py:22
  20.9 2.9 %collective-permute-start.3 = (bf16[208,768]{1,0:T(8,128)(2,1)S(1)}, bf16[208,768]{1,0:T(8,128)(2,1)S(1)}, u32[]{:S(2)}, u32[]{:S(2)}) collective-permute-start(bf16[208,768]{1,0:T(8,128)(2,1)S(1)} %get-tuple-element.16.own_ref), channel_id=1, source_target_pairs={{0,16},{16,0},{32,48},{48,32},{64,80},{80,64},{96,112},{112,96},{1... | collective-permute-start | bytes 958472 | tf_op jit(solution)/shard_map/ppermute | solution.py:22
  23.7 3.5 %collective-permute-start.2 = (bf16[208,768]{1,0:T(8,128)(2,1)S(1)}, bf16[208,768]{1,0:T(8,128)(2,1)S(1)}, u32[]{:S(2)}, u32[]{:S(2)}) collective-permute-start(bf16[208,768]{1,0:T(8,128)(2,1)S(1)} %get-tuple-element.16.own_ref), channel_id=1, source_target_pairs={{0,1008},{16,32},{32,16},{48,64},{64,48},{80,96},{96,80},{112,128}... | collective-permute-start | bytes 958472 | tf_op jit(solution)/shard_map/ppermute | solution.py:22
  28.6 0.0 collective-permute-done.3.other_ref
  28.6 0.0 copy-start.2
  28.6 12.1 %collective-permute-done.2.next_ref = bf16[208,768]{1,0:T(8,128)(2,1)S(1)} collective-permute-done((bf16[208,768]{1,0:T(8,128)(2,1)S(1)}, bf16[208,768]{1,0:T(8,128)(2,1)S(1)}, u32[]{:S(2)}, u32[]{:S(2)}) %collective-permute-start.2) | collective-permute-done | bytes 319520 | tf_op jit(solution)/shard_map/ppermute | solution.py:22
  40.6 0.0 copy-start.4
  40.6 0.0 collective-permute-done.1.across_ref
  40.7 0.0 collective-permute-done.inside_ref
  40.7 3.7 %shard_map.86 = (f32[8,128]{1,0:T(8,128)S(1)}, bf16[384,768]{1,0:T(8,128)(2,1)S(1)}) custom-call(f32[1]{0:T(128)S(6)} %copy.10.scale_ref, f32[1]{0:T(128)S(6)} %copy.11.shift_ref, s32[1]{0:T(128)} %bitcast.odd_ref, f32[1,192]{1,0:T(1,128)S(1)} %bitcast.10, bf16[416,768]{1,0:T(8,128)(2,1)S(1)} %collective-permute-done.inside_ref, ...), custom_call_target="tpu_custom_call" | custom-call | flops 452984832 | bytes 4128768 | tf_op jit(solution)/shard_map/pallas_call | solution.py:50
  44.3 0.0 copy-done.2
  44.3 0.0 copy-done.4
  44.4 0.0 copy-start.3
  44.4 1.0 copy-done.3
  45.3 0.0 copy-start.5
  45.3 1.0 copy-done.5
  46.3 0.0 copy-start
  46.3 0.0 copy-start.1
  46.3 2.5 %shard_map.87 = (bf16[384,768]{1,0:T(8,128)(2,1)}, bf16[384,768]{1,0:T(8,128)(2,1)}, bf16[192,768]{1,0:T(8,128)(2,1)}, bf16[192,768]{1,0:T(8,128)(2,1)}, f32[192,768]{1,0:T(8,128)S(1)}) custom-call(s32[1]{0:T(128)} %bitcast.odd_ref, bf16[384,768]{1,0:T(8,128)(2,1)S(1)} %get-tuple-element.17.factors, bf16[416,768]{1,0:T(8,128)(2,1)S(1)} %collective-permute-done.inside_ref, ...), custom_call_target="tpu_custom_call" | custom-call | flops 905969664 | bytes 4128768 | tf_op jit(solution)/shard_map/pallas_call | solution.py:50
  48.8 11.4 %collective-permute-start.4 = (bf16[384,768]{1,0:T(8,128)(2,1)}, bf16[384,768]{1,0:T(8,128)(2,1)S(1)}, u32[]{:S(2)}, u32[]{:S(2)}) collective-permute-start(bf16[384,768]{1,0:T(8,128)(2,1)} %get-tuple-element.18), channel_id=1, source_target_pairs={{0,992},{16,1008},{32,64},{48,80},{64,32},{80,48},{96,128},{112,14... | collective-permute-start | bytes 1769480 | tf_op jit(solution)/shard_map/ppermute | solution.py:22
  60.2 1.9 %collective-permute-start.5 = (bf16[384,768]{1,0:T(8,128)(2,1)}, bf16[384,768]{1,0:T(8,128)(2,1)S(1)}, u32[]{:S(2)}, u32[]{:S(2)}) collective-permute-start(bf16[384,768]{1,0:T(8,128)(2,1)} %get-tuple-element.19), channel_id=1, source_target_pairs={{0,32},{16,48},{32,0},{48,16},{64,96},{80,112},{96,64},{112,80},{1... | collective-permute-start | bytes 1769480 | tf_op jit(solution)/shard_map/ppermute | solution.py:22
  62.2 1.9 %collective-permute-start.6 = (bf16[192,768]{1,0:T(8,128)(2,1)}, bf16[192,768]{1,0:T(8,128)(2,1)S(1)}, u32[]{:S(2)}, u32[]{:S(2)}) collective-permute-start(bf16[192,768]{1,0:T(8,128)(2,1)} %get-tuple-element.20), channel_id=1, source_target_pairs={{0,1008},{16,32},{32,16},{48,64},{64,48},{80,96},{96,80},{112,128}... | collective-permute-start | bytes 884744 | tf_op jit(solution)/shard_map/ppermute | solution.py:22
  64.1 3.0 %collective-permute-start.7 = (bf16[192,768]{1,0:T(8,128)(2,1)}, bf16[192,768]{1,0:T(8,128)(2,1)}, u32[]{:S(2)}, u32[]{:S(2)}) collective-permute-start(bf16[192,768]{1,0:T(8,128)(2,1)} %get-tuple-element.21), channel_id=1, source_target_pairs={{0,16},{16,0},{32,48},{48,32},{64,80},{80,64},{96,112},{112,96},{1... | collective-permute-start | bytes 884744 | tf_op jit(solution)/shard_map/ppermute | solution.py:22
  67.1 11.1 %all_to_all.10 = f32[32,1,128]{2,1,0:T(1,128)S(1)} all-to-all(f32[32,1,128]{2,1,0:T(1,128)S(1)} %broadcast_in_dim.13), channel_id=1, replica_groups={{0,4,8,12,16,20,24,28,32,36,40,44,48,52,56,60,64,68,72,76,80,84,88,92,9..., dimensions={0} | all-to-all | bytes 32768 | tf_op jit(solution)/shard_map/all_to_all | solution.py:271
  78.2 41.5 %all_to_all.11 = f32[32,1,128]{2,1,0:T(1,128)S(1)} all-to-all(f32[32,1,128]{2,1,0:T(1,128)S(1)} %broadcast_in_dim.14), channel_id=1, replica_groups={{0,1,2,3,128,129,130,131,256,257,258,259,384,385,386,387,512,513,514,51..., dimensions={0} | all-to-all | bytes 32768 | tf_op jit(solution)/shard_map/all_to_all | solution.py:271
  119.8 0.0 collective-permute-done.6.next_ref
  119.8 0.0 collective-permute-done.7.other_ref
  119.8 0.0 collective-permute-done.4.across_ref
  119.8 0.0 collective-permute-done.5.inside_ref
  119.8 0.0 copy-done
  119.8 0.0 copy-done.1
  119.8 2.6 %shard_map.88 = (f32[192,768]{1,0:T(8,128)}, f32[192,768]{1,0:T(8,128)}, f32[1,1]{1,0:T(1,128)}) custom-call(f32[192,768]{1,0:T(8,128)S(1)} %copy-done, f32[192,768]{1,0:T(8,128)S(1)} %copy-done.1, bf16[384,768]{1,0:T(8,128)(2,1)S(1)} %collective-permute-done.4.across_ref, bf16[384,768]{1,0:T(8,128)(2,1)S(1)} %collective-permute-done.5.inside_ref, ...), custom_call_target="tpu_custom_call" | custom-call | flops 2949120 | bytes 4423680 | tf_op jit(solution)/shard_map/pallas_call | solution.py:50
  (4 shorter events, 0.0 us)
Async XLA Ops:
  0.6 0.7 copy-start.7
  0.6 0.7 copy-start.6
  2.8 37.9 %collective-permute-start.1 = (bf16[416,768]{1,0:T(8,128)(2,1)S(1)}, bf16[416,768]{1,0:T(8,128)(2,1)S(1)}, u32[]{:S(2)}, u32[]{:S(2)}) collective-permute-start(bf16[416,768]{1,0:T(8,128)(2,1)S(1)} %get-tuple-element.15), channel_id=1, source_target_pairs={{0,992},{16,1008},{32,64},{48,80},{64,32},{80,48},{96,128},{112,14... | collective-permute-start | bytes 1916936 | tf_op jit(solution)/shard_map/ppermute | solution.py:22
  18.9 21.7 %collective-permute-start = (bf16[416,768]{1,0:T(8,128)(2,1)S(1)}, bf16[416,768]{1,0:T(8,128)(2,1)S(1)}, u32[]{:S(2)}, u32[]{:S(2)}) collective-permute-start(bf16[416,768]{1,0:T(8,128)(2,1)S(1)} %get-tuple-element.15), channel_id=1, source_target_pairs={{0,32},{16,48},{32,0},{48,16},{64,96},{80,112},{96,64},{112,80},{1... | collective-permute-start | bytes 1916936 | tf_op jit(solution)/shard_map/ppermute | solution.py:22
  20.9 7.7 %collective-permute-start.3 = (bf16[208,768]{1,0:T(8,128)(2,1)S(1)}, bf16[208,768]{1,0:T(8,128)(2,1)S(1)}, u32[]{:S(2)}, u32[]{:S(2)}) collective-permute-start(bf16[208,768]{1,0:T(8,128)(2,1)S(1)} %get-tuple-element.16.own_ref), channel_id=1, source_target_pairs={{0,16},{16,0},{32,48},{48,32},{64,80},{80,64},{96,112},{112,96},{1... | collective-permute-start | bytes 958472 | tf_op jit(solution)/shard_map/ppermute | solution.py:22
  23.7 16.9 %collective-permute-start.2 = (bf16[208,768]{1,0:T(8,128)(2,1)S(1)}, bf16[208,768]{1,0:T(8,128)(2,1)S(1)}, u32[]{:S(2)}, u32[]{:S(2)}) collective-permute-start(bf16[208,768]{1,0:T(8,128)(2,1)S(1)} %get-tuple-element.16.own_ref), channel_id=1, source_target_pairs={{0,1008},{16,32},{32,16},{48,64},{64,48},{80,96},{96,80},{112,128}... | collective-permute-start | bytes 958472 | tf_op jit(solution)/shard_map/ppermute | solution.py:22
  28.6 15.8 %copy-start.2 = (bf16[208,768]{1,0:T(8,128)(2,1)}, bf16[208,768]{1,0:T(8,128)(2,1)S(1)}, u32[]{:S(2)}) copy-start(bf16[208,768]{1,0:T(8,128)(2,1)S(1)} %collective-permute-done.3.other_ref) | copy-start | bytes 958468
  40.6 3.7 %copy-start.4 = (bf16[208,768]{1,0:T(8,128)(2,1)}, bf16[208,768]{1,0:T(8,128)(2,1)S(1)}, u32[]{:S(2)}) copy-start(bf16[208,768]{1,0:T(8,128)(2,1)S(1)} %collective-permute-done.2.next_ref) | copy-start | bytes 958468
  44.4 1.0 copy-start.3
  45.3 1.0 copy-start.5
  46.3 73.5 %copy-start = (f32[192,768]{1,0:T(8,128)S(1)}, f32[192,768]{1,0:T(8,128)}, u32[]{:S(2)}) copy-start(f32[192,768]{1,0:T(8,128)} %img_ref.3) | copy-start | bytes 1769476
  46.3 73.5 %copy-start.1 = (f32[192,768]{1,0:T(8,128)S(1)}, f32[192,768]{1,0:T(8,128)}, u32[]{:S(2)}) copy-start(f32[192,768]{1,0:T(8,128)} %txt_ref.3) | copy-start | bytes 1769476
  48.8 71.0 %collective-permute-start.4 = (bf16[384,768]{1,0:T(8,128)(2,1)}, bf16[384,768]{1,0:T(8,128)(2,1)S(1)}, u32[]{:S(2)}, u32[]{:S(2)}) collective-permute-start(bf16[384,768]{1,0:T(8,128)(2,1)} %get-tuple-element.18), channel_id=1, source_target_pairs={{0,992},{16,1008},{32,64},{48,80},{64,32},{80,48},{96,128},{112,14... | collective-permute-start | bytes 1769480 | tf_op jit(solution)/shard_map/ppermute | solution.py:22
  60.2 59.6 %collective-permute-start.5 = (bf16[384,768]{1,0:T(8,128)(2,1)}, bf16[384,768]{1,0:T(8,128)(2,1)S(1)}, u32[]{:S(2)}, u32[]{:S(2)}) collective-permute-start(bf16[384,768]{1,0:T(8,128)(2,1)} %get-tuple-element.19), channel_id=1, source_target_pairs={{0,32},{16,48},{32,0},{48,16},{64,96},{80,112},{96,64},{112,80},{1... | collective-permute-start | bytes 1769480 | tf_op jit(solution)/shard_map/ppermute | solution.py:22
  62.2 57.6 %collective-permute-start.6 = (bf16[192,768]{1,0:T(8,128)(2,1)}, bf16[192,768]{1,0:T(8,128)(2,1)S(1)}, u32[]{:S(2)}, u32[]{:S(2)}) collective-permute-start(bf16[192,768]{1,0:T(8,128)(2,1)} %get-tuple-element.20), channel_id=1, source_target_pairs={{0,1008},{16,32},{32,16},{48,64},{64,48},{80,96},{96,80},{112,128}... | collective-permute-start | bytes 884744 | tf_op jit(solution)/shard_map/ppermute | solution.py:22
  64.1 55.7 %collective-permute-start.7 = (bf16[192,768]{1,0:T(8,128)(2,1)}, bf16[192,768]{1,0:T(8,128)(2,1)}, u32[]{:S(2)}, u32[]{:S(2)}) collective-permute-start(bf16[192,768]{1,0:T(8,128)(2,1)} %get-tuple-element.21), channel_id=1, source_target_pairs={{0,16},{16,0},{32,48},{48,32},{64,80},{80,64},{96,112},{112,96},{1... | collective-permute-start | bytes 884744 | tf_op jit(solution)/shard_map/ppermute | solution.py:22

commit v6 on v5

--- a/solution.py
+++ b/solution.py
@@ -110,13 +110,27 @@
             target[rows:block, :] = extra
 
 
-def stack_blocks(rows, odd_ref, inside_ref, across_ref, next_ref, other_ref, own_ref, txts, imgs):
+def stack_blocks(
+    rows, odd_ref, inside_ref, across_ref, next_ref, other_ref, own_ref, txts, imgs, tails, sems
+):
     block = rows + EXTRA
+    copies = []
+    for number, source in enumerate((next_ref, other_ref)):
+        copies += [
+            pltpu.make_async_copy(
+                source.at[0:rows],
+                txts.at[2 * number * rows : (2 * number + 1) * rows],
+                sems.at[2 * number],
+            ),
+            pltpu.make_async_copy(
+                source.at[rows:block], tails.at[number], sems.at[2 * number + 1]
+            ),
+        ]
+    for copy in copies:
+        copy.start()
     imgs[0:rows, :] = inside_ref[0:rows, :]
     imgs[rows : 2 * rows, :] = across_ref[0:rows, :]
-    txts[0:rows, :] = next_ref[0:rows, :]
     txts[rows : 2 * rows, :] = own_ref[0:rows, :]
-    txts[2 * rows : 3 * rows, :] = other_ref[0:rows, :]
 
     @pl.when(odd_ref[0] == 0)
     def _():
@@ -126,8 +140,11 @@
     def _():
         txts[3 * rows : 4 * rows, :] = across_ref[block : block + rows, :]
 
-
-def score_kernel(
+    for copy in copies:
+        copy.wait()
+
+
+def tile_kernel(
     scale_ref,
     shift_ref,
     odd_ref,
@@ -138,18 +155,25 @@
     other_ref,
     own_ref,
     sums_ref,
+    inside_out,
+    across_out,
+    next_out,
+    other_out,
+    own_out,
     factors,
     txts,
     imgs,
     scores,
     columns,
+    tails,
+    sems,
 ):
     rows = own_ref.shape[0] - EXTRA
     block = rows + EXTRA
     scale = scale_ref[0]
     shift = shift_ref[0]
 
-    stack_blocks(rows, odd_ref, inside_ref, across_ref, next_ref, other_ref, own_ref, txts, imgs)
+    stack_blocks(rows, odd_ref, inside_ref, across_ref, next_ref, other_ref, own_ref, txts, imgs, tails, sems)
 
     lane = lax.broadcasted_iota(jnp.int32, (1, 4 * rows), 1)
     txt_keys = jnp.zeros((1, 4 * rows), jnp.float32)
@@ -159,7 +183,7 @@
         across_ref[block + rows : 2 * block, :].astype(jnp.float32),
     )
     extras = [
-        source[rows:block, :].astype(jnp.float32) for source in (next_ref, own_ref, other_ref)
+        part.astype(jnp.float32) for part in (tails[0], own_ref[rows:block, :], tails[1])
     ]
     for slot, extra in enumerate((*extras, ahead)):
         keys = extra[0:1] * 256.0 + extra[1:2]
@@ -207,25 +231,6 @@
         place == 0, loss_part, jnp.where(place == 1, weight_part, 0.0)
     )
 
-
-def grad_kernel(
-    odd_ref,
-    factors,
-    inside_ref,
-    across_ref,
-    next_ref,
-    other_ref,
-    own_ref,
-    inside_out,
-    across_out,
-    next_out,
-    other_out,
-    own_out,
-    txts,
-    imgs,
-):
-    rows = own_out.shape[0]
-    stack_blocks(rows, odd_ref, inside_ref, across_ref, next_ref, other_ref, own_ref, txts, imgs)
     img_grads = jnp.dot(factors[...], txts[...], preferred_element_type=jnp.float32)
     img_grads = img_grads.astype(jnp.bfloat16)
     inside_out[0:rows, :] = img_grads[0:rows]
@@ -313,41 +318,32 @@
     inside = with_chip_inside(pair)
     next_core = with_next_core(txt_block)
     other_core = with_other_core(txt_block)
-    blocks = (inside, across, next_core, other_core, txt_block)
-    stacks = [
-        pltpu.VMEM((4 * rows, width), jnp.bfloat16),
-        pltpu.VMEM((2 * rows, width), jnp.bfloat16),
-    ]
-    sums, factors = call(
-        score_kernel,
-        [full(8, 128), half(2 * rows, 4 * rows)],
-        (scale, shift, odd, row_weights, *blocks),
-        smem * 3 + vmem(6),
-        stacks
-        + [
-            pltpu.VMEM((2 * rows, 4 * rows), jnp.float32),
-            pltpu.VMEM((2 * rows, EXTRA), jnp.float32),
-        ],
-        16 * rows * rows * width,
-        24 * rows * rows,
-        28 * rows * width,
-        VMEM_BYTES,
-    )
-    parts = call(
-        grad_kernel,
+    near = [pltpu.with_memory_space_constraint(x, pltpu.HBM) for x in (next_core, other_core)]
+    blocks = (inside, across, *near, txt_block)
+    sums, *parts = call(
+        tile_kernel,
         [
+            full(8, 128),
             half(2 * rows, width),
             half(2 * rows, width),
             half(rows, width),
             half(rows, width),
             full(rows, width),
         ],
-        (odd, factors, *blocks),
-        smem + vmem(6),
-        stacks,
-        32 * rows * rows * width,
-        0,
-        28 * rows * width,
+        (scale, shift, odd, row_weights, *blocks),
+        smem * 3 + vmem(3) + hbm + vmem(1),
+        [
+            pltpu.VMEM((2 * rows, 4 * rows), jnp.bfloat16),
+            pltpu.VMEM((4 * rows, width), jnp.bfloat16),
+            pltpu.VMEM((2 * rows, width), jnp.bfloat16),
+            pltpu.VMEM((2 * rows, 4 * rows), jnp.float32),
+            pltpu.VMEM((2 * rows, EXTRA), jnp.float32),
+            pltpu.VMEM((2, EXTRA, width), jnp.bfloat16),
+            pltpu.SemaphoreType.DMA((4,)),
+        ],
+        48 * rows * rows * width,
+        24 * rows * rows,
+        40 * rows * width,
         VMEM_BYTES,
     )
     planes, columns = plane_and_column_groups()

time: 123 us -> 123 us (level)
    unnamed x16 -> x12, local copies, waits for them, and re-layouts: 2.64 us -> 1.38 us
    pallas_call x4 -> x3, Pallas kernels: 10.2 us -> 10.3 us  [call(): pl.pallas_call(kernel, out_shape=outs, in_specs=specs, out_specs=vmem(len...]
  transfers between devices with their start and end apart: 8 -> 8, of which waited for: 1 -> 1; matrix products, arithmetic and copies ran while one was open for 0% -> 1% of each run, Pallas kernels for 0% -> 0%
where the time goes in v6:
time: 123 us; the launch traced here: 122 us
  blocking collectives  52.7 us (43%)
  starting transfers between devices  42.7 us (35%)
  waiting for transfers between devices  12.1 us (10%)
  Pallas kernels  10.3 us (8%)
  between operations  2.1 us (2%)
  local copies, waits for them, and re-layouts  2.06 us (2%)
    all_to_all x2, blocking collectives, exchange(): lax.all_to_all(spread, ('blk', 'group'), 0, 0, tiled=True, axis_index_gro...  52.7 us
    ppermute x8, starting transfers between devices, exchange_pairs(): return lax.ppermute(value, 'blk', sorted(pairs))  42.7 us
    ppermute x8, waiting for transfers between devices, exchange_pairs(): return lax.ppermute(value, 'blk', sorted(pairs))  12.1 us
    pallas_call x3, Pallas kernels, call(): pl.pallas_call(kernel, out_shape=outs, in_specs=specs, out_specs=vmem(len...  10.3 us
  transfers between devices with their start and end apart: 8, of which 1 were waited for; matrix products, arithmetic and copies ran while one was open for 1% of the time, Pallas kernels for 0%

profile of v6, /device:TPU:1, one launch (start us, length us, event | category | flops | bytes accessed | tf_op | source)
XLA Modules:
  0.0 122.5 jit_solution(16337545254659340658)
XLA Ops:
  0.6 0.0 copy-start.3
  0.6 0.0 copy-start.2
  0.7 0.7 copy-done.3
  1.3 0.0 copy-done.2
  1.3 1.4 %shard_map.85 = (bf16[416,768]{1,0:T(8,128)(2,1)S(1)}, bf16[208,768]{1,0:T(8,128)(2,1)S(1)}) custom-call(f32[192,768]{1,0:T(8,128)} %img_ref.3, f32[192,768]{1,0:T(8,128)} %txt_ref.3, s32[1,192]{1,0:T(1,128)S(1)} %bitcast.9, f32[1,192]{1,0:T(1,128)S(1)} %bitcast.10), custom_call_target="tpu_custom_call" | custom-call | flops 884736 | bytes 2359296 | tf_op jit(solution)/shard_map/pallas_call | solution.py:50
  2.8 16.2 %collective-permute-start.1 = (bf16[416,768]{1,0:T(8,128)(2,1)S(1)}, bf16[416,768]{1,0:T(8,128)(2,1)S(1)}, u32[]{:S(2)}, u32[]{:S(2)}) collective-permute-start(bf16[416,768]{1,0:T(8,128)(2,1)S(1)} %get-tuple-element.14), channel_id=1, source_target_pairs={{0,992},{16,1008},{32,64},{48,80},{64,32},{80,48},{96,128},{112,14... | collective-permute-start | bytes 1916936 | tf_op jit(solution)/shard_map/ppermute | solution.py:22
  18.9 1.9 %collective-permute-start = (bf16[416,768]{1,0:T(8,128)(2,1)S(1)}, bf16[416,768]{1,0:T(8,128)(2,1)S(1)}, u32[]{:S(2)}, u32[]{:S(2)}) collective-permute-start(bf16[416,768]{1,0:T(8,128)(2,1)S(1)} %get-tuple-element.14), channel_id=1, source_target_pairs={{0,32},{16,48},{32,0},{48,16},{64,96},{80,112},{96,64},{112,80},{1... | collective-permute-start | bytes 1916936 | tf_op jit(solution)/shard_map/ppermute | solution.py:22
  20.9 2.9 %collective-permute-start.3 = (bf16[208,768]{1,0:T(8,128)(2,1)S(1)}, bf16[208,768]{1,0:T(8,128)(2,1)S(1)}, u32[]{:S(2)}, u32[]{:S(2)}) collective-permute-start(bf16[208,768]{1,0:T(8,128)(2,1)S(1)} %get-tuple-element.15.own_ref), channel_id=1, source_target_pairs={{0,16},{16,0},{32,48},{48,32},{64,80},{80,64},{96,112},{112,96},{1... | collective-permute-start | bytes 958472 | tf_op jit(solution)/shard_map/ppermute | solution.py:22
  23.7 3.5 %collective-permute-start.2 = (bf16[208,768]{1,0:T(8,128)(2,1)S(1)}, bf16[208,768]{1,0:T(8,128)(2,1)S(1)}, u32[]{:S(2)}, u32[]{:S(2)}) collective-permute-start(bf16[208,768]{1,0:T(8,128)(2,1)S(1)} %get-tuple-element.15.own_ref), channel_id=1, source_target_pairs={{0,1008},{16,32},{32,16},{48,64},{64,48},{80,96},{96,80},{112,128}... | collective-permute-start | bytes 958472 | tf_op jit(solution)/shard_map/ppermute | solution.py:22
  28.6 0.0 collective-permute-done.3.other_ref
  28.6 0.0 copy-start.4
  28.6 12.1 %collective-permute-done.2.next_ref = bf16[208,768]{1,0:T(8,128)(2,1)S(1)} collective-permute-done((bf16[208,768]{1,0:T(8,128)(2,1)S(1)}, bf16[208,768]{1,0:T(8,128)(2,1)S(1)}, u32[]{:S(2)}, u32[]{:S(2)}) %collective-permute-start.2) | collective-permute-done | bytes 319520 | tf_op jit(solution)/shard_map/ppermute | solution.py:22
  40.6 0.0 copy-start.5
  40.6 0.0 collective-permute-done.1.across_ref
  40.7 0.0 collective-permute-done.inside_ref
  40.7 0.0 copy-done.4
  40.7 0.7 copy-done.5
  41.4 0.0 copy-start
  41.4 0.0 copy-start.1
  41.4 7.3 %shard_map.86 = (f32[8,128]{1,0:T(8,128)S(1)}, bf16[384,768]{1,0:T(8,128)(2,1)}, bf16[384,768]{1,0:T(8,128)(2,1)}, bf16[192,768]{1,0:T(8,128)(2,1)}, bf16[192,768]{1,0:T(8,128)(2,1)}, /*index=5*/f32[192,768]{1,0:T(8,128)S(1)}) custom-call(f32[1]{0:T(128)S(6)} %copy.10.scale_ref, f32[1]{0:T(128)S(6)} %copy.11.shift_ref, s32[1]{0:T(128)} %bitcast.odd_ref, ...), custom_call_target="tpu_custom_call" | custom-call | flops 1358954496 | bytes 5898240 | tf_op jit(solution)/shard_map/pallas_call | solution.py:50
  48.7 11.4 %collective-permute-start.4 = (bf16[384,768]{1,0:T(8,128)(2,1)}, bf16[384,768]{1,0:T(8,128)(2,1)S(1)}, u32[]{:S(2)}, u32[]{:S(2)}) collective-permute-start(bf16[384,768]{1,0:T(8,128)(2,1)} %get-tuple-element.16), channel_id=1, source_target_pairs={{0,992},{16,1008},{32,64},{48,80},{64,32},{80,48},{96,128},{112,14... | collective-permute-start | bytes 1769480 | tf_op jit(solution)/shard_map/ppermute | solution.py:22
  60.1 1.9 %collective-permute-start.5 = (bf16[384,768]{1,0:T(8,128)(2,1)}, bf16[384,768]{1,0:T(8,128)(2,1)S(1)}, u32[]{:S(2)}, u32[]{:S(2)}) collective-permute-start(bf16[384,768]{1,0:T(8,128)(2,1)} %get-tuple-element.17), channel_id=1, source_target_pairs={{0,32},{16,48},{32,0},{48,16},{64,96},{80,112},{96,64},{112,80},{1... | collective-permute-start | bytes 1769480 | tf_op jit(solution)/shard_map/ppermute | solution.py:22
  62.1 1.9 %collective-permute-start.6 = (bf16[192,768]{1,0:T(8,128)(2,1)}, bf16[192,768]{1,0:T(8,128)(2,1)S(1)}, u32[]{:S(2)}, u32[]{:S(2)}) collective-permute-start(bf16[192,768]{1,0:T(8,128)(2,1)} %get-tuple-element.18), channel_id=1, source_target_pairs={{0,1008},{16,32},{32,16},{48,64},{64,48},{80,96},{96,80},{112,128}... | collective-permute-start | bytes 884744 | tf_op jit(solution)/shard_map/ppermute | solution.py:22
  64.0 3.0 %collective-permute-start.7 = (bf16[192,768]{1,0:T(8,128)(2,1)}, bf16[192,768]{1,0:T(8,128)(2,1)S(1)}, u32[]{:S(2)}, u32[]{:S(2)}) collective-permute-start(bf16[192,768]{1,0:T(8,128)(2,1)} %get-tuple-element.19), channel_id=1, source_target_pairs={{0,16},{16,0},{32,48},{48,32},{64,80},{80,64},{96,112},{112,96},{1... | collective-permute-start | bytes 884744 | tf_op jit(solution)/shard_map/ppermute | solution.py:22
  67.0 11.1 %all_to_all.10 = f32[32,1,128]{2,1,0:T(1,128)S(1)} all-to-all(f32[32,1,128]{2,1,0:T(1,128)S(1)} %broadcast_in_dim.13), channel_id=1, replica_groups={{0,4,8,12,16,20,24,28,32,36,40,44,48,52,56,60,64,68,72,76,80,84,88,92,9..., dimensions={0} | all-to-all | bytes 32768 | tf_op jit(solution)/shard_map/all_to_all | solution.py:276
  78.1 0.5 reduce_sum.9
  78.6 0.7 broadcast_in_dim.14
  79.3 41.5 %all_to_all.11 = f32[32,1,128]{2,1,0:T(1,128)S(1)} all-to-all(f32[32,1,128]{2,1,0:T(1,128)S(1)} %broadcast_in_dim.14), channel_id=1, replica_groups={{0,1,2,3,128,129,130,131,256,257,258,259,384,385,386,387,512,513,514,51..., dimensions={0} | all-to-all | bytes 32768 | tf_op jit(solution)/shard_map/all_to_all | solution.py:276
  120.8 0.0 collective-permute-done.6.next_ref
  120.8 0.0 collective-permute-done.7.other_ref
  120.9 0.0 collective-permute-done.4.across_ref
  120.9 0.0 collective-permute-done.5.inside_ref
  120.9 0.0 copy-done
  120.9 0.0 copy-done.1
  120.9 1.6 %shard_map.87 = (f32[192,768]{1,0:T(8,128)}, f32[192,768]{1,0:T(8,128)}, f32[1,1]{1,0:T(1,128)}) custom-call(f32[192,768]{1,0:T(8,128)S(1)} %copy-done, f32[192,768]{1,0:T(8,128)S(1)} %copy-done.1, bf16[384,768]{1,0:T(8,128)(2,1)S(1)} %collective-permute-done.4.across_ref, bf16[384,768]{1,0:T(8,128)(2,1)S(1)} %collective-permute-done.5.inside_ref, ...), custom_call_target="tpu_custom_call" | custom-call | flops 2949120 | bytes 4423680 | tf_op jit(solution)/shard_map/pallas_call | solution.py:50
  (2 shorter events, 0.0 us)
Async XLA Ops:
  0.6 0.7 copy-start.3
  0.6 0.7 copy-start.2
  2.8 37.9 %collective-permute-start.1 = (bf16[416,768]{1,0:T(8,128)(2,1)S(1)}, bf16[416,768]{1,0:T(8,128)(2,1)S(1)}, u32[]{:S(2)}, u32[]{:S(2)}) collective-permute-start(bf16[416,768]{1,0:T(8,128)(2,1)S(1)} %get-tuple-element.14), channel_id=1, source_target_pairs={{0,992},{16,1008},{32,64},{48,80},{64,32},{80,48},{96,128},{112,14... | collective-permute-start | bytes 1916936 | tf_op jit(solution)/shard_map/ppermute | solution.py:22
  18.9 21.7 %collective-permute-start = (bf16[416,768]{1,0:T(8,128)(2,1)S(1)}, bf16[416,768]{1,0:T(8,128)(2,1)S(1)}, u32[]{:S(2)}, u32[]{:S(2)}) collective-permute-start(bf16[416,768]{1,0:T(8,128)(2,1)S(1)} %get-tuple-element.14), channel_id=1, source_target_pairs={{0,32},{16,48},{32,0},{48,16},{64,96},{80,112},{96,64},{112,80},{1... | collective-permute-start | bytes 1916936 | tf_op jit(solution)/shard_map/ppermute | solution.py:22
  20.9 7.7 %collective-permute-start.3 = (bf16[208,768]{1,0:T(8,128)(2,1)S(1)}, bf16[208,768]{1,0:T(8,128)(2,1)S(1)}, u32[]{:S(2)}, u32[]{:S(2)}) collective-permute-start(bf16[208,768]{1,0:T(8,128)(2,1)S(1)} %get-tuple-element.15.own_ref), channel_id=1, source_target_pairs={{0,16},{16,0},{32,48},{48,32},{64,80},{80,64},{96,112},{112,96},{1... | collective-permute-start | bytes 958472 | tf_op jit(solution)/shard_map/ppermute | solution.py:22
  23.7 16.9 %collective-permute-start.2 = (bf16[208,768]{1,0:T(8,128)(2,1)S(1)}, bf16[208,768]{1,0:T(8,128)(2,1)S(1)}, u32[]{:S(2)}, u32[]{:S(2)}) collective-permute-start(bf16[208,768]{1,0:T(8,128)(2,1)S(1)} %get-tuple-element.15.own_ref), channel_id=1, source_target_pairs={{0,1008},{16,32},{32,16},{48,64},{64,48},{80,96},{96,80},{112,128}... | collective-permute-start | bytes 958472 | tf_op jit(solution)/shard_map/ppermute | solution.py:22
  28.6 12.1 %copy-start.4 = (bf16[208,768]{1,0:T(8,128)(2,1)}, bf16[208,768]{1,0:T(8,128)(2,1)S(1)}, u32[]{:S(2)}) copy-start(bf16[208,768]{1,0:T(8,128)(2,1)S(1)} %collective-permute-done.3.other_ref) | copy-start | bytes 958468
  40.6 0.7 copy-start.5
  41.4 79.5 %copy-start = (f32[192,768]{1,0:T(8,128)S(1)}, f32[192,768]{1,0:T(8,128)}, u32[]{:S(2)}) copy-start(f32[192,768]{1,0:T(8,128)} %img_ref.3) | copy-start | bytes 1769476
  41.4 79.5 %copy-start.1 = (f32[192,768]{1,0:T(8,128)S(1)}, f32[192,768]{1,0:T(8,128)}, u32[]{:S(2)}) copy-start(f32[192,768]{1,0:T(8,128)} %txt_ref.3) | copy-start | bytes 1769476
  48.7 72.2 %collective-permute-start.4 = (bf16[384,768]{1,0:T(8,128)(2,1)}, bf16[384,768]{1,0:T(8,128)(2,1)S(1)}, u32[]{:S(2)}, u32[]{:S(2)}) collective-permute-start(bf16[384,768]{1,0:T(8,128)(2,1)} %get-tuple-element.16), channel_id=1, source_target_pairs={{0,992},{16,1008},{32,64},{48,80},{64,32},{80,48},{96,128},{112,14... | collective-permute-start | bytes 1769480 | tf_op jit(solution)/shard_map/ppermute | solution.py:22
  60.1 60.7 %collective-permute-start.5 = (bf16[384,768]{1,0:T(8,128)(2,1)}, bf16[384,768]{1,0:T(8,128)(2,1)S(1)}, u32[]{:S(2)}, u32[]{:S(2)}) collective-permute-start(bf16[384,768]{1,0:T(8,128)(2,1)} %get-tuple-element.17), channel_id=1, source_target_pairs={{0,32},{16,48},{32,0},{48,16},{64,96},{80,112},{96,64},{112,80},{1... | collective-permute-start | bytes 1769480 | tf_op jit(solution)/shard_map/ppermute | solution.py:22
  62.1 58.8 %collective-permute-start.6 = (bf16[192,768]{1,0:T(8,128)(2,1)}, bf16[192,768]{1,0:T(8,128)(2,1)S(1)}, u32[]{:S(2)}, u32[]{:S(2)}) collective-permute-start(bf16[192,768]{1,0:T(8,128)(2,1)} %get-tuple-element.18), channel_id=1, source_target_pairs={{0,1008},{16,32},{32,16},{48,64},{64,48},{80,96},{96,80},{112,128}... | collective-permute-start | bytes 884744 | tf_op jit(solution)/shard_map/ppermute | solution.py:22
  64.0 56.9 %collective-permute-start.7 = (bf16[192,768]{1,0:T(8,128)(2,1)}, bf16[192,768]{1,0:T(8,128)(2,1)S(1)}, u32[]{:S(2)}, u32[]{:S(2)}) collective-permute-start(bf16[192,768]{1,0:T(8,128)(2,1)} %get-tuple-element.19), channel_id=1, source_target_pairs={{0,16},{16,0},{32,48},{48,32},{64,80},{80,64},{96,112},{112,96},{1... | collective-permute-start | bytes 884744 | tf_op jit(solution)/shard_map/ppermute | solution.py:22

commit v7 on v6

--- a/solution.py
+++ b/solution.py
@@ -222,7 +222,7 @@
         return total + weights * penalty
 
     total = lax.fori_loop(
-        0, 2 * rows // CHUNK, step, jnp.zeros((CHUNK, 4 * rows), jnp.float32)
+        0, 2 * rows // CHUNK, step, jnp.zeros((CHUNK, 4 * rows), jnp.float32), unroll=3
     )
     loss_part = jnp.sum(jnp.sum(total, 0, keepdims=True), 1, keepdims=True)
     weight_part = jnp.sum(weight_ref[...], 1, keepdims=True)
@@ -270,12 +270,15 @@
     loss_out[...] = sums[:, 0:1] / sums[:, 1:2]
 
 
-def exchange(part, groups):
-    count = len(groups[0])
-    spread = jnp.broadcast_to(part.reshape(1, 1, -1), (count, 1, part.shape[-1]))
+def spread_kernel(rows_ref, sum_ref):
+    total = jnp.sum(rows_ref[...], 0, keepdims=True)
+    sum_ref[...] = jnp.broadcast_to(total, sum_ref.shape)
+
+
+def exchange(spread, groups):
     return lax.all_to_all(
         spread, ("blk", "group"), 0, 0, tiled=True, axis_index_groups=groups
-    ).reshape(count, -1)
+    )
 
 
 def plane_and_column_groups():
@@ -347,13 +350,25 @@
         VMEM_BYTES,
     )
     planes, columns = plane_and_column_groups()
-    gathered = exchange(sums[0:1], planes)
+    first = jnp.broadcast_to(sums[0:1].reshape(1, 1, -1), (len(planes[0]), 1, sums.shape[1]))
+    gathered = exchange(first, planes)
     inside_part, across_part, next_part, other_part, own_part = parts
     across_back = with_chip_across(across_part)
     inside_back = with_chip_inside(inside_part)
     next_back = with_next_core(next_part)
     other_back = with_other_core(other_part)
-    gathered = exchange(jnp.sum(gathered, 0, keepdims=True), columns)
+    (second,) = call(
+        spread_kernel,
+        [full(len(columns[0]), 1, sums.shape[1])],
+        (gathered,),
+        vmem(1),
+        [],
+        4096,
+        0,
+        32768,
+        VMEM_BYTES,
+    )
+    gathered = exchange(second, columns).reshape(len(columns[0]), -1)
     image_grad, text_grad, loss = call(
         finish_kernel,
         [full(rows, width), full(rows, width), full(1, 1)],

time: 123 us -> 120 us (0.976)
  Pallas kernels: 10.3 us -> 8.14 us
    pallas_call x3 -> x4, Pallas kernels: 10.3 us -> 8.14 us  [call(): pl.pallas_call(kernel, out_shape=outs, in_specs=specs, out_specs=vmem(len...]
  transfers between devices with their start and end apart: 8 -> 8, of which waited for: 1 -> 1; matrix products, arithmetic and copies ran while one was open for 1% -> 0% of each run, Pallas kernels for 0% -> 0%
where the time goes in v7:
time: 120 us; the launch traced here: 119 us
  blocking collectives  52.7 us (44%)
  starting transfers between devices  42.7 us (36%)
  waiting for transfers between devices  12.1 us (10%)
  Pallas kernels  8.14 us (7%)
  between operations  2.1 us (2%)
  local copies, waits for them, and re-layouts  1.41 us (1%)
    all_to_all x2, blocking collectives, exchange(): lax.all_to_all(spread, ('blk', 'group'), 0, 0, tiled=True, axis_index_gro...  52.7 us
    ppermute x8, starting transfers between devices, exchange_pairs(): return lax.ppermute(value, 'blk', sorted(pairs))  42.7 us
    ppermute x8, waiting for transfers between devices, exchange_pairs(): return lax.ppermute(value, 'blk', sorted(pairs))  12.1 us
    pallas_call x4, Pallas kernels, call(): pl.pallas_call(kernel, out_shape=outs, in_specs=specs, out_specs=vmem(len...  8.14 us
  transfers between devices with their start and end apart: 8, of which 1 were waited for; matrix products, arithmetic and copies ran while one was open for 0% of the time, Pallas kernels for 0%

profile of v7, /device:TPU:1, one launch (start us, length us, event | category | flops | bytes accessed | tf_op | source)
XLA Modules:
  0.0 119.1 jit_solution(14626067508963050732)
XLA Ops:
  0.6 0.0 copy-start.3
  0.6 0.0 copy-start.2
  0.7 0.7 copy-done.3
  1.3 0.0 copy-done.2
  1.3 1.4 %shard_map.85 = (bf16[416,768]{1,0:T(8,128)(2,1)S(1)}, bf16[208,768]{1,0:T(8,128)(2,1)S(1)}) custom-call(f32[192,768]{1,0:T(8,128)} %img_ref.3, f32[192,768]{1,0:T(8,128)} %txt_ref.3, s32[1,192]{1,0:T(1,128)S(1)} %bitcast.8, f32[1,192]{1,0:T(1,128)S(1)} %bitcast.9), custom_call_target="tpu_custom_call" | custom-call | flops 884736 | bytes 2359296 | tf_op jit(solution)/shard_map/pallas_call | solution.py:50
  2.8 16.2 %collective-permute-start.1 = (bf16[416,768]{1,0:T(8,128)(2,1)S(1)}, bf16[416,768]{1,0:T(8,128)(2,1)S(1)}, u32[]{:S(2)}, u32[]{:S(2)}) collective-permute-start(bf16[416,768]{1,0:T(8,128)(2,1)S(1)} %get-tuple-element.14), channel_id=1, source_target_pairs={{0,992},{16,1008},{32,64},{48,80},{64,32},{80,48},{96,128},{112,14... | collective-permute-start | bytes 1916936 | tf_op jit(solution)/shard_map/ppermute | solution.py:22
  18.9 1.9 %collective-permute-start = (bf16[416,768]{1,0:T(8,128)(2,1)S(1)}, bf16[416,768]{1,0:T(8,128)(2,1)S(1)}, u32[]{:S(2)}, u32[]{:S(2)}) collective-permute-start(bf16[416,768]{1,0:T(8,128)(2,1)S(1)} %get-tuple-element.14), channel_id=1, source_target_pairs={{0,32},{16,48},{32,0},{48,16},{64,96},{80,112},{96,64},{112,80},{1... | collective-permute-start | bytes 1916936 | tf_op jit(solution)/shard_map/ppermute | solution.py:22
  20.9 2.9 %collective-permute-start.3 = (bf16[208,768]{1,0:T(8,128)(2,1)S(1)}, bf16[208,768]{1,0:T(8,128)(2,1)S(1)}, u32[]{:S(2)}, u32[]{:S(2)}) collective-permute-start(bf16[208,768]{1,0:T(8,128)(2,1)S(1)} %get-tuple-element.15.own_ref), channel_id=1, source_target_pairs={{0,16},{16,0},{32,48},{48,32},{64,80},{80,64},{96,112},{112,96},{1... | collective-permute-start | bytes 958472 | tf_op jit(solution)/shard_map/ppermute | solution.py:22
  23.7 3.5 %collective-permute-start.2 = (bf16[208,768]{1,0:T(8,128)(2,1)S(1)}, bf16[208,768]{1,0:T(8,128)(2,1)S(1)}, u32[]{:S(2)}, u32[]{:S(2)}) collective-permute-start(bf16[208,768]{1,0:T(8,128)(2,1)S(1)} %get-tuple-element.15.own_ref), channel_id=1, source_target_pairs={{0,1008},{16,32},{32,16},{48,64},{64,48},{80,96},{96,80},{112,128}... | collective-permute-start | bytes 958472 | tf_op jit(solution)/shard_map/ppermute | solution.py:22
  28.6 0.0 collective-permute-done.3.other_ref
  28.6 0.0 copy-start.4
  28.6 12.1 %collective-permute-done.2.next_ref = bf16[208,768]{1,0:T(8,128)(2,1)S(1)} collective-permute-done((bf16[208,768]{1,0:T(8,128)(2,1)S(1)}, bf16[208,768]{1,0:T(8,128)(2,1)S(1)}, u32[]{:S(2)}, u32[]{:S(2)}) %collective-permute-start.2) | collective-permute-done | bytes 319520 | tf_op jit(solution)/shard_map/ppermute | solution.py:22
  40.6 0.0 copy-start.5
  40.6 0.0 collective-permute-done.1.across_ref
  40.7 0.0 collective-permute-done.inside_ref
  40.7 0.0 copy-done.4
  40.7 0.7 copy-done.5
  41.4 0.0 copy-start
  41.4 0.0 copy-start.1
  41.4 5.0 %shard_map.86 = (f32[8,128]{1,0:T(8,128)S(1)}, bf16[384,768]{1,0:T(8,128)(2,1)S(1)}, bf16[384,768]{1,0:T(8,128)(2,1)S(1)}, bf16[192,768]{1,0:T(8,128)(2,1)S(1)},...) custom-call(f32[1]{0:T(128)S(6)} %copy.10.scale_ref, f32[1]{0:T(128)S(6)} %copy.11.shift_ref, s32[1]{0:T(128)} %bitcast.odd_ref, ...), custom_call_target="tpu_custom_call" | custom-call | flops 1358954496 | bytes 5898240 | tf_op jit(solution)/shard_map/pallas_call | solution.py:50
  46.4 11.4 %collective-permute-start.4 = (bf16[384,768]{1,0:T(8,128)(2,1)S(1)}, bf16[384,768]{1,0:T(8,128)(2,1)S(1)}, u32[]{:S(2)}, u32[]{:S(2)}) collective-permute-start(bf16[384,768]{1,0:T(8,128)(2,1)S(1)} %get-tuple-element.16), channel_id=1, source_target_pairs={{0,992},{16,1008},{32,64},{48,80},{64,32},{80,48},{96,128},{112,14... | collective-permute-start | bytes 1769480 | tf_op jit(solution)/shard_map/ppermute | solution.py:22
  57.9 1.9 %collective-permute-start.5 = (bf16[384,768]{1,0:T(8,128)(2,1)S(1)}, bf16[384,768]{1,0:T(8,128)(2,1)S(1)}, u32[]{:S(2)}, u32[]{:S(2)}) collective-permute-start(bf16[384,768]{1,0:T(8,128)(2,1)S(1)} %get-tuple-element.17), channel_id=1, source_target_pairs={{0,32},{16,48},{32,0},{48,16},{64,96},{80,112},{96,64},{112,80},{1... | collective-permute-start | bytes 1769480 | tf_op jit(solution)/shard_map/ppermute | solution.py:22
  59.8 1.9 %collective-permute-start.6 = (bf16[192,768]{1,0:T(8,128)(2,1)S(1)}, bf16[192,768]{1,0:T(8,128)(2,1)S(1)}, u32[]{:S(2)}, u32[]{:S(2)}) collective-permute-start(bf16[192,768]{1,0:T(8,128)(2,1)S(1)} %get-tuple-element.18), channel_id=1, source_target_pairs={{0,1008},{16,32},{32,16},{48,64},{64,48},{80,96},{96,80},{112,128}... | collective-permute-start | bytes 884744 | tf_op jit(solution)/shard_map/ppermute | solution.py:22
  61.7 3.0 %collective-permute-start.7 = (bf16[192,768]{1,0:T(8,128)(2,1)S(1)}, bf16[192,768]{1,0:T(8,128)(2,1)S(1)}, u32[]{:S(2)}, u32[]{:S(2)}) collective-permute-start(bf16[192,768]{1,0:T(8,128)(2,1)S(1)} %get-tuple-element.19), channel_id=1, source_target_pairs={{0,16},{16,0},{32,48},{48,32},{64,80},{80,64},{96,112},{112,96},{1... | collective-permute-start | bytes 884744 | tf_op jit(solution)/shard_map/ppermute | solution.py:22
  64.7 11.1 %all_to_all.10.rows_ref = f32[32,1,128]{2,1,0:T(1,128)S(1)} all-to-all(f32[32,1,128]{2,1,0:T(1,128)S(1)} %broadcast_in_dim.8), channel_id=1, replica_groups={{0,4,8,12,16,20,24,28,32,36,40,44,48,52,56,60,64,68,72,76,80,84,88,92,9..., dimensions={0} | all-to-all | bytes 32768 | tf_op jit(solution)/shard_map/all_to_all | solution.py:279
  75.9 41.5 %all_to_all.11 = f32[32,1,128]{2,1,0:T(1,128)S(1)} all-to-all(f32[32,1,128]{2,1,0:T(1,128)S(1)} %shard_map.87), channel_id=1, replica_groups={{0,1,2,3,128,129,130,131,256,257,258,259,384,385,386,387,512,513,514,51..., dimensions={0} | all-to-all | bytes 32768 | tf_op jit(solution)/shard_map/all_to_all | solution.py:279
  117.4 0.0 collective-permute-done.6.next_ref
  117.4 0.0 collective-permute-done.7.other_ref
  117.4 0.0 collective-permute-done.4.across_ref
  117.4 0.0 collective-permute-done.5.inside_ref
  117.5 0.0 copy-done
  117.5 0.0 copy-done.1
  117.5 1.6 %shard_map.88 = (f32[192,768]{1,0:T(8,128)}, f32[192,768]{1,0:T(8,128)}, f32[1,1]{1,0:T(1,128)}) custom-call(f32[192,768]{1,0:T(8,128)S(1)} %copy-done, f32[192,768]{1,0:T(8,128)S(1)} %copy-done.1, bf16[384,768]{1,0:T(8,128)(2,1)S(1)} %collective-permute-done.4.across_ref, bf16[384,768]{1,0:T(8,128)(2,1)S(1)} %collective-permute-done.5.inside_ref, ...), custom_call_target="tpu_custom_call" | custom-call | flops 2949120 | bytes 4423680 | tf_op jit(solution)/shard_map/pallas_call | solution.py:50
  (3 shorter events, 0.1 us)
Async XLA Ops:
  0.6 0.7 copy-start.3
  0.6 0.7 copy-start.2
  2.8 37.9 %collective-permute-start.1 = (bf16[416,768]{1,0:T(8,128)(2,1)S(1)}, bf16[416,768]{1,0:T(8,128)(2,1)S(1)}, u32[]{:S(2)}, u32[]{:S(2)}) collective-permute-start(bf16[416,768]{1,0:T(8,128)(2,1)S(1)} %get-tuple-element.14), channel_id=1, source_target_pairs={{0,992},{16,1008},{32,64},{48,80},{64,32},{80,48},{96,128},{112,14... | collective-permute-start | bytes 1916936 | tf_op jit(solution)/shard_map/ppermute | solution.py:22
  18.9 21.7 %collective-permute-start = (bf16[416,768]{1,0:T(8,128)(2,1)S(1)}, bf16[416,768]{1,0:T(8,128)(2,1)S(1)}, u32[]{:S(2)}, u32[]{:S(2)}) collective-permute-start(bf16[416,768]{1,0:T(8,128)(2,1)S(1)} %get-tuple-element.14), channel_id=1, source_target_pairs={{0,32},{16,48},{32,0},{48,16},{64,96},{80,112},{96,64},{112,80},{1... | collective-permute-start | bytes 1916936 | tf_op jit(solution)/shard_map/ppermute | solution.py:22
  20.9 7.7 %collective-permute-start.3 = (bf16[208,768]{1,0:T(8,128)(2,1)S(1)}, bf16[208,768]{1,0:T(8,128)(2,1)S(1)}, u32[]{:S(2)}, u32[]{:S(2)}) collective-permute-start(bf16[208,768]{1,0:T(8,128)(2,1)S(1)} %get-tuple-element.15.own_ref), channel_id=1, source_target_pairs={{0,16},{16,0},{32,48},{48,32},{64,80},{80,64},{96,112},{112,96},{1... | collective-permute-start | bytes 958472 | tf_op jit(solution)/shard_map/ppermute | solution.py:22
  23.7 16.9 %collective-permute-start.2 = (bf16[208,768]{1,0:T(8,128)(2,1)S(1)}, bf16[208,768]{1,0:T(8,128)(2,1)S(1)}, u32[]{:S(2)}, u32[]{:S(2)}) collective-permute-start(bf16[208,768]{1,0:T(8,128)(2,1)S(1)} %get-tuple-element.15.own_ref), channel_id=1, source_target_pairs={{0,1008},{16,32},{32,16},{48,64},{64,48},{80,96},{96,80},{112,128}... | collective-permute-start | bytes 958472 | tf_op jit(solution)/shard_map/ppermute | solution.py:22
  28.6 12.1 %copy-start.4 = (bf16[208,768]{1,0:T(8,128)(2,1)}, bf16[208,768]{1,0:T(8,128)(2,1)S(1)}, u32[]{:S(2)}) copy-start(bf16[208,768]{1,0:T(8,128)(2,1)S(1)} %collective-permute-done.3.other_ref) | copy-start | bytes 958468
  40.6 0.7 copy-start.5
  41.4 76.1 %copy-start = (f32[192,768]{1,0:T(8,128)S(1)}, f32[192,768]{1,0:T(8,128)}, u32[]{:S(2)}) copy-start(f32[192,768]{1,0:T(8,128)} %img_ref.3) | copy-start | bytes 1769476
  41.4 76.1 %copy-start.1 = (f32[192,768]{1,0:T(8,128)S(1)}, f32[192,768]{1,0:T(8,128)}, u32[]{:S(2)}) copy-start(f32[192,768]{1,0:T(8,128)} %txt_ref.3) | copy-start | bytes 1769476
  46.4 71.0 %collective-permute-start.4 = (bf16[384,768]{1,0:T(8,128)(2,1)S(1)}, bf16[384,768]{1,0:T(8,128)(2,1)S(1)}, u32[]{:S(2)}, u32[]{:S(2)}) collective-permute-start(bf16[384,768]{1,0:T(8,128)(2,1)S(1)} %get-tuple-element.16), channel_id=1, source_target_pairs={{0,992},{16,1008},{32,64},{48,80},{64,32},{80,48},{96,128},{112,14... | collective-permute-start | bytes 1769480 | tf_op jit(solution)/shard_map/ppermute | solution.py:22
  57.9 59.6 %collective-permute-start.5 = (bf16[384,768]{1,0:T(8,128)(2,1)S(1)}, bf16[384,768]{1,0:T(8,128)(2,1)S(1)}, u32[]{:S(2)}, u32[]{:S(2)}) collective-permute-start(bf16[384,768]{1,0:T(8,128)(2,1)S(1)} %get-tuple-element.17), channel_id=1, source_target_pairs={{0,32},{16,48},{32,0},{48,16},{64,96},{80,112},{96,64},{112,80},{1... | collective-permute-start | bytes 1769480 | tf_op jit(solution)/shard_map/ppermute | solution.py:22
  59.8 57.6 %collective-permute-start.6 = (bf16[192,768]{1,0:T(8,128)(2,1)S(1)}, bf16[192,768]{1,0:T(8,128)(2,1)S(1)}, u32[]{:S(2)}, u32[]{:S(2)}) collective-permute-start(bf16[192,768]{1,0:T(8,128)(2,1)S(1)} %get-tuple-element.18), channel_id=1, source_target_pairs={{0,1008},{16,32},{32,16},{48,64},{64,48},{80,96},{96,80},{112,128}... | collective-permute-start | bytes 884744 | tf_op jit(solution)/shard_map/ppermute | solution.py:22
  61.7 55.7 %collective-permute-start.7 = (bf16[192,768]{1,0:T(8,128)(2,1)S(1)}, bf16[192,768]{1,0:T(8,128)(2,1)S(1)}, u32[]{:S(2)}, u32[]{:S(2)}) collective-permute-start(bf16[192,768]{1,0:T(8,128)(2,1)S(1)} %get-tuple-element.19), channel_id=1, source_target_pairs={{0,16},{16,0},{32,48},{48,32},{64,80},{80,64},{96,112},{112,96},{1... | collective-permute-start | bytes 884744 | tf_op jit(solution)/shard_map/ppermute | solution.py:22
